TPU v7x, 256 devices: a whole 4x4x8 slice. The times are simulated.
256 devices in a mesh: gx: 8 (over z_lo, x), gy: 4 (over z_hi), gz: 8 (over y, core).
Axes of the slice: x: 4, y: 4, z: 8 (z_hi: 4, z_lo: 2; z = z_hi * 2 + z_lo), core: 2. Of those that a mesh axis runs over, the one named last changes fastest.
Arguments:
- volume: bfloat16 [4, 32, 32, 1024], P(None, 'gx', 'gy', 'gz'), may hold values from -6 to 6
- cotangent: bfloat16 [64, 32, 32, 1024], P(None, 'gx', 'gy', 'gz'), may hold values from -0.015625 to 0.015625
- w1_master: float32 [3456], replicated, may hold values from -0.625 to 0.625
- w1_first: float32 [3456], replicated, may hold values from -6 to 6
- w1_second: float32 [3456], replicated, may hold values from 0.1 to 4
- w2_master: float32 [55296], P(('gx', 'gy', 'gz')), may hold values from -0.21875 to 0.21875
- w2_first: float32 [55296], P(('gx', 'gy', 'gz')), may hold values from -6 to 6
- w2_second: float32 [55296], P(('gx', 'gy', 'gz')), may hold values from 0.1 to 4
Outputs:
- w1_new: float32 [3456], replicated
- w1_first_new: float32 [3456], replicated
- w1_second_new: float32 [3456], replicated
- w2_new: float32 [55296], P(('gx', 'gy', 'gz'))
- w2_first_new: float32 [55296], P(('gx', 'gy', 'gz'))
- w2_second_new: float32 [55296], P(('gx', 'gy', 'gz'))
All inputs are finite; a program needn't handle non-finite values.
Results may differ from a plain program's by a relative error of at most 0.00055.
Values may be sent and summed in bfloat16 or wider, within the bound.
No kernel may reach another device: no remote copies, remote signals or barrier semaphores. Data moves between devices by JAX's collectives and lax.ppermute only.
A program may use at most 128 MiB of HBM per device.

v0:
```python
import jax
import jax.numpy as jnp
from jax import lax
from jax.sharding import PartitionSpec as P

CI = 4
C1 = 32
C2 = 64


OFFSETS = [(a, b, c) for a in range(3) for b in range(3) for c in range(3)]


def with_halo(array, sides, width):
    for axis, dim in sides:
        size, length = (lax.axis_size(axis), array.shape[dim])
        up = [(i, (i + 1) % size) for i in range(size - 1)]
        down = [(j, i) for i, j in up]
        last = lax.slice_in_dim(array, length - width, length, axis=dim)
        initial = lax.slice_in_dim(array, 0, width, axis=dim)
        before = lax.ppermute(last, axis, up)
        after = lax.ppermute(initial, axis, down)
        array = jnp.concatenate([before, array, after], axis=dim)
    return array


def window(padded, a, b, c, extent):
    return padded[:, a : a + extent[0], b : b + extent[1], c : c + extent[2]]


def forward_first(padded, weights, extent):
    total = None
    for index, (a, b, c) in enumerate(OFFSETS):
        term = jnp.einsum(
            "ci,ixyz->cxyz",
            weights[:, index, :],
            window(padded, a, b, c, extent),
            preferred_element_type=jnp.float32,
        )
        total = term if total is None else total + term
    return total


def moments(master, first, second, grad):
    first_new = 0.9 * first + 0.1 * grad
    second_new = 0.999 * second + 0.001 * grad * grad
    direction = (
        first_new / (1.0 - 0.9**10) / (jnp.sqrt(second_new / (1.0 - 0.999**10)) + 1e-06)
        + 0.01 * master
    )
    return (first_new, second_new, direction)


def local(volume, cotangent, w1_master, w1_first, w1_second, w2_master, w2_first, w2_second):
    extent = volume.shape[1:]
    wide_half = lax.all_gather(
        w2_master.astype(jnp.bfloat16), ("gx", "gy", "gz"), axis=0, tiled=True
    ).reshape(C2, 27, C1)
    narrow_half = w1_master.astype(jnp.bfloat16).reshape(C1, 27, CI)
    field = with_halo(volume, (("gx", 1), ("gy", 2), ("gz", 3)), 1)
    pre_first = forward_first(field, narrow_half, extent)
    act_first = jax.nn.silu(pre_first).astype(jnp.bfloat16)
    act_ext = with_halo(act_first, (("gx", 1), ("gy", 2), ("gz", 3)), 1)
    wide_terms = []
    for index, (a, b, c) in enumerate(OFFSETS):
        wide_terms.append(
            jnp.einsum(
                "dxyz,cxyz->dc",
                cotangent,
                window(act_ext, a, b, c, extent),
                preferred_element_type=jnp.float32,
            )
        )
    grad_wide = jnp.stack(wide_terms, axis=1).reshape(-1)
    wide_owned = lax.psum_scatter(grad_wide, ("gx", "gy", "gz"), scatter_dimension=0, tiled=True)
    cot_ext = with_halo(cotangent, (("gx", 1), ("gy", 2), ("gz", 3)), 1)
    grad_act = None
    for index, (a, b, c) in enumerate(OFFSETS):
        term = jnp.einsum(
            "dc,dxyz->cxyz",
            wide_half[:, index, :],
            window(cot_ext, 2 - a, 2 - b, 2 - c, extent),
            preferred_element_type=jnp.float32,
        )
        grad_act = term if grad_act is None else grad_act + term
    sig = jax.nn.sigmoid(pre_first)
    grad_pre = (grad_act * sig * (1.0 + pre_first * (1.0 - sig))).astype(jnp.bfloat16)
    narrow_terms = []
    for index, (a, b, c) in enumerate(OFFSETS):
        narrow_terms.append(
            jnp.einsum(
                "cxyz,ixyz->ci",
                grad_pre,
                window(field, a, b, c, extent),
                preferred_element_type=jnp.float32,
            )
        )
    grad_narrow = jnp.stack(narrow_terms, axis=1).reshape(-1)
    length = w2_master.shape[0]
    anchor = lax.axis_index(("gx", "gy", "gz")) * length
    owner_block = (anchor + jnp.arange(length, dtype=jnp.int32)) // (27 * C1)
    selector = (owner_block[:, None] == jnp.arange(C2, dtype=jnp.int32)[None, :]).astype(
        jnp.float32
    )
    weight_part = jnp.dot(w2_master * w2_master, selector, precision=lax.Precision.HIGHEST)
    narrow_total = lax.psum(grad_narrow, ("gx", "gy", "gz"))
    wide_first, wide_second, wide_dir = moments(w2_master, w2_first, w2_second, wide_owned)
    update_part = jnp.dot(wide_dir * wide_dir, selector, precision=lax.Precision.HIGHEST)
    weight_sq, update_sq = lax.psum((weight_part, update_part), ("gx", "gy", "gz"))
    wide_ratio = jnp.sqrt(weight_sq) / (jnp.sqrt(update_sq) + 1e-06)
    entry_ratio = jnp.dot(selector, wide_ratio, precision=lax.Precision.HIGHEST)
    w2_new = w2_master - 0.01 * (entry_ratio * wide_dir)
    narrow_first, narrow_second, narrow_dir = moments(w1_master, w1_first, w1_second, narrow_total)
    narrow_wsq = jnp.sum((w1_master * w1_master).reshape(C1, -1), axis=1)
    narrow_usq = jnp.sum((narrow_dir * narrow_dir).reshape(C1, -1), axis=1)
    narrow_ratio = jnp.sqrt(narrow_wsq) / (jnp.sqrt(narrow_usq) + 1e-06)
    w1_new = w1_master - 0.01 * (narrow_ratio[:, None] * narrow_dir.reshape(C1, -1)).reshape(-1)
    return (w1_new, narrow_first, narrow_second, w2_new, wide_first, wide_second)


def solution(mesh):
    placed = (
        P(None, "gx", "gy", "gz"),
        P(None, "gx", "gy", "gz"),
        P(),
        P(),
        P(),
        P(("gx", "gy", "gz")),
        P(("gx", "gy", "gz")),
        P(("gx", "gy", "gz")),
    )
    return jax.shard_map(
        local,
        mesh=mesh,
        in_specs=placed,
        out_specs=(
            P(),
            P(),
            P(),
            P(("gx", "gy", "gz")),
            P(("gx", "gy", "gz")),
            P(("gx", "gy", "gz")),
        ),
        check_vma=False,
    )
```

profile of v0, /device:TPU:1, one launch (start us, length us, event | category | flops | bytes accessed | tf_op | source)
XLA Modules:
  0.0 783.8 jit_solution(4584650843438965063)
XLA Ops:
  8.0 3.9 collective-permute-start.6
  17.7 4.9 collective-permute-start.8
  24.1 5.5 collective-permute-done.9
  29.9 5.2 collective-permute-start.10
  47.8 4.3 collective-permute-start.12
  53.4 4.0 collective-permute-start
  58.7 5.8 collective-permute-start.14
  66.4 3.8 collective-permute-done.15
  70.5 4.4 collective-permute-start.16
  77.2 3.1 collective-permute-start.2
  82.0 3.2 collective-permute-done.17
  101.6 3.6 collective-permute-start.5
  113.0 3.8 pad_maximum_fusion
  116.8 243.2 %all-reduce.8.cloned.1.call-done = f32[55296]{0:T(1024)} async-done(((f32[55296]{0:T(1024)}), f32[55296]{0:T(1024)}) %all-reduce.8.cloned.1.call-update) | async-done | bytes 221200
  366.5 238.1 %all-reduce.6.cloned.1.call-done = bf16[55296]{0:T(1024)(128)(2,1)} async-done(((bf16[55296]{0:T(1024)(128)(2,1)}), bf16[55296]{0:T(1024)(128)(2,1)}) %all-reduce.6.cloned.1.call-update) | async-done | bytes 110608
  606.6 2.6 fusion.378
  609.3 3.6 fusion.377
  627.9 2.1 fusion.148
  634.7 2.1 fusion.144
  647.3 2.1 fusion.273
  657.0 2.1 fusion.137
  665.3 2.1 fusion.131
  681.8 2.1 fusion.119
  700.1 74.7 %all-reduce.2 = (f32[3456]{0:T(1024)S(1)}, f32[64]{0:T(128)S(1)}, f32[64]{0:T(128)S(1)}) all-reduce(f32[3456]{0:T(1024)S(1)} %reshape.56, f32[64]{0:T(128)S(1)} %copy-done.55, f32[64]{0:T(128)S(1)} %copy-done.56), channel_id=1, replica_groups=mesh['gx'=8,'gy'=4,'gz'=8] {'gx','gy','gz'}, use_global_device_ids=true, to_apply=%region_1.2 | all-reduce | flops 3584 | bytes 28672 | tf_op jit(solution)/shard_map/psum | solution.py:106
  (353 shorter events, 138.2 us)
Async XLA Ops:
  7.2 352.8 %all-reduce.8.cloned.1.call-start = ((), (), s32[]{:S(2)}) async-start(), calls=%async_computation.1 | async-start | bytes 442368
  8.0 9.5 %collective-permute-start.6 = (bf16[4,1,8,128]{3,0,2,1:T(4,128)(2,1)S(1)}, bf16[4,1,8,128]{3,0,2,1:T(4,128)(2,1)S(1)}, u32[]{:S(2)}, u32[]{:S(2)}) collective-permute-start(bf16[4,1,8,128]{3,0,2,1:T(4,128)(2,1)S(1)} %copy.549), channel_id=1, source_target_pairs={{0,32},{32,64},{64,96},{96,128},{128,160},{160,192},{192,224},{1,3... | collective-permute-start | bytes 24584 | tf_op jit(solution)/shard_map/ppermute | solution.py:21
  12.0 5.6 collective-permute-start.7
  17.7 6.5 collective-permute-start.8
  22.6 7.1 collective-permute-start.9
  29.9 8.7 %collective-permute-start.10 = (bf16[4,6,10,1]{3,0,2,1:T(4,128)(2,1)S(1)}, bf16[4,6,10,1]{3,0,2,1:T(4,128)(2,1)S(1)}, u32[]{:S(2)}, u32[]{:S(2)}) collective-permute-start(bf16[4,6,10,1]{3,0,2,1:T(4,128)(2,1)S(1)} %get-tuple-element.88), channel_id=1, source_target_pairs={{0,1},{1,2},{2,3},{3,4},{4,5},{5,6},{6,7},{8,9},{9,10},{10,11},{11... | collective-permute-start | bytes 1448 | tf_op jit(solution)/shard_map/ppermute | solution.py:21
  35.1 5.5 collective-permute-start.11
  47.8 10.9 %collective-permute-start.12 = (bf16[32,1,8,128]{3,0,2,1:T(8,128)(2,1)S(1)}, bf16[32,1,8,128]{3,0,2,1:T(8,128)(2,1)S(1)}, u32[]{:S(2)}, u32[]{:S(2)}) collective-permute-start(bf16[32,1,8,128]{3,0,2,1:T(8,128)(2,1)S(1)} %get-tuple-element.57), channel_id=1, source_target_pairs={{0,32},{32,64},{64,96},{96,128},{128,160},{160,192},{192,224},{1,3... | collective-permute-start | bytes 196616 | tf_op jit(solution)/shard_map/ppermute | solution.py:21
  52.0 6.7 collective-permute-start.13
  53.4 23.5 %collective-permute-start = (bf16[64,1,8,128]{3,0,2,1:T(8,128)(2,1)S(1)}, bf16[64,1,8,128]{3,0,2,1:T(8,128)(2,1)S(1)}, u32[]{:S(2)}, u32[]{:S(2)}) collective-permute-start(bf16[64,1,8,128]{3,0,2,1:T(8,128)(2,1)S(1)} %get-tuple-element.50), channel_id=1, source_target_pairs={{0,32},{32,64},{64,96},{96,128},{128,160},{160,192},{192,224},{1,3... | collective-permute-start | bytes 393224 | tf_op jit(solution)/shard_map/ppermute | solution.py:21
  57.4 19.8 %collective-permute-start.1 = (bf16[64,1,8,128]{3,0,2,1:T(8,128)(2,1)S(1)}, bf16[64,1,8,128]{3,0,2,1:T(8,128)(2,1)S(1)}, u32[]{:S(2)}, u32[]{:S(2)}) collective-permute-start(bf16[64,1,8,128]{3,0,2,1:T(8,128)(2,1)S(1)} %get-tuple-element.49), channel_id=1, source_target_pairs={{32,0},{64,32},{96,64},{128,96},{160,128},{192,160},{224,192},{33,... | collective-permute-start | bytes 393224 | tf_op jit(solution)/shard_map/ppermute | solution.py:22
  58.7 7.7 collective-permute-start.14
  64.5 5.7 collective-permute-start.15
  70.5 11.4 %collective-permute-start.16 = (bf16[32,6,10,1]{3,0,2,1:T(8,128)(2,1)S(1)}, bf16[32,6,10,1]{3,0,2,1:T(8,128)(2,1)S(1)}, u32[]{:S(2)}, u32[]{:S(2)}) collective-permute-start(bf16[32,6,10,1]{3,0,2,1:T(8,128)(2,1)S(1)} %get-tuple-element.54), channel_id=1, source_target_pairs={{0,1},{1,2},{2,3},{3,4},{4,5},{5,6},{6,7},{8,9},{9,10},{10,11},{11... | collective-permute-start | bytes 11528 | tf_op jit(solution)/shard_map/ppermute | solution.py:21
  74.9 10.3 %collective-permute-start.17 = (bf16[32,6,10,1]{3,0,2,1:T(8,128)(2,1)S(1)}, bf16[32,6,10,1]{3,0,2,1:T(8,128)(2,1)S(1)}, u32[]{:S(2)}, u32[]{:S(2)}) collective-permute-start(bf16[32,6,10,1]{3,0,2,1:T(8,128)(2,1)S(1)} %get-tuple-element.53), channel_id=1, source_target_pairs={{1,0},{2,1},{3,2},{4,3},{5,4},{6,5},{7,6},{9,8},{10,9},{11,10},{12... | collective-permute-start | bytes 11528 | tf_op jit(solution)/shard_map/ppermute | solution.py:22
  77.2 17.8 %collective-permute-start.2 = (bf16[64,6,1,128]{3,0,2,1:T(8,128)(2,1)S(1)}, bf16[64,6,1,128]{3,0,2,1:T(8,128)(2,1)S(1)}, u32[]{:S(2)}, u32[]{:S(2)}) collective-permute-start(bf16[64,6,1,128]{3,0,2,1:T(8,128)(2,1)S(1)} %get-tuple-element.20), channel_id=1, source_target_pairs={{0,8},{8,16},{16,24},{1,9},{9,17},{17,25},{2,10},{10,18},{18,26},{... | collective-permute-start | bytes 294920 | tf_op jit(solution)/shard_map/ppermute | solution.py:21
  80.3 15.5 %collective-permute-start.3 = (bf16[64,6,1,128]{3,0,2,1:T(8,128)(2,1)S(1)}, bf16[64,6,1,128]{3,0,2,1:T(8,128)(2,1)S(1)}, u32[]{:S(2)}, u32[]{:S(2)}) collective-permute-start(bf16[64,6,1,128]{3,0,2,1:T(8,128)(2,1)S(1)} %get-tuple-element.21), channel_id=1, source_target_pairs={{8,0},{16,8},{24,16},{9,1},{17,9},{25,17},{10,2},{18,10},{26,18},{... | collective-permute-start | bytes 294920 | tf_op jit(solution)/shard_map/ppermute | solution.py:22
  99.1 11.0 %collective-permute-start.4 = (bf16[64,6,10,1]{0,1,3,2:T(8,128)(2,1)S(1)}, bf16[64,6,10,1]{0,1,3,2:T(8,128)(2,1)S(1)}, u32[]{:S(2)}, u32[]{:S(2)}) collective-permute-start(bf16[64,6,10,1]{0,1,3,2:T(8,128)(2,1)S(1)} %copy.253), channel_id=1, source_target_pairs={{1,0},{2,1},{3,2},{4,3},{5,4},{6,5},{7,6},{9,8},{10,9},{11,10},{12... | collective-permute-start | bytes 23048 | tf_op jit(solution)/shard_map/ppermute | solution.py:22
  101.6 10.0 %collective-permute-start.5 = (bf16[64,6,10,1]{0,1,3,2:T(8,128)(2,1)S(1)}, bf16[64,6,10,1]{0,1,3,2:T(8,128)(2,1)S(1)}, u32[]{:S(2)}, u32[]{:S(2)}) collective-permute-start(bf16[64,6,10,1]{0,1,3,2:T(8,128)(2,1)S(1)} %copy.257), channel_id=1, source_target_pairs={{0,1},{1,2},{2,3},{3,4},{4,5},{5,6},{6,7},{8,9},{9,10},{10,11},{11... | collective-permute-start | bytes 23048 | tf_op jit(solution)/shard_map/ppermute | solution.py:21
  110.1 494.5 %all-reduce.6.cloned.1.call-start = ((), (), s32[]{:S(2)}) async-start(), calls=%async_computation | async-start | bytes 221184
  697.3 77.4 %copy-start.51 = (f32[3456]{0:T(1024)S(1)}, f32[3456]{0:T(1024)}, u32[]{:S(2)}) copy-start(f32[3456]{0:T(1024)} %param.11) | copy-start | bytes 41476
  697.5 77.9 %copy-start.57 = (s32[216]{0:T(256)S(1)}, s32[216]{0:T(256)}, u32[]{:S(2)}) copy-start(s32[216]{0:T(256)} %and_select_fusion) | copy-start | bytes 2596
  697.5 78.1 %copy-start.53 = (f32[216]{0:T(256)S(1)}, f32[216]{0:T(256)}, u32[]{:S(2)}) copy-start(f32[216]{0:T(256)} %param.13) | copy-start | bytes 2596
  697.5 78.2 %copy-start.54 = (f32[216]{0:T(256)S(1)}, f32[216]{0:T(256)}, u32[]{:S(2)}) copy-start(f32[216]{0:T(256)} %get-tuple-element.13) | copy-start | bytes 2596
  (54 other events, 359.8 us)
Sparse Core Ops, SparseCore 0:
  110.2 249.6 all-reduce.7
  365.5 239.0 all-reduce.5
where the time goes:
time: 787 us; the launch traced here: 784 us
  waiting for transfers between devices  496 us (63%)
  blocking collectives  74.7 us (9%)
  local copies, waits for them, and re-layouts  67.6 us (9%)
  matrix products  66.6 us (8%)
  starting transfers between devices  53.1 us (7%)
  between operations  15.3 us (2%)
  other arithmetic  10.5 us (1%)
    unnamed x4, waiting for transfers between devices  481 us
    psum x1, blocking collectives, local(): narrow_total = lax.psum(grad_narrow, ('gx', 'gy', 'gz'))  74.7 us
    unnamed x152, local copies, waits for them, and re-layouts  44.4 us
    dot_general x27, matrix products, local(): jnp.einsum('dc,dxyz->cxyz', wide_half[:, index, :], window(cot_ext, 2 - a...  39.4 us
    ppermute x9, starting transfers between devices, with_halo(): before = lax.ppermute(last, axis, up)  39.2 us
  transfers between devices with their start and end apart: 20, of which 6 were waited for; matrix products, arithmetic and copies ran while one was open for 4% of the time, Pallas kernels for 0%

commit v1 on v0

v1 whole, which is shorter than its diff:
```python
import jax
import jax.numpy as jnp
from jax import lax
from jax.experimental import pallas as pl
from jax.experimental.pallas import tpu as pltpu
from jax.sharding import Mesh, PartitionSpec as P

CI = 4
C1 = 32
C2 = 64
F32 = jnp.float32
BF16 = jnp.bfloat16
GX = ("zl", "x")
GY = ("zh",)
GZ = ("y", "core")
VMEM = pl.BlockSpec(memory_space=pltpu.VMEM)
PARAMS = pltpu.CompilerParams(vmem_limit_bytes=32 * 1024 * 1024)


def dot(a, b):
    return lax.dot_general(a, b, (((1,), (0,)), ((), ())), preferred_element_type=F32)


def dot_nt(a, b):
    return lax.dot_general(a, b, (((1,), (1,)), ((), ())), preferred_element_type=F32)


def dot_tn(a, b):
    return lax.dot_general(a, b, (((0,), (0,)), ((), ())), preferred_element_type=F32)


def call(kernel, out_shapes, *args, flops=0):
    return pl.pallas_call(
        kernel,
        out_shape=out_shapes,
        in_specs=[VMEM] * len(args),
        out_specs=jax.tree.map(lambda _: VMEM, out_shapes),
        compiler_params=PARAMS,
    )(*args)


def shape(dims, dtype):
    return jax.ShapeDtypeStruct(dims, dtype)


def y_messages(c_ref, l_ref, r_ref, up_ref, dn_ref):
    slabs = [l_ref] + [c_ref.at[x] for x in range(4)] + [r_ref]
    first, last = [], []
    for xe, slab in enumerate(slabs):
        up_ref[xe * 64 : xe * 64 + 64, :] = slab[448:512, :]
        dn_ref[xe * 64 : xe * 64 + 64, :] = slab[0:64, :]
        vol = slab[512:544, :].astype(F32)
        first.append(vol[0:4])
        last.append(vol[28:32])
    fill = jnp.zeros((8, 128), F32)
    up_ref[384:416, :] = jnp.concatenate(last + [fill], axis=0).astype(BF16)
    dn_ref[384:416, :] = jnp.concatenate(first + [fill], axis=0).astype(BF16)


def assemble(c_ref, l_ref, r_ref, yp_ref, yn_ref, e_ref, ve_ref, up_ref, dn_ref):
    slabs = [l_ref] + [c_ref.at[x] for x in range(4)] + [r_ref]
    before = yp_ref[384:416, :].astype(F32)
    after = yn_ref[384:416, :].astype(F32)
    for xe, slab in enumerate(slabs):
        e_ref[xe, 0:64, :] = yp_ref[xe * 64 : xe * 64 + 64, :]
        e_ref[xe, 64:576, :] = slab[0:512, :]
        e_ref[xe, 576:640, :] = yn_ref[xe * 64 : xe * 64 + 64, :]
        vol = slab[512:544, :].astype(F32)
        ve_ref[xe] = jnp.concatenate(
            [before[xe * 4 : xe * 4 + 4], vol, after[xe * 4 : xe * 4 + 4], jnp.zeros((8, 128), F32)], axis=0
        ).astype(BF16)
    row = lax.broadcasted_iota(jnp.int32, (32, 768), 0)
    lane = lax.broadcasted_iota(jnp.int32, (32, 768), 1)
    pick = (row < 6) & (lane == row * 128 + 127)
    pick = pick | ((row >= 16) & (row < 22) & (lane == (row - 16) * 128))
    pick = pick.astype(F32).astype(BF16)
    cot = jnp.concatenate([e_ref[xe] for xe in range(6)], axis=1)
    vol = jnp.concatenate([ve_ref[xe] for xe in range(6)], axis=1)
    vol = jnp.concatenate([vol, jnp.zeros((80, 768), BF16)], axis=0)
    edge = jnp.concatenate([dot_nt(pick, cot), dot_nt(pick, vol)], axis=1).astype(BF16)
    up_ref[...] = edge[0:16]
    dn_ref[...] = edge[16:32]


def roll(v, by):
    return pltpu.roll(v, by % v.shape[1], 1)


def gradients(e_ref, ve_ref, ml_ref, mr_ref, wt_ref, wb_ref, out_ref, ga_ref):
    lane = lax.broadcasted_iota(jnp.int32, (1, 128), 1)
    low, high = lane == 0, lane == 127
    eye = (
        lax.broadcasted_iota(jnp.int32, (48, 128), 0) == lax.broadcasted_iota(jnp.int32, (48, 128), 1)
    ).astype(F32).astype(BF16)
    left = dot_nt(eye, ml_ref[:, 640:768])
    right = dot_nt(eye, mr_ref[:, 640:768])
    shifted = []
    for xe in range(6):
        v = ve_ref[xe].astype(F32)
        shifted.append(
            (
                jnp.where(low, left[:, xe : xe + 1], roll(v, 1)).astype(BF16),
                ve_ref[xe],
                jnp.where(high, right[:, xe : xe + 1], roll(v, -1)).astype(BF16),
            )
        )
    rest = jnp.zeros((80, 128), BF16)
    patches = jnp.concatenate(
        [
            jnp.concatenate([shifted[x + a][c] for a in range(3) for c in range(3)] + [rest], axis=0)
            for x in range(4)
        ],
        axis=1,
    )
    pre = dot(wb_ref[...], patches)
    sig = 1.0 / (1.0 + jnp.exp(-pre))
    act = (pre * sig).astype(BF16)
    slope = sig * (1.0 + pre * (1.0 - sig))
    halos = []
    for ref in (ml_ref, mr_ref):
        m = ref[:, 0:640].astype(F32)
        halos.append(
            jnp.concatenate(
                [
                    jnp.concatenate([m[a : a + 4, 128 * k : 128 * k + 256] for a in range(3)], axis=1)
                    for k in range(4)
                ],
                axis=0,
            ).astype(BF16)
        )
    none = jnp.zeros((32, 64), BF16)
    blocks = []
    for c in range(3):
        for yl in range(2):
            cells = []
            for a in range(3):
                for yp in range(4):
                    b = yp - yl
                    if 0 <= b <= 2:
                        tap = (2 - a) * 9 + (2 - b) * 3 + (2 - c)
                        cells.append(wt_ref[tap * 32 : tap * 32 + 32, :])
                    else:
                        cells.append(none)
            blocks.append(jnp.concatenate(cells, axis=1))
    bank = jnp.concatenate(blocks, axis=0)
    from_left = dot_nt(bank[0:64], halos[0])
    from_right = dot_nt(bank[128:192], halos[1])
    for k in range(4):
        for xp in range(2):
            cells = jnp.concatenate(
                [
                    jnp.concatenate(
                        [e_ref[2 * xp + j + a, 128 * k : 128 * k + 256, :] for j in range(2)], axis=1
                    )
                    for a in range(3)
                ],
                axis=0,
            )
            v = dot(bank, cells)
            for j in range(2):
                x = 2 * xp + j
                at = slice(128 * j, 128 * j + 128)
                col = 4 * k + x
                ga_ref[64 * k : 64 * k + 64, 128 * x : 128 * x + 128] = (
                    v[64:128, at]
                    + jnp.where(low, from_left[:, col : col + 1], roll(v[0:64, at], 1))
                    + jnp.where(high, from_right[:, col : col + 1], roll(v[128:192, at], -1))
                )
    grad_pre = (ga_ref[...] * slope).astype(BF16)
    product = dot_nt(grad_pre, patches)
    total = product[0:32]
    for y in range(1, 8):
        total = total + roll(product[32 * y : 32 * y + 32], -4 * y)
    row = lax.broadcasted_iota(jnp.int32, (512, 128), 0)
    col = lax.broadcasted_iota(jnp.int32, (512, 128), 1)
    group, inner = row // 48, row % 48
    a, c = group // 3, group % 3
    b, i = inner // 4, inner % 4
    chosen = (b < 3) & (group < 9) & (col == (9 * a + 3 * b + c) * 4 + i)
    narrow = lax.dot_general(
        total,
        chosen.astype(F32),
        (((1,), (0,)), ((), ())),
        precision=lax.Precision.HIGHEST,
        preferred_element_type=F32,
    )
    act32 = act.astype(F32)
    before, after = [], []
    for x in range(4):
        part = act32[:, 128 * x : 128 * x + 128]
        before.append(jnp.where(low, 0.0, roll(part, 1)).astype(BF16))
        after.append(jnp.where(high, 0.0, roll(part, -1)).astype(BF16))
    before = jnp.concatenate(before, axis=1)
    after = jnp.concatenate(after, axis=1)
    empty = jnp.zeros((32, 512), BF16)
    rows = []
    for k in range(4):
        parts = []
        for yl in range(2):
            at = slice(64 * k + 32 * yl, 64 * k + 32 * yl + 32)
            parts += [before[at], act[at], after[at], empty]
        rows.append(jnp.concatenate(parts, axis=0))
    acts = jnp.concatenate(rows, axis=1)
    cots = jnp.concatenate(
        [
            jnp.concatenate(
                [e_ref[x + a, 128 * k : 128 * k + 256, :] for k in range(4) for x in range(4)], axis=1
            )
            for a in range(3)
        ],
        axis=0,
    )
    wide = dot_nt(cots, acts)
    row = lax.broadcasted_iota(jnp.int32, (16, 512), 0)
    lanes = lax.broadcasted_iota(jnp.int32, (16, 512), 1)
    pick = ((row < 4) & (lanes == row * 128)) | ((row >= 4) & (row < 8) & (lanes == (row - 4) * 128 + 127))
    edges = dot_nt(pick.astype(F32).astype(BF16), act)
    gap = jnp.zeros((4, 64), F32)
    one = jnp.zeros((4, 32), F32)
    table = []
    for k in range(4):
        e0 = edges[0:4, 64 * k : 64 * k + 32]
        e1 = edges[0:4, 64 * k + 32 : 64 * k + 64]
        table.append(jnp.concatenate([gap, e0, one, gap, e1, one], axis=1))
    for k in range(4):
        e0 = edges[4:8, 64 * k : 64 * k + 32]
        e1 = edges[4:8, 64 * k + 32 : 64 * k + 64]
        table.append(jnp.concatenate([e0, one, gap, e1, one, gap], axis=1))
    table = jnp.concatenate(table, axis=0).astype(BF16)
    wide = wide + dot_tn(jnp.concatenate(halos, axis=0), table)
    taps = []
    for a in range(3):
        for b in range(3):
            at = (2 - a) * 256 + (2 - b) * 64
            taps.append((wide[at : at + 64, 0:128] + wide[at + 64 : at + 128, 128:256])[:, 0:96])
    wide = jnp.concatenate(taps + [jnp.zeros((64, 32), F32)], axis=1)
    for p in range(8):
        out_ref[p, :, 0:896] = wide[8 * p : 8 * p + 8]
        for j in range(4):
            out_ref[p, :, 896 + 128 * j : 1024 + 128 * j] = narrow[8 * j : 8 * j + 8]


def second_stage(in_ref, out_ref):
    total = in_ref[0]
    for p in range(1, 8):
        total = total + in_ref[p]
    narrow = total[:, 896:1408]
    for owner in range(8):
        x, yh = owner // 2, owner % 2
        block = jnp.concatenate(
            [total[owner : owner + 1, 128 * j : 128 * j + 128] for j in range(7)] + [jnp.zeros((1, 128), F32)],
            axis=0,
        )
        both = jnp.concatenate([narrow, block], axis=1)
        for q in range(4):
            out_ref[x * 8 + yh * 4 + q] = both


def moments(master, first, second, grad):
    first_new = 0.9 * first + 0.1 * grad
    second_new = 0.999 * second + 0.001 * grad * grad
    direction = (
        first_new / (1.0 - 0.9**10) / (jnp.sqrt(second_new / (1.0 - 0.999**10)) + 1e-06)
        + 0.01 * master
    )
    return (first_new, second_new, direction)


def update(in_ref, wide_ref, narrow_ref, wide_out, narrow_out):
    total = in_ref[0]
    for p in range(1, 32):
        total = total + in_ref[p]
    inside = (
        lax.broadcasted_iota(jnp.int32, (8, 128), 0) * 128 + lax.broadcasted_iota(jnp.int32, (8, 128), 1)
    ) < 864
    master, first, second = wide_ref[0], wide_ref[1], wide_ref[2]
    first_new, second_new, direction = moments(master, first, second, total[:, 512:640])
    direction = jnp.where(inside, direction, 0.0)
    ratio = jnp.sqrt(jnp.sum(master * master, keepdims=True)) / (
        jnp.sqrt(jnp.sum(direction * direction, keepdims=True)) + 1e-06
    )
    wide_out[0] = master - 0.01 * (ratio * direction)
    wide_out[1] = first_new
    wide_out[2] = second_new
    grad = jnp.concatenate([total[:, 128 * j : 128 * j + 128] for j in range(4)], axis=0)
    master, first, second = narrow_ref[0], narrow_ref[1], narrow_ref[2]
    first_new, second_new, direction = moments(master, first, second, grad)
    direction = jnp.where(lax.broadcasted_iota(jnp.int32, (32, 128), 1) < 108, direction, 0.0)
    ratio = jnp.sqrt(jnp.sum(master * master, axis=1, keepdims=True)) / (
        jnp.sqrt(jnp.sum(direction * direction, axis=1, keepdims=True)) + 1e-06
    )
    narrow_out[0] = master - 0.01 * (ratio * direction)
    narrow_out[1] = first_new
    narrow_out[2] = second_new


def exchange(up, down, axes):
    size = lax.axis_size(axes)
    pairs = [(i, i + 1) for i in range(size - 1)]
    before = lax.ppermute(up, axes, pairs)
    after = lax.ppermute(down, axes, [(j, i) for i, j in pairs])
    return before, after


def spread(value, axes):
    size = lax.axis_size(axes)
    return lax.all_to_all(
        jnp.broadcast_to(value[None], (size,) + value.shape), axes, 0, 0, tiled=True
    )


def local(volume, cotangent, w1_master, w1_first, w1_second, w2_master, w2_first, w2_second):
    cot = cotangent.reshape(2, 4, 4, 2, 4, 8, 128).transpose(4, 5, 0, 2, 1, 3, 6).reshape(4, 512, 128)
    vol = volume.transpose(1, 2, 0, 3).reshape(4, 32, 128)
    slabs = jnp.concatenate([cot, vol], axis=1)
    before_x, after_x = exchange(slabs[3], slabs[0], GX)
    owned = jnp.stack([w2_master, w2_first, w2_second])
    near = spread(owned, GZ)
    bank = spread(near[:, 0].astype(BF16), GX + GY).reshape(2, 4, 4, 2, 864)
    bank = bank.transpose(4, 0, 2, 1, 3).reshape(864, 64)
    half = lax.axis_index("y") // 2
    block = lax.dynamic_slice_in_dim(near, half * 4, 4, axis=0).transpose(1, 0, 2).reshape(3, 864)
    block = jnp.pad(block, ((0, 0), (0, 160))).reshape(3, 8, 128)
    narrow_half = w1_master.astype(BF16).reshape(C1, 3, 3, 3, CI)
    band = (
        jnp.arange(12)[None, None, :] == jnp.arange(8)[:, None, None] + jnp.arange(3)[None, :, None]
    ).astype(BF16)
    narrow_band = jnp.einsum("cabsi,ybe->ycasei", narrow_half, band).reshape(256, 432)
    narrow_band = jnp.pad(narrow_band, ((0, 0), (0, 80)))
    narrow = jnp.pad(
        jnp.stack([w1_master, w1_first, w1_second]).reshape(3, C1, 108), ((0, 0), (0, 0), (0, 20))
    )
    up, down = call(
        y_messages, (shape((416, 128), BF16), shape((416, 128), BF16)), slabs, before_x, after_x
    )
    before_y, after_y = exchange(up, down, GY)
    cells, fields, up, down = call(
        assemble,
        (
            shape((6, 640, 128), BF16),
            shape((6, 48, 128), BF16),
            shape((16, 768), BF16),
            shape((16, 768), BF16),
        ),
        slabs,
        before_x,
        after_x,
        before_y,
        after_y,
    )
    before_z, after_z = exchange(up, down, GZ)
    sums = pl.pallas_call(
        gradients,
        out_shape=shape((8, 8, 1408), F32),
        in_specs=[VMEM] * 6,
        out_specs=VMEM,
        scratch_shapes=[pltpu.VMEM((256, 512), F32)],
        compiler_params=PARAMS,
    )(cells, fields, before_z, after_z, bank, narrow_band)
    sums = lax.all_to_all(sums, ("zl", "zh"), 0, 0, tiled=True)
    sums = call(second_stage, shape((32, 8, 640), F32), sums)
    sums = lax.all_to_all(sums, ("x", "y", "core"), 0, 0, tiled=True)
    wide_new, narrow_new = call(
        update, (shape((3, 8, 128), F32), shape((3, 32, 128), F32)), sums, block, narrow
    )
    quarter = (lax.axis_index("y") % 2) * 2 + lax.axis_index("core")
    wide_new = lax.dynamic_slice_in_dim(wide_new.reshape(3, 1024), quarter * 216, 216, axis=1)
    narrow_new = narrow_new[:, :, :108].reshape(3, 3456)
    return (
        narrow_new[0],
        narrow_new[1],
        narrow_new[2],
        wide_new[0],
        wide_new[1],
        wide_new[2],
    )


def solution(mesh):
    parts = Mesh(mesh.devices.reshape(2, 4, 4, 4, 2), GX + GY + GZ)
    field = P(None, GX, GY, GZ)
    owned = P(GX + GY + GZ)
    return jax.shard_map(
        local,
        mesh=parts,
        in_specs=(field, field, P(), P(), P(), owned, owned, owned),
        out_specs=(P(), P(), P(), owned, owned, owned),
        check_vma=False,
    )
```

time: 787 us -> 94.6 us (0.12)
  waiting for transfers between devices: 496 us -> 13.2 us
  matrix products: 66.6 us -> 0.61 us
  local copies, waits for them, and re-layouts: 67.6 us -> 9.44 us
  blocking collectives: 74.7 us -> 18.6 us
  between operations: 15.3 us -> 1.1 us
  other arithmetic: 10.5 us -> 0.09 us
    unnamed x4 -> x0, waiting for transfers between devices: 481 us -> none
    psum x1 -> x0, blocking collectives: 74.7 us -> none  [local(): narrow_total = lax.psum(grad_narrow, ('gx', 'gy', 'gz'))]
    dot_general x111 -> x1, matrix products: 66.6 us -> 0.61 us  [local(): jnp.einsum('cabsi,ybe->ycasei', narrow_half, band).reshape(256, 432)]
    unnamed x152 -> x16, local copies, waits for them, and re-layouts: 44.4 us -> 0.05 us
    ppermute x18 -> x6, starting transfers between devices: 53 us -> 18 us  [the longest x3 13.5 us: exchange(): before = lax.ppermute(up, axes, pairs)]
    all_to_all x0 -> x3, starting transfers between devices: none -> 27.5 us  [the longest x2 18.8 us: spread(): lax.all_to_all(jnp.broadcast_to(value[None], (size,) + value.shape), axes...]
    all_to_all x0 -> x1, blocking collectives: none -> 18.6 us  [local(): sums = lax.all_to_all(sums, ('zl', 'zh'), 0, 0, tiled=True)]
    ppermute x18 -> x6, waiting for transfers between devices: 14.6 us -> 0.74 us  [the longest x3 0.73 us: exchange(): after = lax.ppermute(down, axes, [(j, i) for i, j in pairs])]
  transfers between devices with their start and end apart: 20 -> 9, of which waited for: 6 -> 3; matrix products, arithmetic and copies ran while one was open for 4% -> 5% of each run, Pallas kernels for 0% -> 0%
where the time goes in v1:
time: 94.6 us; the launch traced here: 94 us
  starting transfers between devices  45.5 us (48%)
  blocking collectives  18.6 us (20%)
  waiting for transfers between devices  13.2 us (14%)
  local copies, waits for them, and re-layouts  9.44 us (10%)
  Pallas kernels  5.4 us (6%)
  between operations  1.1 us (1%)
    all_to_all x2, starting transfers between devices, spread(): lax.all_to_all(jnp.broadcast_to(value[None], (size,) + value.shape), axes...  18.8 us
    all_to_all x1, blocking collectives, local(): sums = lax.all_to_all(sums, ('zl', 'zh'), 0, 0, tiled=True)  18.6 us
    ppermute x3, starting transfers between devices, exchange(): before = lax.ppermute(up, axes, pairs)  13.5 us
    all_to_all x1, waiting for transfers between devices, local(): sums = lax.all_to_all(sums, ('x', 'y', 'core'), 0, 0, tiled=True)  12.4 us
    all_to_all x1, starting transfers between devices, local(): sums = lax.all_to_all(sums, ('x', 'y', 'core'), 0, 0, tiled=True)  8.73 us
    ppermute x3, starting transfers between devices, exchange(): after = lax.ppermute(down, axes, [(j, i) for i, j in pairs])  4.5 us
    pallas_call x1, Pallas kernels, local(): pl.pallas_call(gradients, out_shape=shape((8, 8, 1408), F32), in_specs=[V...  3.84 us
  transfers between devices with their start and end apart: 9, of which 3 were waited for; matrix products, arithmetic and copies ran while one was open for 5% of the time, Pallas kernels for 0%

profile of v1, /device:TPU:1, one launch (start us, length us, event | category | flops | bytes accessed | tf_op | source)
XLA Modules:
  0.0 94.0 jit_solution(11429883062536925575)
XLA Ops:
  0.7 1.6 %copy.31 = bf16[2,4,4,2,4,8,128]{6,3,1,2,0,5,4:T(2,128)(2,1)S(1)} copy(bf16[2,4,4,2,4,8,128]{6,5,4,3,2,1,0:T(8,128)(2,1)} %bitcast.51) | data formatting | bytes 1048576 | tf_op jit(solution)/shard_map/reshape | solution.py:313
  2.3 0.8 copy.32
  3.1 4.0 %collective-permute-start = (bf16[544,128]{1,0:T(8,128)(2,1)S(1)}, bf16[544,128]{1,0:T(8,128)(2,1)S(1)}, u32[]{:S(2)}, u32[]{:S(2)}) collective-permute-start(bf16[544,128]{1,0:T(8,128)(2,1)S(1)} %get-tuple-element.23), channel_id=1, source_target_pairs={{0,32},{32,64},{64,96},{96,128},{128,160},{160,192},{192,224},{1,3... | collective-permute-start | bytes 417800 | tf_op jit(solution)/shard_map/ppermute | solution.py:300
  7.0 1.3 %collective-permute-start.1 = (bf16[544,128]{1,0:T(8,128)(2,1)S(1)}, bf16[544,128]{1,0:T(8,128)(2,1)S(1)}, u32[]{:S(2)}, u32[]{:S(2)}) collective-permute-start(bf16[544,128]{1,0:T(8,128)(2,1)S(1)} %get-tuple-element.22), channel_id=1, source_target_pairs={{32,0},{64,32},{96,64},{128,96},{160,128},{192,160},{224,192},{33,... | collective-permute-start | bytes 417800 | tf_op jit(solution)/shard_map/ppermute | solution.py:301
  8.4 0.6 broadcast_in_dim.4
  9.0 5.4 %all-to-all-start = ((f32[8,3,216]{2,1,0:T(4,128)}), f32[8,3,216]{2,1,0:T(4,128)S(1)}, u32[]{:S(2)}, u32[]{:S(2)}) async-start(f32[8,3,216]{2,1,0:T(4,128)} %broadcast_in_dim.4), calls=%async_computation | async-start | bytes 65536 | tf_op jit(solution)/shard_map/all_to_all | solution.py:307
  14.5 4.9 %collective-permute-start.2 = (bf16[416,128]{1,0:T(8,128)(2,1)S(1)}, bf16[416,128]{1,0:T(8,128)(2,1)S(1)}, u32[]{:S(2)}, u32[]{:S(2)}) collective-permute-start(bf16[416,128]{1,0:T(8,128)(2,1)S(1)} %get-tuple-element.14), channel_id=1, source_target_pairs={{0,8},{8,16},{16,24},{1,9},{9,17},{17,25},{2,10},{10,18},{18,26},{... | collective-permute-start | bytes 319496 | tf_op jit(solution)/shard_map/ppermute | solution.py:300
  19.4 1.3 %collective-permute-start.3 = (bf16[416,128]{1,0:T(8,128)(2,1)S(1)}, bf16[416,128]{1,0:T(8,128)(2,1)S(1)}, u32[]{:S(2)}, u32[]{:S(2)}) collective-permute-start(bf16[416,128]{1,0:T(8,128)(2,1)S(1)} %get-tuple-element.15), channel_id=1, source_target_pairs={{8,0},{16,8},{24,16},{9,1},{17,9},{25,17},{10,2},{18,10},{26,18},{... | collective-permute-start | bytes 319496 | tf_op jit(solution)/shard_map/ppermute | solution.py:301
  21.4 0.7 broadcast_in_dim.5
  22.0 13.4 %all-to-all-start.1 = ((bf16[32,8,216]{2,1,0:T(8,128)(2,1)}), bf16[32,8,216]{2,1,0:T(8,128)(2,1)S(1)}, u32[]{:S(2)}, u32[]{:S(2)}) async-start(bf16[32,8,216]{2,1,0:T(8,128)(2,1)} %broadcast_in_dim.5), calls=%async_computation.1 | async-start | bytes 262144 | tf_op jit(solution)/shard_map/all_to_all | solution.py:307
  35.9 4.6 %collective-permute-start.4 = (bf16[16,768]{1,0:T(8,128)(2,1)S(1)}, bf16[16,768]{1,0:T(8,128)(2,1)S(1)}, u32[]{:S(2)}, u32[]{:S(2)}) collective-permute-start(bf16[16,768]{1,0:T(8,128)(2,1)S(1)} %get-tuple-element.18), channel_id=1, source_target_pairs={{0,1},{1,2},{2,3},{3,4},{4,5},{5,6},{6,7},{8,9},{9,10},{10,11},{11... | collective-permute-start | bytes 73736 | tf_op jit(solution)/shard_map/ppermute | solution.py:300
  40.5 1.9 %collective-permute-start.5 = (bf16[16,768]{1,0:T(8,128)(2,1)S(1)}, bf16[16,768]{1,0:T(8,128)(2,1)S(1)}, u32[]{:S(2)}, u32[]{:S(2)}) collective-permute-start(bf16[16,768]{1,0:T(8,128)(2,1)S(1)} %get-tuple-element.19), channel_id=1, source_target_pairs={{1,0},{2,1},{3,2},{4,3},{5,4},{6,5},{7,6},{9,8},{10,9},{11,10},{12... | collective-permute-start | bytes 73736 | tf_op jit(solution)/shard_map/ppermute | solution.py:301
  42.4 0.6 convolution_bitcast_fusion
  43.1 0.6 copy.36
  45.2 0.7 collective-permute-done.5.mr_ref
  46.0 3.8 %shard_map.129 = f32[8,8,1408]{2,1,0:T(8,128)S(1)} custom-call(bf16[6,640,128]{2,1,0:T(8,128)(2,1)S(1)} %get-tuple-element.16.e_ref, bf16[6,48,128]{2,1,0:T(8,128)(2,1)S(1)} %get-tuple-element.17.ve_ref, bf16[16,768]{1,0:T(8,128)(2,1)S(1)} %collective-permute-done.4.ml_ref, bf16[16,768]{1,0:T(8,128)(2,1)S(1)} %collective-permute-done.5.mr_ref, ...), custom_call_target="tpu_custom_call" | custom-call | tf_op jit(solution)/shard_map/pallas_call | solution.py:352
  49.8 18.6 %all_to_all.20.in_ref = f32[8,8,1408]{2,1,0:T(8,128)S(1)} all-to-all(f32[8,8,1408]{2,1,0:T(8,128)S(1)} %shard_map.129), channel_id=1, replica_groups=mesh['zl'=2,'x'=4,'zh'=4,'y'=4,'core'=2] {'zl','zh'}, dimensions={0} | all-to-all | bytes 720896 | tf_op jit(solution)/shard_map/all_to_all | solution.py:360
  68.4 0.9 shard_map.130
  69.3 8.7 %all-to-all-start.3 = ((f32[32,8,640]{2,1,0:T(8,128)}), f32[32,8,640]{2,1,0:T(8,128)S(1)}, u32[]{:S(2)}, u32[]{:S(2)}) async-start(f32[32,8,640]{2,1,0:T(8,128)} %shard_map.130), calls=%async_computation.3 | async-start | bytes 1310720 | tf_op jit(solution)/shard_map/all_to_all | solution.py:362
  78.6 12.4 %all-to-all-done.3.in_ref = f32[32,8,640]{2,1,0:T(8,128)S(1)} async-done(((f32[32,8,640]{2,1,0:T(8,128)}), f32[32,8,640]{2,1,0:T(8,128)S(1)}, u32[]{:S(2)}, u32[]{:S(2)}) %all-to-all-start.3) | async-done | bytes 655392 | tf_op jit(solution)/shard_map/all_to_all | solution.py:362
  91.2 0.7 squeeze.27
  92.0 0.7 squeeze.28
  92.7 0.7 squeeze.29
  93.4 0.6 fusion.10
  (49 shorter events, 3.3 us)
Async XLA Ops:
  0.6 7.7 %copy-start.5 = (f32[216]{0:T(256)S(1)}, f32[216]{0:T(256)}, u32[]{:S(2)}) copy-start(f32[216]{0:T(256)} %param.13) | copy-start | bytes 2596
  0.6 7.7 %copy-start.4 = (f32[216]{0:T(256)S(1)}, f32[216]{0:T(256)}, u32[]{:S(2)}) copy-start(f32[216]{0:T(256)} %param.14) | copy-start | bytes 2596
  0.7 7.7 %copy-start.3 = (f32[216]{0:T(256)S(1)}, f32[216]{0:T(256)}, u32[]{:S(2)}) copy-start(f32[216]{0:T(256)} %param.15) | copy-start | bytes 2596
  3.1 17.7 %copy-start = (f32[3456]{0:T(1024)S(1)}, f32[3456]{0:T(1024)}, u32[]{:S(2)}) copy-start(f32[3456]{0:T(1024)} %param.10) | copy-start | bytes 41476
  3.1 11.4 %collective-permute-start = (bf16[544,128]{1,0:T(8,128)(2,1)S(1)}, bf16[544,128]{1,0:T(8,128)(2,1)S(1)}, u32[]{:S(2)}, u32[]{:S(2)}) collective-permute-start(bf16[544,128]{1,0:T(8,128)(2,1)S(1)} %get-tuple-element.23), channel_id=1, source_target_pairs={{0,32},{32,64},{64,96},{96,128},{128,160},{160,192},{192,224},{1,3... | collective-permute-start | bytes 417800 | tf_op jit(solution)/shard_map/ppermute | solution.py:300
  7.0 7.4 %collective-permute-start.1 = (bf16[544,128]{1,0:T(8,128)(2,1)S(1)}, bf16[544,128]{1,0:T(8,128)(2,1)S(1)}, u32[]{:S(2)}, u32[]{:S(2)}) collective-permute-start(bf16[544,128]{1,0:T(8,128)(2,1)S(1)} %get-tuple-element.22), channel_id=1, source_target_pairs={{32,0},{64,32},{96,64},{128,96},{160,128},{192,160},{224,192},{33,... | collective-permute-start | bytes 417800 | tf_op jit(solution)/shard_map/ppermute | solution.py:301
  9.0 12.3 %all-to-all-start = ((f32[8,3,216]{2,1,0:T(4,128)}), f32[8,3,216]{2,1,0:T(4,128)S(1)}, u32[]{:S(2)}, u32[]{:S(2)}) async-start(f32[8,3,216]{2,1,0:T(4,128)} %broadcast_in_dim.4), calls=%async_computation | async-start | bytes 65536 | tf_op jit(solution)/shard_map/all_to_all | solution.py:307
  14.5 20.9 %collective-permute-start.2 = (bf16[416,128]{1,0:T(8,128)(2,1)S(1)}, bf16[416,128]{1,0:T(8,128)(2,1)S(1)}, u32[]{:S(2)}, u32[]{:S(2)}) collective-permute-start(bf16[416,128]{1,0:T(8,128)(2,1)S(1)} %get-tuple-element.14), channel_id=1, source_target_pairs={{0,8},{8,16},{16,24},{1,9},{9,17},{17,25},{2,10},{10,18},{18,26},{... | collective-permute-start | bytes 319496 | tf_op jit(solution)/shard_map/ppermute | solution.py:300
  19.4 16.0 %collective-permute-start.3 = (bf16[416,128]{1,0:T(8,128)(2,1)S(1)}, bf16[416,128]{1,0:T(8,128)(2,1)S(1)}, u32[]{:S(2)}, u32[]{:S(2)}) collective-permute-start(bf16[416,128]{1,0:T(8,128)(2,1)S(1)} %get-tuple-element.15), channel_id=1, source_target_pairs={{8,0},{16,8},{24,16},{9,1},{17,9},{25,17},{10,2},{18,10},{26,18},{... | collective-permute-start | bytes 319496 | tf_op jit(solution)/shard_map/ppermute | solution.py:301
  22.0 22.6 %all-to-all-start.1 = ((bf16[32,8,216]{2,1,0:T(8,128)(2,1)}), bf16[32,8,216]{2,1,0:T(8,128)(2,1)S(1)}, u32[]{:S(2)}, u32[]{:S(2)}) async-start(bf16[32,8,216]{2,1,0:T(8,128)(2,1)} %broadcast_in_dim.5), calls=%async_computation.1 | async-start | bytes 262144 | tf_op jit(solution)/shard_map/all_to_all | solution.py:307
  35.9 9.3 %collective-permute-start.4 = (bf16[16,768]{1,0:T(8,128)(2,1)S(1)}, bf16[16,768]{1,0:T(8,128)(2,1)S(1)}, u32[]{:S(2)}, u32[]{:S(2)}) collective-permute-start(bf16[16,768]{1,0:T(8,128)(2,1)S(1)} %get-tuple-element.18), channel_id=1, source_target_pairs={{0,1},{1,2},{2,3},{3,4},{4,5},{5,6},{6,7},{8,9},{9,10},{10,11},{11... | collective-permute-start | bytes 73736 | tf_op jit(solution)/shard_map/ppermute | solution.py:300
  40.5 5.4 %collective-permute-start.5 = (bf16[16,768]{1,0:T(8,128)(2,1)S(1)}, bf16[16,768]{1,0:T(8,128)(2,1)S(1)}, u32[]{:S(2)}, u32[]{:S(2)}) collective-permute-start(bf16[16,768]{1,0:T(8,128)(2,1)S(1)} %get-tuple-element.19), channel_id=1, source_target_pairs={{1,0},{2,1},{3,2},{4,3},{5,4},{6,5},{7,6},{9,8},{10,9},{11,10},{12... | collective-permute-start | bytes 73736 | tf_op jit(solution)/shard_map/ppermute | solution.py:301
  68.4 9.8 %copy-start.1 = (f32[3456]{0:T(1024)S(1)}, f32[3456]{0:T(1024)}, u32[]{:S(2)}) copy-start(f32[3456]{0:T(1024)} %param.11) | copy-start | bytes 41476
  68.4 9.9 %copy-start.2 = (f32[3456]{0:T(1024)S(1)}, f32[3456]{0:T(1024)}, u32[]{:S(2)}) copy-start(f32[3456]{0:T(1024)} %param.12) | copy-start | bytes 41476
  69.3 21.7 %all-to-all-start.3 = ((f32[32,8,640]{2,1,0:T(8,128)}), f32[32,8,640]{2,1,0:T(8,128)S(1)}, u32[]{:S(2)}, u32[]{:S(2)}) async-start(f32[32,8,640]{2,1,0:T(8,128)} %shard_map.130), calls=%async_computation.3 | async-start | bytes 1310720 | tf_op jit(solution)/shard_map/all_to_all | solution.py:362

commit v2 on v1

v2 whole, which is shorter than its diff:
```python
import jax
import jax.numpy as jnp
from jax import lax
from jax.experimental import pallas as pl
from jax.experimental.pallas import tpu as pltpu
from jax.sharding import Mesh, PartitionSpec as P

CI = 4
C1 = 32
C2 = 64
F32 = jnp.float32
BF16 = jnp.bfloat16
GX = ("zl", "x")
GY = ("zh",)
GZ = ("y", "core")
VMEM = pl.BlockSpec(memory_space=pltpu.VMEM)
PARAMS = pltpu.CompilerParams(vmem_limit_bytes=32 * 1024 * 1024)


def dot(a, b):
    return lax.dot_general(a, b, (((1,), (0,)), ((), ())), preferred_element_type=F32)


def dot_nt(a, b):
    return lax.dot_general(a, b, (((1,), (1,)), ((), ())), preferred_element_type=F32)


def dot_tn(a, b):
    return lax.dot_general(a, b, (((0,), (0,)), ((), ())), preferred_element_type=F32)


def call(kernel, out_shapes, *args, scratch=(), space=VMEM):
    return pl.pallas_call(
        kernel,
        out_shape=out_shapes,
        in_specs=[space] * len(args),
        out_specs=jax.tree.map(lambda _: VMEM, out_shapes),
        scratch_shapes=scratch,
        compiler_params=PARAMS,
    )(*args)


def shape(dims, dtype):
    return jax.ShapeDtypeStruct(dims, dtype)


def roll(v, by):
    return pltpu.roll(v, by % v.shape[1], 1)


def lanes():
    return lax.broadcasted_iota(jnp.int32, (1, 128), 1)


def within(v, low, high):
    return jnp.where((lanes() >= low) & (lanes() < high), v, 0.0)


def two_rows(v):
    return [v[:, 0:128], jnp.concatenate([v[:, 128:216], jnp.zeros((1, 40), F32)], axis=1)]


def place(two, q):
    lane = lax.broadcasted_iota(jnp.int32, (1, 128), 1)
    row, at = divmod(216 * q, 128)
    one, last = roll(two[0:1], at), roll(jnp.where(lane < 88, two[1:2], 0.0), at)
    gap = jnp.zeros((1, 128), F32)
    pieces = [gap] * row + [
        jnp.where(lane >= at, one, 0.0),
        jnp.where(lane < at, one, 0.0) + jnp.where(lane >= at, last, 0.0),
        jnp.where(lane < at, last, 0.0),
    ]
    return jnp.concatenate((pieces + [gap] * 8)[:8], axis=0)


def take(block, q):
    lane = lax.broadcasted_iota(jnp.int32, (1, 128), 1)
    row, at = divmod(216 * q, 128)
    moved = [roll(block[r : r + 1], -at) for r in range(row, min(row + 3, 8))]
    one = jnp.where(lane < 128 - at, moved[0], moved[1])
    two = jnp.where(lane < 128 - at, moved[1], moved[2]) if len(moved) > 2 else moved[1]
    return jnp.concatenate([one, two], axis=0)


def along_gz():
    return lax.axis_index("y") * 2 + lax.axis_index("core")


def pack(
    cot_hbm, vol_hbm, w2_hbm, f2_hbm, s2_hbm, slab_ref, up_ref, dn_ref, out_ref, own_ref,
    cot_ref, vol_ref, w2_ref, f2_ref, s2_ref, cot32, vol32, sems,
):
    copies = [
        pltpu.make_async_copy(source, target, sems.at[i])
        for i, (source, target) in enumerate(
            ((cot_hbm, cot_ref), (vol_hbm, vol_ref), (w2_hbm, w2_ref), (f2_hbm, f2_ref), (s2_hbm, s2_ref))
        )
    ]
    for copy in copies:
        copy.start()
    for copy in copies:
        copy.wait()
    cot32[...] = cot_ref[...].astype(F32)
    vol32[...] = vol_ref[...].astype(F32)
    for x in range(4):
        for y in range(8):
            slab_ref[x, 64 * y : 64 * y + 64, :] = cot32[pl.ds(8 * x + y, 64, stride=32), :].astype(BF16)
        slab_ref[x, 512:544, :] = jnp.concatenate(
            [vol32[pl.ds(8 * x + y, 4, stride=32), :] for y in range(8)], axis=0
        ).astype(BF16)
    up_ref[...] = slab_ref[3]
    dn_ref[...] = slab_ref[0]
    row = lax.broadcasted_iota(jnp.int32, (16, 512), 0)
    lane = lax.broadcasted_iota(jnp.int32, (16, 512), 1)
    pick = ((row < 4) & (lane == row * 128)) | ((row >= 4) & (row < 8) & (lane == row * 128 - 385))
    cells = jnp.concatenate([slab_ref[x] for x in range(4)], axis=1)
    cells = jnp.concatenate([cells, jnp.zeros((96, 512), BF16)], axis=0)
    edge = dot_nt(pick.astype(F32).astype(BF16), cells)
    own = [row for ref in (w2_ref, f2_ref, s2_ref) for row in two_rows(ref[...])]
    own_ref[...] = jnp.concatenate(own + [jnp.zeros((2, 128), F32)], axis=0)
    ends = []
    for side in range(2):
        at = slice(4 * side, 4 * side + 4)
        tail = edge[at, 512:640]
        tail = [sum(roll(tail[x : x + 1], 32 * x) for x in range(4))] + own[0:2] + [jnp.zeros((5, 128), F32)]
        ends.append(jnp.concatenate([edge[at, 128 * j : 128 * j + 128] for j in range(4)] + tail, axis=0))
    me = along_gz()
    for p in range(8):
        message = jnp.where(me < p, ends[1], ends[0]).astype(BF16)
        for x in range(8):
            out_ref[8 * x + p] = message


def y_messages(slab_ref, l_ref, r_ref, in_ref, up_ref, dn_ref, bank_ref, beyond_ref):
    slabs = [l_ref] + [slab_ref.at[x] for x in range(4)] + [r_ref]
    first, last = [], []
    for xe, slab in enumerate(slabs):
        up_ref[xe * 64 : xe * 64 + 64, :] = slab[448:512, :]
        dn_ref[xe * 64 : xe * 64 + 64, :] = slab[0:64, :]
        vol = slab[512:544, :].astype(F32)
        first.append(vol[0:4])
        last.append(vol[28:32])
    fill = [jnp.zeros((8, 128), F32)]
    four = [jnp.zeros((4, 128), F32)]
    across, along = lax.axis_index("zl") * 4 + lax.axis_index("x"), along_gz()
    rows_up, rows_dn = [], []
    for side in range(2):
        other = along + 2 * side - 1
        inside = (other >= 0) & (other <= 7)
        other = jnp.clip(other, 0, 7)
        mid = jnp.where(inside, in_ref[8 * across + other].astype(F32), 0.0)
        before = in_ref[8 * jnp.maximum(across - 1, 0) + other].astype(F32)
        before = jnp.where(inside & (across > 0), before, 0.0)
        after = in_ref[8 * jnp.minimum(across + 1, 7) + other].astype(F32)
        after = jnp.where(inside & (across < 7), after, 0.0)
        parts = [
            jnp.concatenate(
                [before[4 * j + 3 : 4 * j + 4], mid[4 * j : 4 * j + 4], after[4 * j : 4 * j + 1]], axis=0
            )
            for j in range(4)
        ]
        tail = [before[16:17]] + [mid[16:17]] * 4 + [after[16:17]]
        tail = [roll(row, -32 * x) for row, x in zip(tail, (3, 0, 1, 2, 3, 0), strict=True)]
        parts.append(within(jnp.concatenate(tail, axis=0), 0, 32))
        for j in range(5):
            beyond_ref[8 * side : 8 * side + 8, 128 * j : 128 * j + 128] = jnp.concatenate(
                [parts[j], jnp.zeros((2, 128), F32)], axis=0
            )
        rows_up.append(within(roll(parts[3], -64), 0, 64) + within(roll(parts[4], 36), 64, 68))
        rows_dn.append(within(parts[0], 0, 64) + within(roll(parts[4], 64), 64, 68))
    up_ref[384:432, :] = jnp.concatenate(last + fill + rows_up + four, axis=0).astype(BF16)
    dn_ref[384:432, :] = jnp.concatenate(first + fill + rows_dn + four, axis=0).astype(BF16)
    bank = jnp.concatenate([in_ref[p, 16:24, :].astype(F32)[1:3] for p in range(64)], axis=0).astype(BF16)
    up_ref[432:560, :] = bank
    dn_ref[432:560, :] = bank
    bank_ref[...] = bank


def assemble(slab_ref, l_ref, r_ref, beyond_ref, yp_ref, yn_ref, e_ref, ve_ref):
    slabs = [l_ref] + [slab_ref.at[x] for x in range(4)] + [r_ref]
    along_y = lax.axis_index("zh")
    some, more = along_y > 0, along_y < 3
    before = jnp.where(some, yp_ref[384:432, :].astype(F32), 0.0)
    after = jnp.where(more, yn_ref[384:432, :].astype(F32), 0.0)
    for xe, slab in enumerate(slabs):
        e_ref[xe, 0:64, :] = jnp.where(some, yp_ref[xe * 64 : xe * 64 + 64, :].astype(F32), 0.0).astype(BF16)
        e_ref[xe, 64:576, :] = slab[0:512, :]
        e_ref[xe, 576:640, :] = jnp.where(more, yn_ref[xe * 64 : xe * 64 + 64, :].astype(F32), 0.0).astype(BF16)
        vol = slab[512:544, :].astype(F32)
        ve_ref[xe] = jnp.concatenate(
            [before[xe * 4 : xe * 4 + 4], vol, after[xe * 4 : xe * 4 + 4], jnp.zeros((8, 128), F32)], axis=0
        ).astype(BF16)
    ends = []
    for side in range(2):
        parts = [roll(beyond_ref[8 * side : 8 * side + 6, 128 * j : 128 * j + 128], 64) for j in range(5)]
        prev = before[32 + 6 * side : 38 + 6 * side]
        nxt = after[32 + 6 * side : 38 + 6 * side]
        tiles = [within(prev, 0, 64) + within(parts[0], 64, 128)]
        for k in range(1, 4):
            tiles.append(jnp.where(lanes() < 64, parts[k - 1], parts[k]))
        tiles.append(within(parts[3], 0, 64) + within(roll(nxt, 64), 64, 128))
        tiles.append(
            within(roll(prev, -64), 0, 4) + within(roll(parts[4], -60), 4, 36) + within(roll(nxt, -28), 36, 40)
        )
        ends.append(
            jnp.concatenate([jnp.concatenate(tiles, axis=1), jnp.zeros((10, 768), F32)], axis=0).astype(BF16)
        )
    return ends


def flatten(narrow):
    lane = lax.broadcasted_iota(jnp.int32, (1, 128), 1)
    rows = [jnp.zeros((1, 128), F32) for _ in range(33)]
    for c in range(32):
        row, at = divmod(108 * c, 128)
        moved = roll(jnp.where(lane < 108, narrow[c : c + 1], 0.0), at)
        if at + 108 <= 128:
            rows[row] = rows[row] + moved
        else:
            rows[row] = rows[row] + jnp.where(lane >= at, moved, 0.0)
            rows[row + 1] = rows[row + 1] + jnp.where(lane < at, moved, 0.0)
    return jnp.concatenate(rows[:32], axis=0)


def turned(yp_ref, yn_ref, own_ref, far_ref, rows_ref):
    me = lax.axis_index("zh")
    for by, ref, first in ((0, own_ref, 0), (3, yp_ref, 432), (1, yn_ref, 432), (2, far_ref, 0)):
        zh = (me + by) % 4
        for across in range(8):
            at = pl.multiple_of(64 * across + 16 * zh, 16)
            rows_ref[pl.ds(at, 16), :] = ref[first + 16 * across : first + 16 * across + 16, :].astype(F32)
    parts = []
    for q in range(4):
        parts.append(rows_ref[pl.ds(2 * q, 64, stride=8), :].T)
        parts.append(rows_ref[pl.ds(2 * q + 1, 64, stride=8), :].T[0:88])
    return jnp.concatenate(parts, axis=0).astype(BF16)


def narrow_lanes():
    row = lax.broadcasted_iota(jnp.int32, (512, 128), 0)
    col = lax.broadcasted_iota(jnp.int32, (512, 128), 1)
    group, inner = row // 48, row % 48
    a, c = group // 3, group % 3
    b, i = inner // 4, inner % 4
    return ((b < 3) & (group < 9) & (col == (9 * a + 3 * b + c) * 4 + i)).astype(F32)


def narrow_rows(w1_ref, out_ref):
    lane = lax.broadcasted_iota(jnp.int32, (1, 128), 1)
    rows = []
    for c in range(32):
        row, at = divmod(108 * c, 128)
        piece = roll(w1_ref[row : row + 1, :], -at)
        if at > 20:
            piece = jnp.where(lane < 128 - at, piece, roll(w1_ref[row + 1 : row + 2, :], -at))
        rows.append(jnp.where(lane < 108, piece, 0.0))
    bank = jnp.concatenate(rows, axis=0).astype(BF16)
    first = dot_nt(bank, narrow_lanes().astype(BF16))
    for y in range(8):
        out_ref[32 * y : 32 * y + 32, :] = roll(first, 4 * y).astype(BF16)


def gradients(
    slab_ref, l_ref, r_ref, beyond_ref, yp_ref, yn_ref, bank_ref, far_ref, wb_ref, out_ref, e_ref, ve_ref, ga_ref, rows_ref
):
    ends = assemble(slab_ref, l_ref, r_ref, beyond_ref, yp_ref, yn_ref, e_ref, ve_ref)
    lane = lax.broadcasted_iota(jnp.int32, (1, 128), 1)
    low, high = lane == 0, lane == 127
    eye = (
        lax.broadcasted_iota(jnp.int32, (48, 128), 0) == lax.broadcasted_iota(jnp.int32, (48, 128), 1)
    ).astype(F32).astype(BF16)
    left = dot_nt(eye, ends[0][:, 640:768])
    right = dot_nt(eye, ends[1][:, 640:768])
    shifted = []
    for xe in range(6):
        v = ve_ref[xe].astype(F32)
        shifted.append(
            (
                jnp.where(low, left[:, xe : xe + 1], roll(v, 1)).astype(BF16),
                ve_ref[xe],
                jnp.where(high, right[:, xe : xe + 1], roll(v, -1)).astype(BF16),
            )
        )
    rest = jnp.zeros((80, 128), BF16)
    patches = jnp.concatenate(
        [
            jnp.concatenate([shifted[x + a][c] for a in range(3) for c in range(3)] + [rest], axis=0)
            for x in range(4)
        ],
        axis=1,
    )
    pre = dot(wb_ref[...], patches)
    sig = 1.0 / (1.0 + jnp.exp(-pre))
    act = (pre * sig).astype(BF16)
    slope = sig * (1.0 + pre * (1.0 - sig))
    halos = []
    for end in ends:
        m = end[:, 0:640].astype(F32)
        halos.append(
            jnp.concatenate(
                [
                    jnp.concatenate([m[a : a + 4, 128 * k : 128 * k + 256] for a in range(3)], axis=1)
                    for k in range(4)
                ],
                axis=0,
            ).astype(BF16)
        )
    none = jnp.zeros((32, 64), BF16)
    weights = turned(yp_ref, yn_ref, bank_ref, far_ref, rows_ref)
    blocks = []
    for c in range(3):
        for yl in range(2):
            cells = []
            for a in range(3):
                for yp in range(4):
                    b = yp - yl
                    if 0 <= b <= 2:
                        tap = (2 - a) * 9 + (2 - b) * 3 + (2 - c)
                        cells.append(weights[tap * 32 : tap * 32 + 32])
                    else:
                        cells.append(none)
            blocks.append(jnp.concatenate(cells, axis=1))
    bank = jnp.concatenate(blocks, axis=0)
    from_left = dot_nt(bank[0:64], halos[0])
    from_right = dot_nt(bank[128:192], halos[1])
    for k in range(4):
        for xp in range(2):
            cells = jnp.concatenate(
                [
                    jnp.concatenate(
                        [e_ref[2 * xp + j + a, 128 * k : 128 * k + 256, :] for j in range(2)], axis=1
                    )
                    for a in range(3)
                ],
                axis=0,
            )
            v = dot(bank, cells)
            for j in range(2):
                x = 2 * xp + j
                at = slice(128 * j, 128 * j + 128)
                col = 4 * k + x
                ga_ref[64 * k : 64 * k + 64, 128 * x : 128 * x + 128] = (
                    v[64:128, at]
                    + jnp.where(low, from_left[:, col : col + 1], roll(v[0:64, at], 1))
                    + jnp.where(high, from_right[:, col : col + 1], roll(v[128:192, at], -1))
                )
    grad_pre = (ga_ref[...] * slope).astype(BF16)
    product = dot_nt(grad_pre, patches)
    total = product[0:32]
    for y in range(1, 8):
        total = total + roll(product[32 * y : 32 * y + 32], -4 * y)
    chosen = narrow_lanes()
    narrow = lax.dot_general(
        total,
        chosen,
        (((1,), (0,)), ((), ())),
        precision=lax.Precision.HIGHEST,
        preferred_element_type=F32,
    )
    act32 = act.astype(F32)
    before, after = [], []
    for x in range(4):
        part = act32[:, 128 * x : 128 * x + 128]
        before.append(jnp.where(low, 0.0, roll(part, 1)).astype(BF16))
        after.append(jnp.where(high, 0.0, roll(part, -1)).astype(BF16))
    before = jnp.concatenate(before, axis=1)
    after = jnp.concatenate(after, axis=1)
    empty = jnp.zeros((32, 512), BF16)
    rows = []
    for k in range(4):
        parts = []
        for yl in range(2):
            at = slice(64 * k + 32 * yl, 64 * k + 32 * yl + 32)
            parts += [before[at], act[at], after[at], empty]
        rows.append(jnp.concatenate(parts, axis=0))
    acts = jnp.concatenate(rows, axis=1)
    cots = jnp.concatenate(
        [
            jnp.concatenate(
                [e_ref[x + a, 128 * k : 128 * k + 256, :] for k in range(4) for x in range(4)], axis=1
            )
            for a in range(3)
        ],
        axis=0,
    )
    wide = dot_nt(cots, acts)
    row = lax.broadcasted_iota(jnp.int32, (16, 512), 0)
    lanes = lax.broadcasted_iota(jnp.int32, (16, 512), 1)
    pick = ((row < 4) & (lanes == row * 128)) | ((row >= 4) & (row < 8) & (lanes == (row - 4) * 128 + 127))
    edges = dot_nt(pick.astype(F32).astype(BF16), act)
    gap = jnp.zeros((4, 64), F32)
    one = jnp.zeros((4, 32), F32)
    table = []
    for k in range(4):
        e0 = edges[0:4, 64 * k : 64 * k + 32]
        e1 = edges[0:4, 64 * k + 32 : 64 * k + 64]
        table.append(jnp.concatenate([gap, e0, one, gap, e1, one], axis=1))
    for k in range(4):
        e0 = edges[4:8, 64 * k : 64 * k + 32]
        e1 = edges[4:8, 64 * k + 32 : 64 * k + 64]
        table.append(jnp.concatenate([e0, one, gap, e1, one, gap], axis=1))
    table = jnp.concatenate(table, axis=0).astype(BF16)
    wide = wide + dot_tn(jnp.concatenate(halos, axis=0), table)
    taps = []
    for a in range(3):
        for b in range(3):
            at = (2 - a) * 256 + (2 - b) * 64
            taps.append((wide[at : at + 64, 0:128] + wide[at + 64 : at + 128, 128:256])[:, 0:96])
    wide = jnp.concatenate(taps + [jnp.zeros((64, 32), F32)], axis=1)
    flat = flatten(narrow)
    for p in range(8):
        out_ref[p, :, 0:896] = wide[8 * p : 8 * p + 8]
        for j in range(4):
            out_ref[p, :, 896 + 128 * j : 1024 + 128 * j] = flat[8 * j : 8 * j + 8]


def second_stage(in_ref, out_ref):
    total = in_ref[0]
    for p in range(1, 8):
        total = total + in_ref[p]
    gap = jnp.zeros((1, 128), F32)
    for zh in range(4):
        out_ref[zh, :, 0:512] = total[:, 896:1408]
        for yh in range(2):
            row = 2 * zh + yh
            pieces = [total[row : row + 1, 128 * j : 128 * j + 128] for j in range(7)]
            out_ref[zh, :, 512 + 128 * yh : 640 + 128 * yh] = jnp.concatenate(pieces + [gap], axis=0)


def third_stage(in_ref, own_ref, out_ref):
    total = in_ref[0]
    for p in range(1, 4):
        total = total + in_ref[p]
    for p in range(8):
        yh = p // 4
        out_ref[p, :, 0:512] = total[:, 0:512]
        out_ref[p, :, 512:640] = total[:, 512 + 128 * yh : 640 + 128 * yh]
        out_ref[p, :, 640:768] = own_ref[...]


def moments(master, first, second, grad):
    first_new = 0.9 * first + 0.1 * grad
    second_new = 0.999 * second + 0.001 * grad * grad
    direction = (
        first_new / (1.0 - 0.9**10) / (jnp.sqrt(second_new / (1.0 - 0.999**10)) + 1e-06)
        + 0.01 * master
    )
    return (first_new, second_new, direction)


def runs():
    row = lax.broadcasted_iota(jnp.int32, (27, 128), 0)
    lane = lax.broadcasted_iota(jnp.int32, (27, 128), 1)
    start = (row * 128) // 108
    run = (row * 128 + lane) // 108
    return [(run == start + p, lane == start + p) for p in range(3)]


def run_sums(value):
    total = jnp.zeros((27, 128), F32)
    for inside, column in runs():
        part = jnp.sum(jnp.where(inside, value, 0.0), axis=1, keepdims=True)
        total = total + jnp.where(column, part, 0.0)
    return jnp.sum(total, axis=0, keepdims=True)


def run_spread(value):
    total = jnp.zeros((27, 128), F32)
    for inside, column in runs():
        part = jnp.sum(jnp.where(column, value, 0.0), axis=1, keepdims=True)
        total = total + jnp.where(inside, part, 0.0)
    return total


def update(in_ref, own_ref, m_ref, f_ref, s_ref, w2_ref, f2_ref, s2_ref, w1_ref, f1_ref, s1_ref):
    y = lax.axis_index("y")
    quarter = y % 2 * 2 + lax.axis_index("core")
    total = in_ref[0, :, 0:640]
    for p in range(1, 8):
        total = total + in_ref[p, :, 0:640]
    grad = total[:, 512:640]
    inside = (
        lax.broadcasted_iota(jnp.int32, (8, 128), 0) * 128 + lax.broadcasted_iota(jnp.int32, (8, 128), 1)
    ) < 864
    group = in_ref[pl.ds(y // 2 * 4, 4), :, 640:768]
    block = []
    for j in range(3):
        block.append(sum(place(group[q, 2 * j : 2 * j + 2], q) for q in range(4)))
    _, _, direction = moments(block[0], block[1], block[2], grad)
    direction = jnp.where(inside, direction, 0.0)
    ratio = jnp.sqrt(jnp.sum(block[0] * block[0], keepdims=True)) / (
        jnp.sqrt(jnp.sum(direction * direction, keepdims=True)) + 1e-06
    )
    mine = take(grad, 0)
    for q in range(1, 4):
        mine = jnp.where(quarter == q, take(grad, q), mine)
    master, first, second = (own_ref[2 * j : 2 * j + 2] for j in range(3))
    first_new, second_new, direction = moments(master, first, second, mine)
    for ref, value in (
        (w2_ref, master - 0.01 * (ratio * direction)),
        (f2_ref, first_new),
        (s2_ref, second_new),
    ):
        ref[...] = jnp.concatenate([value[0:1], value[1:2, 0:88]], axis=1)
    tiles = [total[:, 128 * j : 128 * j + 128] for j in range(4)]
    grad = jnp.concatenate(tiles, axis=0)[0:27]
    master = m_ref[...]
    first_new, second_new, direction = moments(master, f_ref[...], s_ref[...], grad)
    ratio = jnp.sqrt(run_sums(master * master)) / (jnp.sqrt(run_sums(direction * direction)) + 1e-06)
    w1_ref[...] = master - 0.01 * (run_spread(ratio) * direction)
    f1_ref[...] = first_new
    s1_ref[...] = second_new


def exchange(up, down, axes):
    size = lax.axis_size(axes)
    pairs = [(i, i + 1) for i in range(size - 1)]
    before = lax.ppermute(up, axes, pairs)
    after = lax.ppermute(down, axes, [(j, i) for i, j in pairs])
    return before, after


def local(volume, cotangent, w1_master, w1_first, w1_second, w2_master, w2_first, w2_second):
    wide = [w.reshape(1, 216) for w in (w2_master, w2_first, w2_second)]
    narrow = [w.reshape(27, 128) for w in (w1_master, w1_first, w1_second)]
    narrow_band = call(narrow_rows, shape((256, 512), BF16), narrow[0])
    face, along_y = shape((544, 128), BF16), shape((560, 128), BF16)
    slabs, up, down, message, own = call(
        pack,
        (shape((4, 544, 128), BF16), face, face, shape((64, 24, 128), BF16), shape((8, 128), F32)),
        cotangent.reshape(2048, 128),
        volume.reshape(128, 128),
        *wide,
        scratch=(
            pltpu.VMEM((2048, 128), BF16),
            pltpu.VMEM((128, 128), BF16),
            pltpu.VMEM((1, 216), F32),
            pltpu.VMEM((1, 216), F32),
            pltpu.VMEM((1, 216), F32),
            pltpu.VMEM((2048, 128), F32),
            pltpu.VMEM((128, 128), F32),
            pltpu.SemaphoreType.DMA((5,)),
        ),
        space=pl.BlockSpec(memory_space=pltpu.HBM),
    )
    before_x, after_x = exchange(up, down, GX)
    message = lax.all_to_all(message, GX + GZ, 0, 0, tiled=True)
    up, down, bank, beyond = call(
        y_messages,
        (along_y, along_y, shape((128, 128), BF16), shape((16, 640), F32)),
        slabs,
        before_x,
        after_x,
        message,
    )
    before_y, after_y, far = (
        lax.ppermute(part, GY, [(i, (i + by) % 4) for i in range(4)])
        for part, by in ((up, 1), (down, 3), (bank, 2))
    )
    sums = call(
        gradients,
        shape((8, 8, 1408), F32),
        slabs,
        before_x,
        after_x,
        beyond,
        before_y,
        after_y,
        bank,
        far,
        narrow_band,
        scratch=(
            pltpu.VMEM((6, 640, 128), BF16),
            pltpu.VMEM((6, 48, 128), BF16),
            pltpu.VMEM((256, 512), F32),
            pltpu.VMEM((512, 128), F32),
        ),
    )
    sums = lax.all_to_all(sums, GX, 0, 0, tiled=True)
    sums = call(second_stage, shape((4, 8, 768), F32), sums)
    sums = lax.all_to_all(sums, GY, 0, 0, tiled=True)
    sums = call(third_stage, shape((8, 8, 768), F32), sums, own)
    sums = lax.all_to_all(sums, GZ, 0, 0, tiled=True)
    one, rows = shape((1, 216), F32), shape((27, 128), F32)
    new = call(update, (one, one, one, rows, rows, rows), sums, own, *narrow)
    return tuple(w.reshape(-1) for w in new[3:] + new[:3])


def solution(mesh):
    parts = Mesh(mesh.devices.reshape(2, 4, 4, 4, 2), GX + GY + GZ)
    field = P(None, GX, GY, GZ)
    owned = P(GX + GY + GZ)
    return jax.shard_map(
        local,
        mesh=parts,
        in_specs=(field, field, P(), P(), P(), owned, owned, owned),
        out_specs=(P(), P(), P(), owned, owned, owned),
        check_vma=False,
    )
```

time: 94.6 us -> 83.9 us (0.89)
  starting transfers between devices: 45.5 us -> 24.6 us
  blocking collectives: 18.6 us -> 38.2 us
  local copies, waits for them, and re-layouts: 9.44 us -> 2.5 us
  waiting for transfers between devices: 13.2 us -> 9.32 us
  Pallas kernels: 5.4 us -> 8.08 us
    all_to_all x1 -> x3, blocking collectives: 18.6 us -> 38.2 us  [the longest x1 14.3 us: local(): sums = lax.all_to_all(sums, GZ, 0, 0, tiled=True)]
    all_to_all x3 -> x1, starting transfers between devices: 27.5 us -> 10.4 us  [local(): message = lax.all_to_all(message, GX + GZ, 0, 0, tiled=True)]
    all_to_all x3 -> x1, waiting for transfers between devices: 12.5 us -> 1.12 us  [local(): message = lax.all_to_all(message, GX + GZ, 0, 0, tiled=True)]
    ppermute x3 -> x1, starting transfers between devices: 13.5 us -> 3.3 us  [exchange(): before = lax.ppermute(up, axes, pairs)]
    ppermute x0 -> x3, starting transfers between devices: none -> 9.6 us  [local(): lax.ppermute(part, GY, [(i, (i + by) % 4) for i in range(4)])]
    reshape x9 -> x0, local copies, waits for them, and re-layouts: 3.52 us -> none  [the longest x1 1.59 us: local(): cotangent.reshape(2, 4, 4, 2, 4, 8, 128).transpose(4, 5, 0, 2, 1, 3, 6)]
    ppermute x3 -> x1, starting transfers between devices: 4.5 us -> 1.29 us  [exchange(): after = lax.ppermute(down, axes, [(j, i) for i, j in pairs])]
    ppermute x0 -> x3, waiting for transfers between devices: none -> 3.03 us  [local(): lax.ppermute(part, GY, [(i, (i + by) % 4) for i in range(4)])]
  transfers between devices with their start and end apart: 9 -> 6, of which waited for: 3 -> 5; matrix products, arithmetic and copies ran while one was open for 5% -> 0% of each run, Pallas kernels for 0% -> 1%
where the time goes in v2:
time: 83.9 us; the launch traced here: 83.4 us
  blocking collectives  38.2 us (46%)
  starting transfers between devices  24.6 us (29%)
  waiting for transfers between devices  9.32 us (11%)
  Pallas kernels  8.08 us (10%)
  local copies, waits for them, and re-layouts  2.5 us (3%)
    all_to_all x1, blocking collectives, local(): sums = lax.all_to_all(sums, GZ, 0, 0, tiled=True)  14.3 us
    all_to_all x1, blocking collectives, local(): sums = lax.all_to_all(sums, GY, 0, 0, tiled=True)  12.3 us
    all_to_all x1, blocking collectives, local(): sums = lax.all_to_all(sums, GX, 0, 0, tiled=True)  11.6 us
    all_to_all x1, starting transfers between devices, local(): message = lax.all_to_all(message, GX + GZ, 0, 0, tiled=True)  10.4 us
    ppermute x3, starting transfers between devices, local(): lax.ppermute(part, GY, [(i, (i + by) % 4) for i in range(4)])  9.6 us
    pallas_call x7, Pallas kernels, call(): pl.pallas_call(kernel, out_shape=out_shapes, in_specs=[space] * len(args)...  8.08 us
    ppermute x1, starting transfers between devices, exchange(): before = lax.ppermute(up, axes, pairs)  3.3 us
    ppermute x3, waiting for transfers between devices, local(): lax.ppermute(part, GY, [(i, (i + by) % 4) for i in range(4)])  3.03 us
  transfers between devices with their start and end apart: 6, of which 5 were waited for; matrix products, arithmetic and copies ran while one was open for 0% of the time, Pallas kernels for 1%

profile of v2, /device:TPU:1, one launch (start us, length us, event | category | flops | bytes accessed | tf_op | source)
XLA Modules:
  0.0 83.4 jit_solution(17407828773582686913)
XLA Ops:
  0.7 0.7 copy-done.6
  1.3 0.0 copy-done.7
  1.3 0.0 copy-done.5
  1.3 1.0 %copy-done = bf16[64,4,8,128]{3,2,1,0:T(8,128)(2,1)S(1)} copy-done((bf16[64,4,8,128]{3,2,1,0:T(8,128)(2,1)S(1)}, bf16[64,4,8,128]{3,2,1,0:T(8,128)(2,1)}, u32[]{:S(2)}) %copy-start) | copy-done | bytes 524312
  2.4 0.8 copy-done.2
  3.1 2.0 %shard_map.127 = (bf16[4,544,128]{2,1,0:T(8,128)(2,1)S(1)}, bf16[544,128]{1,0:T(8,128)(2,1)S(1)}, bf16[544,128]{1,0:T(8,128)(2,1)S(1)}, bf16[64,24,128]{2,1,0:T(8,128)(2,1)}, f32[8,128]{1,0:T(8,128)S(1)}) custom-call(bf16[2048,128]{1,0:T(8,128)(2,1)S(1)} %bitcast.14, bf16[128,128]{1,0:T(8,128)(2,1)S(1)} %bitcast.17, f32[1,216]{1,0:T(1,128)S(1)} %bitcast.20, ...), custom_call_target="tpu_custom_call" | custom-call | tf_op jit(solution)/shard_map/pallas_call | solution.py:33
  5.2 10.4 %all-to-all-start = ((bf16[64,24,128]{2,1,0:T(8,128)(2,1)}), bf16[64,24,128]{2,1,0:T(8,128)(2,1)S(1)}, u32[]{:S(2)}, u32[]{:S(2)}) async-start(bf16[64,24,128]{2,1,0:T(8,128)(2,1)} %get-tuple-element.24), calls=%async_computation | async-start | bytes 786432 | tf_op jit(solution)/shard_map/all_to_all | solution.py:547
  15.5 3.3 %collective-permute-start = (bf16[544,128]{1,0:T(8,128)(2,1)S(1)}, bf16[544,128]{1,0:T(8,128)(2,1)S(1)}, u32[]{:S(2)}, u32[]{:S(2)}) collective-permute-start(bf16[544,128]{1,0:T(8,128)(2,1)S(1)} %get-tuple-element.22), channel_id=1, source_target_pairs={{0,32},{32,64},{64,96},{96,128},{128,160},{160,192},{192,224},{1,3... | collective-permute-start | bytes 417800 | tf_op jit(solution)/shard_map/ppermute | solution.py:518
  18.8 1.3 %collective-permute-start.1 = (bf16[544,128]{1,0:T(8,128)(2,1)S(1)}, bf16[544,128]{1,0:T(8,128)(2,1)S(1)}, u32[]{:S(2)}, u32[]{:S(2)}) collective-permute-start(bf16[544,128]{1,0:T(8,128)(2,1)S(1)} %get-tuple-element.23), channel_id=1, source_target_pairs={{32,0},{64,32},{96,64},{128,96},{160,128},{192,160},{224,192},{33,... | collective-permute-start | bytes 417800 | tf_op jit(solution)/shard_map/ppermute | solution.py:519
  20.1 3.0 %collective-permute-done.l_ref = bf16[544,128]{1,0:T(8,128)(2,1)S(1)} collective-permute-done((bf16[544,128]{1,0:T(8,128)(2,1)S(1)}, bf16[544,128]{1,0:T(8,128)(2,1)S(1)}, u32[]{:S(2)}, u32[]{:S(2)}) %collective-permute-start) | collective-permute-done | bytes 139296 | tf_op jit(solution)/shard_map/ppermute | solution.py:518
  23.1 2.2 %collective-permute-done.1.r_ref = bf16[544,128]{1,0:T(8,128)(2,1)S(1)} collective-permute-done((bf16[544,128]{1,0:T(8,128)(2,1)S(1)}, bf16[544,128]{1,0:T(8,128)(2,1)S(1)}, u32[]{:S(2)}, u32[]{:S(2)}) %collective-permute-start.1) | collective-permute-done | bytes 139296 | tf_op jit(solution)/shard_map/ppermute | solution.py:519
  25.3 1.1 %all-to-all-done.in_ref = bf16[64,24,128]{2,1,0:T(8,128)(2,1)S(1)} async-done(((bf16[64,24,128]{2,1,0:T(8,128)(2,1)}), bf16[64,24,128]{2,1,0:T(8,128)(2,1)S(1)}, u32[]{:S(2)}, u32[]{:S(2)}) %all-to-all-start) | async-done | bytes 393248 | tf_op jit(solution)/shard_map/all_to_all | solution.py:547
  26.4 0.2 shard_map.128
  26.6 3.0 %collective-permute-start.2 = (bf16[560,128]{1,0:T(8,128)(2,1)S(1)}, bf16[560,128]{1,0:T(8,128)(2,1)S(1)}, u32[]{:S(2)}, u32[]{:S(2)}) collective-permute-start(bf16[560,128]{1,0:T(8,128)(2,1)S(1)} %get-tuple-element.26), channel_id=1, source_target_pairs={{0,8},{8,16},{16,24},{24,0},{1,9},{9,17},{17,25},{25,1},{2,10},{10... | collective-permute-start | bytes 430088 | tf_op jit(solution)/shard_map/ppermute | solution.py:557
  29.6 2.2 %collective-permute-start.3 = (bf16[560,128]{1,0:T(8,128)(2,1)S(1)}, bf16[560,128]{1,0:T(8,128)(2,1)S(1)}, u32[]{:S(2)}, u32[]{:S(2)}) collective-permute-start(bf16[560,128]{1,0:T(8,128)(2,1)S(1)} %get-tuple-element.27), channel_id=1, source_target_pairs={{0,24},{8,0},{16,8},{24,16},{1,25},{9,1},{17,9},{25,17},{2,26},{10... | collective-permute-start | bytes 430088 | tf_op jit(solution)/shard_map/ppermute | solution.py:557
  31.8 4.4 %collective-permute-start.4 = (bf16[128,128]{1,0:T(8,128)(2,1)S(1)}, bf16[128,128]{1,0:T(8,128)(2,1)S(1)}, u32[]{:S(2)}, u32[]{:S(2)}) collective-permute-start(bf16[128,128]{1,0:T(8,128)(2,1)S(1)} %get-tuple-element.28.bank_ref), channel_id=1, source_target_pairs={{0,16},{8,24},{16,0},{24,8},{1,17},{9,25},{17,1},{25,9},{2,18},{10... | collective-permute-start | bytes 98312 | tf_op jit(solution)/shard_map/ppermute | solution.py:557
  36.2 0.9 %shard_map.129.wb_ref = bf16[256,512]{1,0:T(8,128)(2,1)S(1)} custom-call(f32[27,128]{1,0:T(8,128)S(1)} %bitcast.15), custom_call_target="tpu_custom_call" | custom-call | tf_op jit(solution)/shard_map/pallas_call | solution.py:33
  37.1 1.8 %collective-permute-done.4.far_ref = bf16[128,128]{1,0:T(8,128)(2,1)S(1)} collective-permute-done((bf16[128,128]{1,0:T(8,128)(2,1)S(1)}, bf16[128,128]{1,0:T(8,128)(2,1)S(1)}, u32[]{:S(2)}, u32[]{:S(2)}) %collective-permute-start.4) | collective-permute-done | bytes 32800 | tf_op jit(solution)/shard_map/ppermute | solution.py:557
  38.9 1.2 %collective-permute-done.3.yn_ref = bf16[560,128]{1,0:T(8,128)(2,1)S(1)} collective-permute-done((bf16[560,128]{1,0:T(8,128)(2,1)S(1)}, bf16[560,128]{1,0:T(8,128)(2,1)S(1)}, u32[]{:S(2)}, u32[]{:S(2)}) %collective-permute-start.3) | collective-permute-done | bytes 143392 | tf_op jit(solution)/shard_map/ppermute | solution.py:557
  40.1 4.1 %shard_map.130 = f32[8,8,1408]{2,1,0:T(8,128)S(1)} custom-call(bf16[4,544,128]{2,1,0:T(8,128)(2,1)S(1)} %get-tuple-element.21.slab_ref, bf16[544,128]{1,0:T(8,128)(2,1)S(1)} %collective-permute-done.l_ref, bf16[544,128]{1,0:T(8,128)(2,1)S(1)} %collective-permute-done.1.r_ref, f32[16,640]{1,0:T(8,128)S(1)} %get-tuple-element.25.beyond_ref, ...), custom_call_target="tpu_custom_call" | custom-call | tf_op jit(solution)/shard_map/pallas_call | solution.py:33
  44.2 11.6 %all_to_all.20.in_ref = f32[8,8,1408]{2,1,0:T(8,128)S(1)} all-to-all(f32[8,8,1408]{2,1,0:T(8,128)S(1)} %shard_map.130), channel_id=1, replica_groups=mesh['zl'=2,'x'=4,'zh'=4,'y'=4,'core'=2] {'zl','x'}, dimensions={0} | all-to-all | bytes 720896 | tf_op jit(solution)/shard_map/all_to_all | solution.py:579
  55.8 12.3 %all_to_all.21.in_ref = f32[4,8,768]{2,1,0:T(8,128)S(1)} all-to-all(f32[4,8,768]{2,1,0:T(8,128)S(1)} %shard_map.131), channel_id=1, replica_groups=mesh['zl'=2,'x'=4,'zh'=4,'y'=4,'core'=2] {'zh'}, dimensions={0} | all-to-all | bytes 196608 | tf_op jit(solution)/shard_map/all_to_all | solution.py:581
  68.2 14.3 %all_to_all.22.in_ref = f32[8,8,768]{2,1,0:T(8,128)S(1)} all-to-all(f32[8,8,768]{2,1,0:T(8,128)S(1)} %shard_map.132), channel_id=1, replica_groups=mesh['zl'=2,'x'=4,'zh'=4,'y'=4,'core'=2] {'y','core'}, dimensions={0} | all-to-all | bytes 393216 | tf_op jit(solution)/shard_map/all_to_all | solution.py:583
  82.5 0.9 %shard_map.133 = (f32[1,216]{1,0:T(1,128)}, f32[1,216]{1,0:T(1,128)}, f32[1,216]{1,0:T(1,128)}, f32[27,128]{1,0:T(8,128)}, f32[27,128]{1,0:T(8,128)}, /*index=5*/f32[27,128]{1,0:T(8,128)}) custom-call(f32[8,8,768]{2,1,0:T(8,128)S(1)} %all_to_all.22.in_ref, f32[8,128]{1,0:T(8,128)S(1)} %get-tuple-element.29.own_ref, f32[27,128]{1,0:T(8,128)S(1)} %bitcast.16, ...), custom_call_target="tpu_custom_call" | custom-call | tf_op jit(solution)/shard_map/pallas_call | solution.py:33
  (14 shorter events, 0.1 us)
Async XLA Ops:
  0.6 0.7 copy-start.6
  0.6 0.7 copy-start.7
  0.7 0.7 copy-start.5
  1.3 1.0 %copy-start = (bf16[64,4,8,128]{3,2,1,0:T(8,128)(2,1)S(1)}, bf16[64,4,8,128]{3,2,1,0:T(8,128)(2,1)}, u32[]{:S(2)}) copy-start(bf16[64,4,8,128]{3,2,1,0:T(8,128)(2,1)} %param.9) | copy-start | bytes 1572868
  2.4 0.8 copy-start.2
  5.2 21.3 %all-to-all-start = ((bf16[64,24,128]{2,1,0:T(8,128)(2,1)}), bf16[64,24,128]{2,1,0:T(8,128)(2,1)S(1)}, u32[]{:S(2)}, u32[]{:S(2)}) async-start(bf16[64,24,128]{2,1,0:T(8,128)(2,1)} %get-tuple-element.24), calls=%async_computation | async-start | bytes 786432 | tf_op jit(solution)/shard_map/all_to_all | solution.py:547
  15.5 7.6 %collective-permute-start = (bf16[544,128]{1,0:T(8,128)(2,1)S(1)}, bf16[544,128]{1,0:T(8,128)(2,1)S(1)}, u32[]{:S(2)}, u32[]{:S(2)}) collective-permute-start(bf16[544,128]{1,0:T(8,128)(2,1)S(1)} %get-tuple-element.22), channel_id=1, source_target_pairs={{0,32},{32,64},{64,96},{96,128},{128,160},{160,192},{192,224},{1,3... | collective-permute-start | bytes 417800 | tf_op jit(solution)/shard_map/ppermute | solution.py:518
  18.8 6.5 %collective-permute-start.1 = (bf16[544,128]{1,0:T(8,128)(2,1)S(1)}, bf16[544,128]{1,0:T(8,128)(2,1)S(1)}, u32[]{:S(2)}, u32[]{:S(2)}) collective-permute-start(bf16[544,128]{1,0:T(8,128)(2,1)S(1)} %get-tuple-element.23), channel_id=1, source_target_pairs={{32,0},{64,32},{96,64},{128,96},{160,128},{192,160},{224,192},{33,... | collective-permute-start | bytes 417800 | tf_op jit(solution)/shard_map/ppermute | solution.py:519
  26.4 9.8 %copy-start.1 = (f32[3456]{0:T(1024)S(1)}, f32[3456]{0:T(1024)}, u32[]{:S(2)}) copy-start(f32[3456]{0:T(1024)} %param.10) | copy-start | bytes 41476
  26.6 12.3 %collective-permute-start.2 = (bf16[560,128]{1,0:T(8,128)(2,1)S(1)}, bf16[560,128]{1,0:T(8,128)(2,1)S(1)}, u32[]{:S(2)}, u32[]{:S(2)}) collective-permute-start(bf16[560,128]{1,0:T(8,128)(2,1)S(1)} %get-tuple-element.26), channel_id=1, source_target_pairs={{0,8},{8,16},{16,24},{24,0},{1,9},{9,17},{17,25},{25,1},{2,10},{10... | collective-permute-start | bytes 430088 | tf_op jit(solution)/shard_map/ppermute | solution.py:557
  29.6 10.5 %collective-permute-start.3 = (bf16[560,128]{1,0:T(8,128)(2,1)S(1)}, bf16[560,128]{1,0:T(8,128)(2,1)S(1)}, u32[]{:S(2)}, u32[]{:S(2)}) collective-permute-start(bf16[560,128]{1,0:T(8,128)(2,1)S(1)} %get-tuple-element.27), channel_id=1, source_target_pairs={{0,24},{8,0},{16,8},{24,16},{1,25},{9,1},{17,9},{25,17},{2,26},{10... | collective-permute-start | bytes 430088 | tf_op jit(solution)/shard_map/ppermute | solution.py:557
  31.8 7.1 %collective-permute-start.4 = (bf16[128,128]{1,0:T(8,128)(2,1)S(1)}, bf16[128,128]{1,0:T(8,128)(2,1)S(1)}, u32[]{:S(2)}, u32[]{:S(2)}) collective-permute-start(bf16[128,128]{1,0:T(8,128)(2,1)S(1)} %get-tuple-element.28.bank_ref), channel_id=1, source_target_pairs={{0,16},{8,24},{16,0},{24,8},{1,17},{9,25},{17,1},{25,9},{2,18},{10... | collective-permute-start | bytes 98312 | tf_op jit(solution)/shard_map/ppermute | solution.py:557
  68.2 14.3 %copy-start.3 = (f32[3456]{0:T(1024)S(1)}, f32[3456]{0:T(1024)}, u32[]{:S(2)}) copy-start(f32[3456]{0:T(1024)} %param.11) | copy-start | bytes 41476
  68.2 14.3 %copy-start.4 = (f32[3456]{0:T(1024)S(1)}, f32[3456]{0:T(1024)}, u32[]{:S(2)}) copy-start(f32[3456]{0:T(1024)} %param.12) | copy-start | bytes 41476

commit v3 on v2

--- a/solution.py
+++ b/solution.py
@@ -29,14 +29,14 @@
     return lax.dot_general(a, b, (((0,), (0,)), ((), ())), preferred_element_type=F32)
 
 
-def call(kernel, out_shapes, *args, scratch=(), space=VMEM):
+def call(kernel, out_shapes, *args, scratch=(), space=VMEM, params=PARAMS):
     return pl.pallas_call(
         kernel,
         out_shape=out_shapes,
         in_specs=[space] * len(args),
         out_specs=jax.tree.map(lambda _: VMEM, out_shapes),
         scratch_shapes=scratch,
-        compiler_params=PARAMS,
+        compiler_params=params,
     )(*args)
 
 
@@ -131,7 +131,12 @@
             out_ref[8 * x + p] = message
 
 
-def y_messages(slab_ref, l_ref, r_ref, in_ref, up_ref, dn_ref, bank_ref, beyond_ref):
+def bank_rows(in_ref, out_ref):
+    rows = [in_ref[p, 16:24, :].astype(F32)[1:3] for p in range(64)]
+    out_ref[...] = jnp.concatenate(rows, axis=0).astype(BF16)
+
+
+def y_messages(slab_ref, l_ref, r_ref, in_ref, bank_ref, up_ref, dn_ref, beyond_ref):
     slabs = [l_ref] + [slab_ref.at[x] for x in range(4)] + [r_ref]
     first, last = [], []
     for xe, slab in enumerate(slabs):
@@ -170,10 +175,8 @@
         rows_dn.append(within(parts[0], 0, 64) + within(roll(parts[4], 64), 64, 68))
     up_ref[384:432, :] = jnp.concatenate(last + fill + rows_up + four, axis=0).astype(BF16)
     dn_ref[384:432, :] = jnp.concatenate(first + fill + rows_dn + four, axis=0).astype(BF16)
-    bank = jnp.concatenate([in_ref[p, 16:24, :].astype(F32)[1:3] for p in range(64)], axis=0).astype(BF16)
-    up_ref[432:560, :] = bank
-    dn_ref[432:560, :] = bank
-    bank_ref[...] = bank
+    up_ref[432:560, :] = bank_ref[...]
+    dn_ref[432:560, :] = bank_ref[...]
 
 
 def assemble(slab_ref, l_ref, r_ref, beyond_ref, yp_ref, yn_ref, e_ref, ve_ref):
@@ -245,7 +248,7 @@
     return ((b < 3) & (group < 9) & (col == (9 * a + 3 * b + c) * 4 + i)).astype(F32)
 
 
-def narrow_rows(w1_ref, out_ref):
+def narrow_rows(w1_ref, out_ref, pick_ref):
     lane = lax.broadcasted_iota(jnp.int32, (1, 128), 1)
     rows = []
     for c in range(32):
@@ -255,13 +258,17 @@
             piece = jnp.where(lane < 128 - at, piece, roll(w1_ref[row + 1 : row + 2, :], -at))
         rows.append(jnp.where(lane < 108, piece, 0.0))
     bank = jnp.concatenate(rows, axis=0).astype(BF16)
-    first = dot_nt(bank, narrow_lanes().astype(BF16))
+    pick = narrow_lanes().astype(BF16)
+    pick_ref[...] = pick
+    first = dot_nt(bank, pick)
     for y in range(8):
         out_ref[32 * y : 32 * y + 32, :] = roll(first, 4 * y).astype(BF16)
 
 
 def gradients(
-    slab_ref, l_ref, r_ref, beyond_ref, yp_ref, yn_ref, bank_ref, far_ref, wb_ref, out_ref, e_ref, ve_ref, ga_ref, rows_ref
+    slab_ref, l_ref, r_ref, beyond_ref, yp_ref, yn_ref, bank_ref, far_ref, wb_ref, pick_ref, sib_ref,
+    keep_ref, send_ref,
+    e_ref, ve_ref, ga_ref, rows_ref, wide_ref,
 ):
     ends = assemble(slab_ref, l_ref, r_ref, beyond_ref, yp_ref, yn_ref, e_ref, ve_ref)
     lane = lax.broadcasted_iota(jnp.int32, (1, 128), 1)
@@ -349,14 +356,12 @@
     total = product[0:32]
     for y in range(1, 8):
         total = total + roll(product[32 * y : 32 * y + 32], -4 * y)
-    chosen = narrow_lanes()
-    narrow = lax.dot_general(
-        total,
-        chosen,
-        (((1,), (0,)), ((), ())),
-        precision=lax.Precision.HIGHEST,
-        preferred_element_type=F32,
-    )
+    split, rest = [], total
+    for _ in range(3):
+        split.append(rest.astype(BF16))
+        rest = rest - split[-1].astype(F32)
+    picked = dot(jnp.concatenate(split, axis=0), pick_ref[...])
+    narrow = picked[0:32] + (picked[32:64] + picked[64:96])
     act32 = act.astype(F32)
     before, after = [], []
     for x in range(4):
@@ -408,34 +413,51 @@
             taps.append((wide[at : at + 64, 0:128] + wide[at + 64 : at + 128, 128:256])[:, 0:96])
     wide = jnp.concatenate(taps + [jnp.zeros((64, 32), F32)], axis=1)
     flat = flatten(narrow)
+    for j in range(7):
+        wide_ref[64 * j : 64 * j + 64, :] = wide[:, 128 * j : 128 * j + 128]
+    core = lax.axis_index("core")
+    gap = jnp.zeros((4, 128), F32)
     for p in range(8):
-        out_ref[p, :, 0:896] = wide[8 * p : 8 * p + 8]
-        for j in range(4):
-            out_ref[p, :, 896 + 128 * j : 1024 + 128 * j] = flat[8 * j : 8 * j + 8]
+        zl, zh = p // 4, p % 4
+        halves = []
+        for yh in range(2):
+            rows = [
+                wide_ref[pl.ds(64 * j + 32 * zl + 2 * zh + yh, 4, stride=8), :] for j in range(7)
+            ]
+            under = [rows[6]] + [flat[16 * yh + 4 * j : 16 * yh + 4 * j + 4] for j in range(4)] + [gap]
+            halves.append(
+                jnp.concatenate([jnp.concatenate(rows[0:6], axis=1), jnp.concatenate(under, axis=1)], axis=0)
+            )
+        keep_ref[p] = jnp.where(core == 0, halves[0], halves[1])
+        send_ref[p] = jnp.where(core == 0, halves[1], halves[0])
+
+
+def first_stage(a_ref, b_ref, out_ref):
+    out_ref[...] = a_ref[...] + b_ref[...]
 
 
 def second_stage(in_ref, out_ref):
     total = in_ref[0]
     for p in range(1, 8):
         total = total + in_ref[p]
-    gap = jnp.zeros((1, 128), F32)
-    for zh in range(4):
-        out_ref[zh, :, 0:512] = total[:, 896:1408]
-        for yh in range(2):
-            row = 2 * zh + yh
-            pieces = [total[row : row + 1, 128 * j : 128 * j + 128] for j in range(7)]
-            out_ref[zh, :, 512 + 128 * yh : 640 + 128 * yh] = jnp.concatenate(pieces + [gap], axis=0)
-
-
-def third_stage(in_ref, own_ref, out_ref):
+    narrow = [total[4:8, 128 * j : 128 * j + 128] for j in range(1, 5)]
+    for x in range(4):
+        block = [total[x : x + 1, 128 * j : 128 * j + 128] for j in range(6)]
+        block += [total[4 + x : 5 + x, 0:128], jnp.zeros((1, 128), F32)]
+        rows = jnp.concatenate(block + narrow, axis=0)
+        for y in range(4):
+            out_ref[4 * x + y] = rows
+
+
+def third_stage(in_ref, own_ref, sib_ref, out_ref):
     total = in_ref[0]
-    for p in range(1, 4):
+    for p in range(1, 16):
         total = total + in_ref[p]
-    for p in range(8):
-        yh = p // 4
-        out_ref[p, :, 0:512] = total[:, 0:512]
-        out_ref[p, :, 512:640] = total[:, 512 + 128 * yh : 640 + 128 * yh]
-        out_ref[p, :, 640:768] = own_ref[...]
+    out_ref[0:24, :] = total
+    even = lax.axis_index("y") % 2 == 0
+    own, sib = own_ref[...], sib_ref[...]
+    out_ref[24:32, :] = jnp.where(even, own, sib)
+    out_ref[32:40, :] = jnp.where(even, sib, own)
 
 
 def moments(master, first, second, grad):
@@ -472,20 +494,19 @@
     return total
 
 
-def update(in_ref, own_ref, m_ref, f_ref, s_ref, w2_ref, f2_ref, s2_ref, w1_ref, f1_ref, s1_ref):
-    y = lax.axis_index("y")
-    quarter = y % 2 * 2 + lax.axis_index("core")
-    total = in_ref[0, :, 0:640]
-    for p in range(1, 8):
-        total = total + in_ref[p, :, 0:640]
-    grad = total[:, 512:640]
+def update(in_ref, other_ref, own_ref, m_ref, f_ref, s_ref, w2_ref, f2_ref, s2_ref, w1_ref, f1_ref, s1_ref):
+    y, core = lax.axis_index("y"), lax.axis_index("core")
+    quarter = y % 2 * 2 + core
+    mine, other = in_ref[...], other_ref[...]
+    low, high = jnp.where(core == 0, mine, other), jnp.where(core == 0, other, mine)
+    grad = jnp.where(y // 2 == 0, low[0:8], high[0:8])
     inside = (
         lax.broadcasted_iota(jnp.int32, (8, 128), 0) * 128 + lax.broadcasted_iota(jnp.int32, (8, 128), 1)
     ) < 864
-    group = in_ref[pl.ds(y // 2 * 4, 4), :, 640:768]
     block = []
     for j in range(3):
-        block.append(sum(place(group[q, 2 * j : 2 * j + 2], q) for q in range(4)))
+        parts = [half[at + 2 * j : at + 2 * j + 2] for at in (24, 32) for half in (low, high)]
+        block.append(sum(place(part, q) for q, part in enumerate(parts)))
     _, _, direction = moments(block[0], block[1], block[2], grad)
     direction = jnp.where(inside, direction, 0.0)
     ratio = jnp.sqrt(jnp.sum(block[0] * block[0], keepdims=True)) / (
@@ -502,8 +523,7 @@
         (s2_ref, second_new),
     ):
         ref[...] = jnp.concatenate([value[0:1], value[1:2, 0:88]], axis=1)
-    tiles = [total[:, 128 * j : 128 * j + 128] for j in range(4)]
-    grad = jnp.concatenate(tiles, axis=0)[0:27]
+    grad = jnp.concatenate([low[8:24], high[8:24]], axis=0)[0:27]
     master = m_ref[...]
     first_new, second_new, direction = moments(master, f_ref[...], s_ref[...], grad)
     ratio = jnp.sqrt(run_sums(master * master)) / (jnp.sqrt(run_sums(direction * direction)) + 1e-06)
@@ -520,10 +540,18 @@
     return before, after
 
 
+def turn(value, by):
+    return lax.ppermute(value, GY, [(i, (i + by) % 4) for i in range(4)])
+
+
+def swap(value):
+    return lax.ppermute(value, "core", [(0, 1), (1, 0)])
+
+
 def local(volume, cotangent, w1_master, w1_first, w1_second, w2_master, w2_first, w2_second):
     wide = [w.reshape(1, 216) for w in (w2_master, w2_first, w2_second)]
     narrow = [w.reshape(27, 128) for w in (w1_master, w1_first, w1_second)]
-    narrow_band = call(narrow_rows, shape((256, 512), BF16), narrow[0])
+    narrow_band, pick = call(narrow_rows, (shape((256, 512), BF16), shape((512, 128), BF16)), narrow[0])
     face, along_y = shape((544, 128), BF16), shape((560, 128), BF16)
     slabs, up, down, message, own = call(
         pack,
@@ -542,24 +570,20 @@
             pltpu.SemaphoreType.DMA((5,)),
         ),
         space=pl.BlockSpec(memory_space=pltpu.HBM),
+        params=pltpu.CompilerParams(vmem_limit_bytes=60 * 1024 * 1024),
     )
     before_x, after_x = exchange(up, down, GX)
+    sibling = lax.ppermute(own, "y", [(0, 1), (1, 0), (2, 3), (3, 2)])
     message = lax.all_to_all(message, GX + GZ, 0, 0, tiled=True)
-    up, down, bank, beyond = call(
-        y_messages,
-        (along_y, along_y, shape((128, 128), BF16), shape((16, 640), F32)),
-        slabs,
-        before_x,
-        after_x,
-        message,
-    )
-    before_y, after_y, far = (
-        lax.ppermute(part, GY, [(i, (i + by) % 4) for i in range(4)])
-        for part, by in ((up, 1), (down, 3), (bank, 2))
-    )
-    sums = call(
+    bank = call(bank_rows, shape((128, 128), BF16), message)
+    far = turn(bank, 2)
+    up, down, beyond = call(
+        y_messages, (along_y, along_y, shape((16, 640), F32)), slabs, before_x, after_x, message, bank
+    )
+    before_y, after_y = turn(up, 1), turn(down, 3)
+    keep, send = call(
         gradients,
-        shape((8, 8, 1408), F32),
+        (shape((8, 8, 768), F32), shape((8, 8, 768), F32)),
         slabs,
         before_x,
         after_x,
@@ -569,20 +593,23 @@
         bank,
         far,
         narrow_band,
+        pick,
+        sibling,
         scratch=(
             pltpu.VMEM((6, 640, 128), BF16),
             pltpu.VMEM((6, 48, 128), BF16),
             pltpu.VMEM((256, 512), F32),
             pltpu.VMEM((512, 128), F32),
+            pltpu.VMEM((448, 128), F32),
         ),
     )
-    sums = lax.all_to_all(sums, GX, 0, 0, tiled=True)
-    sums = call(second_stage, shape((4, 8, 768), F32), sums)
-    sums = lax.all_to_all(sums, GY, 0, 0, tiled=True)
-    sums = call(third_stage, shape((8, 8, 768), F32), sums, own)
-    sums = lax.all_to_all(sums, GZ, 0, 0, tiled=True)
+    sums = call(first_stage, shape((8, 8, 768), F32), keep, swap(send))
+    sums = lax.all_to_all(sums, ("zl", "zh"), 0, 0, tiled=True)
+    sums = call(second_stage, shape((16, 24, 128), F32), sums)
+    sums = lax.all_to_all(sums, ("x", "y"), 0, 0, tiled=True)
+    half = call(third_stage, shape((40, 128), F32), sums, own, sibling)
     one, rows = shape((1, 216), F32), shape((27, 128), F32)
-    new = call(update, (one, one, one, rows, rows, rows), sums, own, *narrow)
+    new = call(update, (one, one, one, rows, rows, rows), half, swap(half), own, *narrow)
     return tuple(w.reshape(-1) for w in new[3:] + new[:3])
 
 

time: 83.9 us -> 77.9 us (0.928)
  blocking collectives: 38.2 us -> 26.2 us
  starting transfers between devices: 24.6 us -> 31 us
  local copies, waits for them, and re-layouts: 2.5 us -> 0.03 us
  waiting for transfers between devices: 9.32 us -> 11 us
    all_to_all x3 -> x2, blocking collectives: 38.2 us -> 26.2 us  [the longest x1 14.1 us: local(): sums = lax.all_to_all(sums, ('x', 'y'), 0, 0, tiled=True)]
    ppermute x3 -> x6, starting transfers between devices: 9.6 us -> 15.9 us  [the longest x3 9.62 us: turn(): return lax.ppermute(value, GY, [(i, (i + by) % 4) for i in range(4)])]
    all_to_all x1, waiting for transfers between devices: 1.12 us -> 6.29 us  [local(): message = lax.all_to_all(message, GX + GZ, 0, 0, tiled=True)]
    ppermute x1, waiting for transfers between devices: 2.97 us -> 0.01 us  [exchange(): before = lax.ppermute(up, axes, pairs)]
    unnamed x16 -> x12, local copies, waits for them, and re-layouts: 2.5 us -> 0.03 us
    ppermute x1, waiting for transfers between devices: 2.2 us -> 0.01 us  [exchange(): after = lax.ppermute(down, axes, [(j, i) for i, j in pairs])]
    ppermute x3 -> x6, waiting for transfers between devices: 3.03 us -> 4.71 us  [the longest x2 1.91 us: swap(): return lax.ppermute(value, 'core', [(0, 1), (1, 0)])]
    pallas_call x7 -> x9, Pallas kernels: 8.08 us -> 8.66 us  [call(): pl.pallas_call(kernel, out_shape=out_shapes, in_specs=[space] * len(args)...]
  transfers between devices with their start and end apart: 6 -> 9, of which waited for: 5 -> 6; matrix products, arithmetic and copies ran while one was open for 0% -> 0% of each run, Pallas kernels for 1% -> 1%
where the time goes in v3:
time: 77.9 us; the launch traced here: 77.6 us
  starting transfers between devices  31 us (40%)
  blocking collectives  26.2 us (34%)
  waiting for transfers between devices  11 us (14%)
  Pallas kernels  8.66 us (11%)
    all_to_all x1, blocking collectives, local(): sums = lax.all_to_all(sums, ('x', 'y'), 0, 0, tiled=True)  14.1 us
    all_to_all x1, blocking collectives, local(): sums = lax.all_to_all(sums, ('zl', 'zh'), 0, 0, tiled=True)  12 us
    all_to_all x1, starting transfers between devices, local(): message = lax.all_to_all(message, GX + GZ, 0, 0, tiled=True)  10.5 us
    ppermute x3, starting transfers between devices, turn(): return lax.ppermute(value, GY, [(i, (i + by) % 4) for i in range(4)])  9.62 us
    pallas_call x9, Pallas kernels, call(): pl.pallas_call(kernel, out_shape=out_shapes, in_specs=[space] * len(args)...  8.66 us
    all_to_all x1, waiting for transfers between devices, local(): message = lax.all_to_all(message, GX + GZ, 0, 0, tiled=True)  6.29 us
    ppermute x2, starting transfers between devices, swap(): return lax.ppermute(value, 'core', [(0, 1), (1, 0)])  6.01 us
    ppermute x1, starting transfers between devices, exchange(): before = lax.ppermute(up, axes, pairs)  3.3 us
  transfers between devices with their start and end apart: 9, of which 6 were waited for; matrix products, arithmetic and copies ran while one was open for 0% of the time, Pallas kernels for 1%

profile of v3, /device:TPU:1, one launch (start us, length us, event | category | flops | bytes accessed | tf_op | source)
XLA Modules:
  0.0 77.6 jit_solution(15664387804618020789)
XLA Ops:
  0.6 3.0 %shard_map.127 = (bf16[4,544,128]{2,1,0:T(8,128)(2,1)}, bf16[544,128]{1,0:T(8,128)(2,1)}, bf16[544,128]{1,0:T(8,128)(2,1)}, bf16[64,24,128]{2,1,0:T(8,128)(2,1)}, f32[8,128]{1,0:T(8,128)}) custom-call(bf16[2048,128]{1,0:T(8,128)(2,1)} %bitcast.18, bf16[128,128]{1,0:T(8,128)(2,1)} %bitcast.19, f32[1,216]{1,0:T(1,128)} %bitcast.20, f32[1,216]{1,0:T(1,128)} %bitcast.21, ...), custom_call_target="tpu_custom_call" | custom-call | tf_op jit(solution)/shard_map/pallas_call | solution.py:33
  3.7 10.5 %all-to-all-start = ((bf16[64,24,128]{2,1,0:T(8,128)(2,1)}), bf16[64,24,128]{2,1,0:T(8,128)(2,1)S(1)}, u32[]{:S(2)}, u32[]{:S(2)}) async-start(bf16[64,24,128]{2,1,0:T(8,128)(2,1)} %get-tuple-element.27), calls=%async_computation | async-start | bytes 786432 | tf_op jit(solution)/shard_map/all_to_all | solution.py:577
  14.2 3.3 %collective-permute-start = (bf16[544,128]{1,0:T(8,128)(2,1)}, bf16[544,128]{1,0:T(8,128)(2,1)S(1)}, u32[]{:S(2)}, u32[]{:S(2)}) collective-permute-start(bf16[544,128]{1,0:T(8,128)(2,1)} %get-tuple-element.25), channel_id=1, source_target_pairs={{0,32},{32,64},{64,96},{96,128},{128,160},{160,192},{192,224},{1,3... | collective-permute-start | bytes 417800 | tf_op jit(solution)/shard_map/ppermute | solution.py:538
  17.5 1.3 %collective-permute-start.1 = (bf16[544,128]{1,0:T(8,128)(2,1)S(1)}, bf16[544,128]{1,0:T(8,128)(2,1)S(1)}, u32[]{:S(2)}, u32[]{:S(2)}) collective-permute-start(bf16[544,128]{1,0:T(8,128)(2,1)S(1)} %copy-done.5), channel_id=1, source_target_pairs={{32,0},{64,32},{96,64},{128,96},{160,128},{192,160},{224,192},{33,... | collective-permute-start | bytes 417800 | tf_op jit(solution)/shard_map/ppermute | solution.py:539
  18.8 6.3 %all-to-all-done.in_ref = bf16[64,24,128]{2,1,0:T(8,128)(2,1)S(1)} async-done(((bf16[64,24,128]{2,1,0:T(8,128)(2,1)}), bf16[64,24,128]{2,1,0:T(8,128)(2,1)S(1)}, u32[]{:S(2)}, u32[]{:S(2)}) %all-to-all-start) | async-done | bytes 393248 | tf_op jit(solution)/shard_map/all_to_all | solution.py:577
  25.1 0.0 collective-permute-done.1.r_ref
  25.2 0.0 copy-start.1
  25.2 0.2 shard_map.129
  25.4 3.0 %collective-permute-start.2 = (bf16[560,128]{1,0:T(8,128)(2,1)S(1)}, bf16[560,128]{1,0:T(8,128)(2,1)S(1)}, u32[]{:S(2)}, u32[]{:S(2)}) collective-permute-start(bf16[560,128]{1,0:T(8,128)(2,1)S(1)} %get-tuple-element.29), channel_id=1, source_target_pairs={{0,8},{8,16},{16,24},{24,0},{1,9},{9,17},{17,25},{25,1},{2,10},{10... | collective-permute-start | bytes 430088 | tf_op jit(solution)/shard_map/ppermute | solution.py:544
  28.4 2.2 %collective-permute-start.3 = (bf16[560,128]{1,0:T(8,128)(2,1)S(1)}, bf16[560,128]{1,0:T(8,128)(2,1)S(1)}, u32[]{:S(2)}, u32[]{:S(2)}) collective-permute-start(bf16[560,128]{1,0:T(8,128)(2,1)S(1)} %get-tuple-element.30), channel_id=1, source_target_pairs={{0,24},{8,0},{16,8},{24,16},{1,25},{9,1},{17,9},{25,17},{2,26},{10... | collective-permute-start | bytes 430088 | tf_op jit(solution)/shard_map/ppermute | solution.py:544
  30.6 4.4 %collective-permute-start.4 = (bf16[128,128]{1,0:T(8,128)(2,1)S(1)}, bf16[128,128]{1,0:T(8,128)(2,1)S(1)}, u32[]{:S(2)}, u32[]{:S(2)}) collective-permute-start(bf16[128,128]{1,0:T(8,128)(2,1)S(1)} %shard_map.128.bank_ref), channel_id=1, source_target_pairs={{0,16},{8,24},{16,0},{24,8},{1,17},{9,25},{17,1},{25,9},{2,18},{10... | collective-permute-start | bytes 98312 | tf_op jit(solution)/shard_map/ppermute | solution.py:544
  35.0 0.3 collective-permute-start.5
  35.3 0.9 %shard_map.130 = (bf16[256,512]{1,0:T(8,128)(2,1)S(1)}, bf16[512,128]{1,0:T(8,128)(2,1)S(1)}) custom-call(f32[27,128]{1,0:T(8,128)S(1)} %bitcast.14), custom_call_target="tpu_custom_call" | custom-call | tf_op jit(solution)/shard_map/pallas_call | solution.py:33
  36.2 1.6 %collective-permute-done.5.sib_ref = f32[8,128]{1,0:T(8,128)S(1)} collective-permute-done((f32[8,128]{1,0:T(8,128)S(1)}, f32[8,128]{1,0:T(8,128)S(1)}, u32[]{:S(2)}, u32[]{:S(2)}) %collective-permute-start.5) | collective-permute-done | bytes 4128 | tf_op jit(solution)/shard_map/ppermute | solution.py:576
  37.7 0.1 collective-permute-done.4.far_ref
  37.8 1.2 %collective-permute-done.3.yn_ref = bf16[560,128]{1,0:T(8,128)(2,1)S(1)} collective-permute-done((bf16[560,128]{1,0:T(8,128)(2,1)S(1)}, bf16[560,128]{1,0:T(8,128)(2,1)S(1)}, u32[]{:S(2)}, u32[]{:S(2)}) %collective-permute-start.3) | collective-permute-done | bytes 143392 | tf_op jit(solution)/shard_map/ppermute | solution.py:544
  39.0 3.6 %shard_map.131 = (f32[8,8,768]{2,1,0:T(8,128)S(1)}, f32[8,8,768]{2,1,0:T(8,128)S(1)}) custom-call(bf16[4,544,128]{2,1,0:T(8,128)(2,1)S(1)} %copy-done, bf16[544,128]{1,0:T(8,128)(2,1)S(1)} %collective-permute-done.l_ref, bf16[544,128]{1,0:T(8,128)(2,1)S(1)} %collective-permute-done.1.r_ref, f32[16,640]{1,0:T(8,128)S(1)} %get-tuple-element.28.beyond_ref, ...), custom_call_target="tpu_custom_call" | custom-call | tf_op jit(solution)/shard_map/pallas_call | solution.py:33
  42.6 2.3 %collective-permute-start.6 = (f32[8,8,768]{2,1,0:T(8,128)S(1)}, f32[8,8,768]{2,1,0:T(8,128)S(1)}, u32[]{:S(2)}, u32[]{:S(2)}) collective-permute-start(f32[8,8,768]{2,1,0:T(8,128)S(1)} %get-tuple-element.35), channel_id=1, source_target_pairs={{0,1},{1,0},{2,3},{3,2},{4,5},{5,4},{6,7},{7,6},{8,9},{9,8},{10,11... | collective-permute-start | bytes 589832 | tf_op jit(solution)/shard_map/ppermute | solution.py:548
  44.9 1.1 %collective-permute-done.6.b_ref = f32[8,8,768]{2,1,0:T(8,128)S(1)} collective-permute-done((f32[8,8,768]{2,1,0:T(8,128)S(1)}, f32[8,8,768]{2,1,0:T(8,128)S(1)}, u32[]{:S(2)}, u32[]{:S(2)}) %collective-permute-start.6) | collective-permute-done | bytes 196640 | tf_op jit(solution)/shard_map/ppermute | solution.py:548
  46.0 12.0 %all_to_all.15.in_ref = f32[8,8,768]{2,1,0:T(8,128)S(1)} all-to-all(f32[8,8,768]{2,1,0:T(8,128)S(1)} %shard_map.132), channel_id=1, replica_groups=mesh['zl'=2,'x'=4,'zh'=4,'y'=4,'core'=2] {'zl','zh'}, dimensions={0} | all-to-all | bytes 393216 | tf_op jit(solution)/shard_map/all_to_all | solution.py:607
  58.0 14.1 %all_to_all.16.in_ref = f32[16,24,128]{2,1,0:T(8,128)S(1)} all-to-all(f32[16,24,128]{2,1,0:T(8,128)S(1)} %shard_map.133), channel_id=1, replica_groups=mesh['zl'=2,'x'=4,'zh'=4,'y'=4,'core'=2] {'x','y'}, dimensions={0} | all-to-all | bytes 393216 | tf_op jit(solution)/shard_map/all_to_all | solution.py:609
  72.2 3.7 %collective-permute-start.7 = (f32[40,128]{1,0:T(8,128)S(1)}, f32[40,128]{1,0:T(8,128)S(1)}, u32[]{:S(2)}, u32[]{:S(2)}) collective-permute-start(f32[40,128]{1,0:T(8,128)S(1)} %shard_map.134.in_ref), channel_id=1, source_target_pairs={{0,1},{1,0},{2,3},{3,2},{4,5},{5,4},{6,7},{7,6},{8,9},{9,8},{10,11... | collective-permute-start | bytes 61448 | tf_op jit(solution)/shard_map/ppermute | solution.py:548
  75.9 0.8 %collective-permute-done.7.other_ref = f32[40,128]{1,0:T(8,128)S(1)} collective-permute-done((f32[40,128]{1,0:T(8,128)S(1)}, f32[40,128]{1,0:T(8,128)S(1)}, u32[]{:S(2)}, u32[]{:S(2)}) %collective-permute-start.7) | collective-permute-done | bytes 20512 | tf_op jit(solution)/shard_map/ppermute | solution.py:548
  76.7 0.9 %shard_map.135 = (f32[1,216]{1,0:T(1,128)}, f32[1,216]{1,0:T(1,128)}, f32[1,216]{1,0:T(1,128)}, f32[27,128]{1,0:T(8,128)}, f32[27,128]{1,0:T(8,128)}, /*index=5*/f32[27,128]{1,0:T(8,128)}) custom-call(f32[40,128]{1,0:T(8,128)S(1)} %shard_map.134.in_ref, f32[40,128]{1,0:T(8,128)S(1)} %collective-permute-done.7.other_ref, f32[8,128]{1,0:T(8,128)S(1)} %copy-done.2, ...), custom_call_target="tpu_custom_call" | custom-call | tf_op jit(solution)/shard_map/pallas_call | solution.py:33
  (17 shorter events, 0.1 us)
Async XLA Ops:
  3.7 13.8 %copy-start.5 = (bf16[544,128]{1,0:T(8,128)(2,1)S(1)}, bf16[544,128]{1,0:T(8,128)(2,1)}, u32[]{:S(2)}) copy-start(bf16[544,128]{1,0:T(8,128)(2,1)} %get-tuple-element.26) | copy-start | bytes 417796
  3.7 21.5 %copy-start = (bf16[4,544,128]{2,1,0:T(8,128)(2,1)S(1)}, bf16[4,544,128]{2,1,0:T(8,128)(2,1)}, u32[]{:S(2)}) copy-start(bf16[4,544,128]{2,1,0:T(8,128)(2,1)} %get-tuple-element.24.slab_ref) | copy-start | bytes 1671172
  3.7 21.4 %all-to-all-start = ((bf16[64,24,128]{2,1,0:T(8,128)(2,1)}), bf16[64,24,128]{2,1,0:T(8,128)(2,1)S(1)}, u32[]{:S(2)}, u32[]{:S(2)}) async-start(bf16[64,24,128]{2,1,0:T(8,128)(2,1)} %get-tuple-element.27), calls=%async_computation | async-start | bytes 786432 | tf_op jit(solution)/shard_map/all_to_all | solution.py:577
  14.2 10.9 %collective-permute-start = (bf16[544,128]{1,0:T(8,128)(2,1)}, bf16[544,128]{1,0:T(8,128)(2,1)S(1)}, u32[]{:S(2)}, u32[]{:S(2)}) collective-permute-start(bf16[544,128]{1,0:T(8,128)(2,1)} %get-tuple-element.25), channel_id=1, source_target_pairs={{0,32},{32,64},{64,96},{96,128},{128,160},{160,192},{192,224},{1,3... | collective-permute-start | bytes 417800 | tf_op jit(solution)/shard_map/ppermute | solution.py:538
  17.5 7.6 %collective-permute-start.1 = (bf16[544,128]{1,0:T(8,128)(2,1)S(1)}, bf16[544,128]{1,0:T(8,128)(2,1)S(1)}, u32[]{:S(2)}, u32[]{:S(2)}) collective-permute-start(bf16[544,128]{1,0:T(8,128)(2,1)S(1)} %copy-done.5), channel_id=1, source_target_pairs={{32,0},{64,32},{96,64},{128,96},{160,128},{192,160},{224,192},{33,... | collective-permute-start | bytes 417800 | tf_op jit(solution)/shard_map/ppermute | solution.py:539
  25.2 10.1 %copy-start.1 = (f32[3456]{0:T(1024)S(1)}, f32[3456]{0:T(1024)}, u32[]{:S(2)}) copy-start(f32[3456]{0:T(1024)} %param.10) | copy-start | bytes 41476
  25.3 9.6 %copy-start.2 = (f32[8,128]{1,0:T(8,128)S(1)}, f32[8,128]{1,0:T(8,128)}, u32[]{:S(2)}) copy-start(f32[8,128]{1,0:T(8,128)} %get-tuple-element.33.own_ref) | copy-start | bytes 12292
  25.4 12.4 %collective-permute-start.2 = (bf16[560,128]{1,0:T(8,128)(2,1)S(1)}, bf16[560,128]{1,0:T(8,128)(2,1)S(1)}, u32[]{:S(2)}, u32[]{:S(2)}) collective-permute-start(bf16[560,128]{1,0:T(8,128)(2,1)S(1)} %get-tuple-element.29), channel_id=1, source_target_pairs={{0,8},{8,16},{16,24},{24,0},{1,9},{9,17},{17,25},{25,1},{2,10},{10... | collective-permute-start | bytes 430088 | tf_op jit(solution)/shard_map/ppermute | solution.py:544
  28.4 10.6 %collective-permute-start.3 = (bf16[560,128]{1,0:T(8,128)(2,1)S(1)}, bf16[560,128]{1,0:T(8,128)(2,1)S(1)}, u32[]{:S(2)}, u32[]{:S(2)}) collective-permute-start(bf16[560,128]{1,0:T(8,128)(2,1)S(1)} %get-tuple-element.30), channel_id=1, source_target_pairs={{0,24},{8,0},{16,8},{24,16},{1,25},{9,1},{17,9},{25,17},{2,26},{10... | collective-permute-start | bytes 430088 | tf_op jit(solution)/shard_map/ppermute | solution.py:544
  30.6 7.2 %collective-permute-start.4 = (bf16[128,128]{1,0:T(8,128)(2,1)S(1)}, bf16[128,128]{1,0:T(8,128)(2,1)S(1)}, u32[]{:S(2)}, u32[]{:S(2)}) collective-permute-start(bf16[128,128]{1,0:T(8,128)(2,1)S(1)} %shard_map.128.bank_ref), channel_id=1, source_target_pairs={{0,16},{8,24},{16,0},{24,8},{1,17},{9,25},{17,1},{25,9},{2,18},{10... | collective-permute-start | bytes 98312 | tf_op jit(solution)/shard_map/ppermute | solution.py:544
  35.0 2.8 %collective-permute-start.5 = (f32[8,128]{1,0:T(8,128)S(1)}, f32[8,128]{1,0:T(8,128)S(1)}, u32[]{:S(2)}, u32[]{:S(2)}) collective-permute-start(f32[8,128]{1,0:T(8,128)S(1)} %copy-done.2), channel_id=1, source_target_pairs={{0,2},{2,0},{4,6},{6,4},{1,3},{3,1},{5,7},{7,5},{8,10},{10,8},{12,... | collective-permute-start | bytes 12296 | tf_op jit(solution)/shard_map/ppermute | solution.py:576
  42.6 3.4 %collective-permute-start.6 = (f32[8,8,768]{2,1,0:T(8,128)S(1)}, f32[8,8,768]{2,1,0:T(8,128)S(1)}, u32[]{:S(2)}, u32[]{:S(2)}) collective-permute-start(f32[8,8,768]{2,1,0:T(8,128)S(1)} %get-tuple-element.35), channel_id=1, source_target_pairs={{0,1},{1,0},{2,3},{3,2},{4,5},{5,4},{6,7},{7,6},{8,9},{9,8},{10,11... | collective-permute-start | bytes 589832 | tf_op jit(solution)/shard_map/ppermute | solution.py:548
  72.1 4.6 %copy-start.3 = (f32[3456]{0:T(1024)S(1)}, f32[3456]{0:T(1024)}, u32[]{:S(2)}) copy-start(f32[3456]{0:T(1024)} %param.11) | copy-start | bytes 41476
  72.1 4.6 %copy-start.4 = (f32[3456]{0:T(1024)S(1)}, f32[3456]{0:T(1024)}, u32[]{:S(2)}) copy-start(f32[3456]{0:T(1024)} %param.12) | copy-start | bytes 41476
  72.2 4.6 %collective-permute-start.7 = (f32[40,128]{1,0:T(8,128)S(1)}, f32[40,128]{1,0:T(8,128)S(1)}, u32[]{:S(2)}, u32[]{:S(2)}) collective-permute-start(f32[40,128]{1,0:T(8,128)S(1)} %shard_map.134.in_ref), channel_id=1, source_target_pairs={{0,1},{1,0},{2,3},{3,2},{4,5},{5,4},{6,7},{7,6},{8,9},{9,8},{10,11... | collective-permute-start | bytes 61448 | tf_op jit(solution)/shard_map/ppermute | solution.py:548

commit v4 on v3

--- a/solution.py
+++ b/solution.py
@@ -136,7 +136,7 @@
     out_ref[...] = jnp.concatenate(rows, axis=0).astype(BF16)
 
 
-def y_messages(slab_ref, l_ref, r_ref, in_ref, bank_ref, up_ref, dn_ref, beyond_ref):
+def y_messages(slab_ref, l_ref, r_ref, in_ref, pb_ref, nb_ref, up_ref, dn_ref, beyond_ref):
     slabs = [l_ref] + [slab_ref.at[x] for x in range(4)] + [r_ref]
     first, last = [], []
     for xe, slab in enumerate(slabs):
@@ -175,8 +175,8 @@
         rows_dn.append(within(parts[0], 0, 64) + within(roll(parts[4], 64), 64, 68))
     up_ref[384:432, :] = jnp.concatenate(last + fill + rows_up + four, axis=0).astype(BF16)
     dn_ref[384:432, :] = jnp.concatenate(first + fill + rows_dn + four, axis=0).astype(BF16)
-    up_ref[432:560, :] = bank_ref[...]
-    dn_ref[432:560, :] = bank_ref[...]
+    up_ref[432:496, :] = pb_ref[0:64, :]
+    dn_ref[432:496, :] = nb_ref[64:128, :]
 
 
 def assemble(slab_ref, l_ref, r_ref, beyond_ref, yp_ref, yn_ref, e_ref, ve_ref):
@@ -186,9 +186,10 @@
     before = jnp.where(some, yp_ref[384:432, :].astype(F32), 0.0)
     after = jnp.where(more, yn_ref[384:432, :].astype(F32), 0.0)
     for xe, slab in enumerate(slabs):
-        e_ref[xe, 0:64, :] = jnp.where(some, yp_ref[xe * 64 : xe * 64 + 64, :].astype(F32), 0.0).astype(BF16)
-        e_ref[xe, 64:576, :] = slab[0:512, :]
-        e_ref[xe, 576:640, :] = jnp.where(more, yn_ref[xe * 64 : xe * 64 + 64, :].astype(F32), 0.0).astype(BF16)
+        at = slice(128 * xe, 128 * xe + 128)
+        e_ref[0:64, at] = jnp.where(some, yp_ref[xe * 64 : xe * 64 + 64, :].astype(F32), 0.0).astype(BF16)
+        e_ref[64:576, at] = slab[0:512, :]
+        e_ref[576:640, at] = jnp.where(more, yn_ref[xe * 64 : xe * 64 + 64, :].astype(F32), 0.0).astype(BF16)
         vol = slab[512:544, :].astype(F32)
         ve_ref[xe] = jnp.concatenate(
             [before[xe * 4 : xe * 4 + 4], vol, after[xe * 4 : xe * 4 + 4], jnp.zeros((8, 128), F32)], axis=0
@@ -225,13 +226,17 @@
     return jnp.concatenate(rows[:32], axis=0)
 
 
-def turned(yp_ref, yn_ref, own_ref, far_ref, rows_ref):
+def turned(yp_ref, yn_ref, own_ref, pb_ref, nb_ref, rows_ref):
     me = lax.axis_index("zh")
-    for by, ref, first in ((0, own_ref, 0), (3, yp_ref, 432), (1, yn_ref, 432), (2, far_ref, 0)):
+    for by in range(4):
         zh = (me + by) % 4
         for across in range(8):
             at = pl.multiple_of(64 * across + 16 * zh, 16)
-            rows_ref[pl.ds(at, 16), :] = ref[first + 16 * across : first + 16 * across + 16, :].astype(F32)
+            if by == 2:
+                ref, row = (yp_ref if across < 4 else yn_ref), 432 + 16 * (across % 4)
+            else:
+                ref, row = (own_ref, nb_ref, None, pb_ref)[by], 16 * across
+            rows_ref[pl.ds(at, 16), :] = ref[row : row + 16, :].astype(F32)
     parts = []
     for q in range(4):
         parts.append(rows_ref[pl.ds(2 * q, 64, stride=8), :].T)
@@ -266,7 +271,7 @@
 
 
 def gradients(
-    slab_ref, l_ref, r_ref, beyond_ref, yp_ref, yn_ref, bank_ref, far_ref, wb_ref, pick_ref, sib_ref,
+    slab_ref, l_ref, r_ref, beyond_ref, yp_ref, yn_ref, bank_ref, pb_ref, nb_ref, wb_ref, pick_ref, sib_ref,
     keep_ref, send_ref,
     e_ref, ve_ref, ga_ref, rows_ref, wide_ref,
 ):
@@ -313,7 +318,7 @@
             ).astype(BF16)
         )
     none = jnp.zeros((32, 64), BF16)
-    weights = turned(yp_ref, yn_ref, bank_ref, far_ref, rows_ref)
+    weights = turned(yp_ref, yn_ref, bank_ref, pb_ref, nb_ref, rows_ref)
     blocks = []
     for c in range(3):
         for yl in range(2):
@@ -332,16 +337,13 @@
     from_right = dot_nt(bank[128:192], halos[1])
     for k in range(4):
         for xp in range(2):
-            cells = jnp.concatenate(
-                [
-                    jnp.concatenate(
-                        [e_ref[2 * xp + j + a, 128 * k : 128 * k + 256, :] for j in range(2)], axis=1
-                    )
-                    for a in range(3)
-                ],
-                axis=0,
+            v = sum(
+                dot(
+                    bank[:, 256 * a : 256 * a + 256],
+                    e_ref[128 * k : 128 * k + 256, 128 * (2 * xp + a) : 128 * (2 * xp + a) + 256],
+                )
+                for a in range(3)
             )
-            v = dot(bank, cells)
             for j in range(2):
                 x = 2 * xp + j
                 at = slice(128 * j, 128 * j + 128)
@@ -378,17 +380,16 @@
             at = slice(64 * k + 32 * yl, 64 * k + 32 * yl + 32)
             parts += [before[at], act[at], after[at], empty]
         rows.append(jnp.concatenate(parts, axis=0))
-    acts = jnp.concatenate(rows, axis=1)
-    cots = jnp.concatenate(
+    wide = jnp.concatenate(
         [
-            jnp.concatenate(
-                [e_ref[x + a, 128 * k : 128 * k + 256, :] for k in range(4) for x in range(4)], axis=1
+            sum(
+                dot_nt(e_ref[128 * k : 128 * k + 256, 128 * a : 128 * a + 512], rows[k])
+                for k in range(4)
             )
             for a in range(3)
         ],
         axis=0,
     )
-    wide = dot_nt(cots, acts)
     row = lax.broadcasted_iota(jnp.int32, (16, 512), 0)
     lanes = lax.broadcasted_iota(jnp.int32, (16, 512), 1)
     pick = ((row < 4) & (lanes == row * 128)) | ((row >= 4) & (row < 8) & (lanes == (row - 4) * 128 + 127))
@@ -552,7 +553,7 @@
     wide = [w.reshape(1, 216) for w in (w2_master, w2_first, w2_second)]
     narrow = [w.reshape(27, 128) for w in (w1_master, w1_first, w1_second)]
     narrow_band, pick = call(narrow_rows, (shape((256, 512), BF16), shape((512, 128), BF16)), narrow[0])
-    face, along_y = shape((544, 128), BF16), shape((560, 128), BF16)
+    face, along_y = shape((544, 128), BF16), shape((496, 128), BF16)
     slabs, up, down, message, own = call(
         pack,
         (shape((4, 544, 128), BF16), face, face, shape((64, 24, 128), BF16), shape((8, 128), F32)),
@@ -576,9 +577,9 @@
     sibling = lax.ppermute(own, "y", [(0, 1), (1, 0), (2, 3), (3, 2)])
     message = lax.all_to_all(message, GX + GZ, 0, 0, tiled=True)
     bank = call(bank_rows, shape((128, 128), BF16), message)
-    far = turn(bank, 2)
+    near_banks = turn(bank, 1), turn(bank, 3)
     up, down, beyond = call(
-        y_messages, (along_y, along_y, shape((16, 640), F32)), slabs, before_x, after_x, message, bank
+        y_messages, (along_y, along_y, shape((16, 640), F32)), slabs, before_x, after_x, message, *near_banks
     )
     before_y, after_y = turn(up, 1), turn(down, 3)
     keep, send = call(
@@ -591,12 +592,12 @@
         before_y,
         after_y,
         bank,
-        far,
+        *near_banks,
         narrow_band,
         pick,
         sibling,
         scratch=(
-            pltpu.VMEM((6, 640, 128), BF16),
+            pltpu.VMEM((640, 768), BF16),
             pltpu.VMEM((6, 48, 128), BF16),
             pltpu.VMEM((256, 512), F32),
             pltpu.VMEM((512, 128), F32),

time: 77.9 us -> 76.6 us (0.983)
  waiting for transfers between devices: 11 us -> 15.8 us
  blocking collectives: 26.2 us -> 21.6 us
  starting transfers between devices: 31 us -> 29.8 us
    ppermute x3 -> x4, waiting for transfers between devices: 1.23 us -> 6.34 us  [turn(): return lax.ppermute(value, GY, [(i, (i + by) % 4) for i in range(4)])]
    all_to_all x1, blocking collectives: 14.1 us -> 9.65 us  [local(): sums = lax.all_to_all(sums, ('x', 'y'), 0, 0, tiled=True)]
    ppermute x3 -> x4, starting transfers between devices: 9.62 us -> 8.9 us  [turn(): return lax.ppermute(value, GY, [(i, (i + by) % 4) for i in range(4)])]
  transfers between devices with their start and end apart: 9 -> 10, of which waited for: 6 -> 8; matrix products, arithmetic and copies ran while one was open for 0% -> 0% of each run, Pallas kernels for 1% -> 1%
where the time goes in v4:
time: 76.6 us; the launch traced here: 76.3 us
  starting transfers between devices  29.8 us (39%)
  blocking collectives  21.6 us (28%)
  waiting for transfers between devices  15.8 us (21%)
  Pallas kernels  8.4 us (11%)
    all_to_all x1, blocking collectives, local(): sums = lax.all_to_all(sums, ('zl', 'zh'), 0, 0, tiled=True)  11.9 us
    all_to_all x1, starting transfers between devices, local(): message = lax.all_to_all(message, GX + GZ, 0, 0, tiled=True)  10.5 us
    all_to_all x1, blocking collectives, local(): sums = lax.all_to_all(sums, ('x', 'y'), 0, 0, tiled=True)  9.65 us
    ppermute x4, starting transfers between devices, turn(): return lax.ppermute(value, GY, [(i, (i + by) % 4) for i in range(4)])  8.9 us
    pallas_call x9, Pallas kernels, call(): pl.pallas_call(kernel, out_shape=out_shapes, in_specs=[space] * len(args)...  8.4 us
    ppermute x4, waiting for transfers between devices, turn(): return lax.ppermute(value, GY, [(i, (i + by) % 4) for i in range(4)])  6.34 us
    all_to_all x1, waiting for transfers between devices, local(): message = lax.all_to_all(message, GX + GZ, 0, 0, tiled=True)  6.29 us
    ppermute x2, starting transfers between devices, swap(): return lax.ppermute(value, 'core', [(0, 1), (1, 0)])  5.48 us
  transfers between devices with their start and end apart: 10, of which 8 were waited for; matrix products, arithmetic and copies ran while one was open for 0% of the time, Pallas kernels for 1%

profile of v4, /device:TPU:1, one launch (start us, length us, event | category | flops | bytes accessed | tf_op | source)
XLA Modules:
  0.0 76.3 jit_solution(681679588988947919)
XLA Ops:
  0.6 3.1 %shard_map.127 = (bf16[4,544,128]{2,1,0:T(8,128)(2,1)}, bf16[544,128]{1,0:T(8,128)(2,1)}, bf16[544,128]{1,0:T(8,128)(2,1)}, bf16[64,24,128]{2,1,0:T(8,128)(2,1)}, f32[8,128]{1,0:T(8,128)}) custom-call(bf16[2048,128]{1,0:T(8,128)(2,1)} %bitcast.18, bf16[128,128]{1,0:T(8,128)(2,1)} %bitcast.19, f32[1,216]{1,0:T(1,128)} %bitcast.20, f32[1,216]{1,0:T(1,128)} %bitcast.21, ...), custom_call_target="tpu_custom_call" | custom-call | tf_op jit(solution)/shard_map/pallas_call | solution.py:33
  3.7 10.5 %all-to-all-start = ((bf16[64,24,128]{2,1,0:T(8,128)(2,1)}), bf16[64,24,128]{2,1,0:T(8,128)(2,1)S(1)}, u32[]{:S(2)}, u32[]{:S(2)}) async-start(bf16[64,24,128]{2,1,0:T(8,128)(2,1)} %get-tuple-element.27), calls=%async_computation | async-start | bytes 786432 | tf_op jit(solution)/shard_map/all_to_all | solution.py:578
  14.2 3.3 %collective-permute-start = (bf16[544,128]{1,0:T(8,128)(2,1)}, bf16[544,128]{1,0:T(8,128)(2,1)S(1)}, u32[]{:S(2)}, u32[]{:S(2)}) collective-permute-start(bf16[544,128]{1,0:T(8,128)(2,1)} %get-tuple-element.25), channel_id=1, source_target_pairs={{0,32},{32,64},{64,96},{96,128},{128,160},{160,192},{192,224},{1,3... | collective-permute-start | bytes 417800 | tf_op jit(solution)/shard_map/ppermute | solution.py:539
  17.5 1.3 %collective-permute-start.1 = (bf16[544,128]{1,0:T(8,128)(2,1)S(1)}, bf16[544,128]{1,0:T(8,128)(2,1)S(1)}, u32[]{:S(2)}, u32[]{:S(2)}) collective-permute-start(bf16[544,128]{1,0:T(8,128)(2,1)S(1)} %copy-done.5), channel_id=1, source_target_pairs={{32,0},{64,32},{96,64},{128,96},{160,128},{192,160},{224,192},{33,... | collective-permute-start | bytes 417800 | tf_op jit(solution)/shard_map/ppermute | solution.py:540
  18.8 6.3 %all-to-all-done.in_ref = bf16[64,24,128]{2,1,0:T(8,128)(2,1)S(1)} async-done(((bf16[64,24,128]{2,1,0:T(8,128)(2,1)}), bf16[64,24,128]{2,1,0:T(8,128)(2,1)S(1)}, u32[]{:S(2)}, u32[]{:S(2)}) %all-to-all-start) | async-done | bytes 393248 | tf_op jit(solution)/shard_map/all_to_all | solution.py:578
  25.1 3.1 %collective-permute-start.2 = (bf16[128,128]{1,0:T(8,128)(2,1)S(1)}, bf16[128,128]{1,0:T(8,128)(2,1)S(1)}, u32[]{:S(2)}, u32[]{:S(2)}) collective-permute-start(bf16[128,128]{1,0:T(8,128)(2,1)S(1)} %shard_map.128.bank_ref), channel_id=1, source_target_pairs={{0,8},{8,16},{16,24},{24,0},{1,9},{9,17},{17,25},{25,1},{2,10},{10... | collective-permute-start | bytes 98312 | tf_op jit(solution)/shard_map/ppermute | solution.py:545
  28.2 2.2 %collective-permute-start.3 = (bf16[128,128]{1,0:T(8,128)(2,1)S(1)}, bf16[128,128]{1,0:T(8,128)(2,1)S(1)}, u32[]{:S(2)}, u32[]{:S(2)}) collective-permute-start(bf16[128,128]{1,0:T(8,128)(2,1)S(1)} %shard_map.128.bank_ref), channel_id=1, source_target_pairs={{0,24},{8,0},{16,8},{24,16},{1,25},{9,1},{17,9},{25,17},{2,26},{10... | collective-permute-start | bytes 98312 | tf_op jit(solution)/shard_map/ppermute | solution.py:545
  30.4 1.2 %collective-permute-done.2.pb_ref = bf16[128,128]{1,0:T(8,128)(2,1)S(1)} collective-permute-done((bf16[128,128]{1,0:T(8,128)(2,1)S(1)}, bf16[128,128]{1,0:T(8,128)(2,1)S(1)}, u32[]{:S(2)}, u32[]{:S(2)}) %collective-permute-start.2) | collective-permute-done | bytes 32800 | tf_op jit(solution)/shard_map/ppermute | solution.py:545
  31.7 1.2 %collective-permute-done.3.nb_ref = bf16[128,128]{1,0:T(8,128)(2,1)S(1)} collective-permute-done((bf16[128,128]{1,0:T(8,128)(2,1)S(1)}, bf16[128,128]{1,0:T(8,128)(2,1)S(1)}, u32[]{:S(2)}, u32[]{:S(2)}) %collective-permute-start.3) | collective-permute-done | bytes 32800 | tf_op jit(solution)/shard_map/ppermute | solution.py:545
  32.8 0.2 shard_map.129
  33.0 3.6 %collective-permute-start.4 = (bf16[496,128]{1,0:T(8,128)(2,1)S(1)}, bf16[496,128]{1,0:T(8,128)(2,1)S(1)}, u32[]{:S(2)}, u32[]{:S(2)}) collective-permute-start(bf16[496,128]{1,0:T(8,128)(2,1)S(1)} %get-tuple-element.29), channel_id=1, source_target_pairs={{0,8},{8,16},{16,24},{24,0},{1,9},{9,17},{17,25},{25,1},{2,10},{10... | collective-permute-start | bytes 380936 | tf_op jit(solution)/shard_map/ppermute | solution.py:545
  36.6 0.3 collective-permute-start.6
  36.9 0.9 %shard_map.130 = (bf16[256,512]{1,0:T(8,128)(2,1)S(1)}, bf16[512,128]{1,0:T(8,128)(2,1)S(1)}) custom-call(f32[27,128]{1,0:T(8,128)S(1)} %bitcast.14), custom_call_target="tpu_custom_call" | custom-call | tf_op jit(solution)/shard_map/pallas_call | solution.py:33
  37.8 1.3 %collective-permute-done.6.sib_ref = f32[8,128]{1,0:T(8,128)S(1)} collective-permute-done((f32[8,128]{1,0:T(8,128)S(1)}, f32[8,128]{1,0:T(8,128)S(1)}, u32[]{:S(2)}, u32[]{:S(2)}) %collective-permute-start.6) | collective-permute-done | bytes 4128 | tf_op jit(solution)/shard_map/ppermute | solution.py:577
  39.1 0.5 collective-permute-done.4.yp_ref
  39.6 3.5 %collective-permute-done.5.yn_ref = bf16[496,128]{1,0:T(8,128)(2,1)S(1)} collective-permute-done((bf16[496,128]{1,0:T(8,128)(2,1)S(1)}, bf16[496,128]{1,0:T(8,128)(2,1)S(1)}, u32[]{:S(2)}, u32[]{:S(2)}) %collective-permute-start.5) | collective-permute-done | bytes 127008 | tf_op jit(solution)/shard_map/ppermute | solution.py:545
  43.0 3.3 %shard_map.131 = (f32[8,8,768]{2,1,0:T(8,128)S(1)}, f32[8,8,768]{2,1,0:T(8,128)S(1)}) custom-call(bf16[4,544,128]{2,1,0:T(8,128)(2,1)S(1)} %copy-done, bf16[544,128]{1,0:T(8,128)(2,1)S(1)} %collective-permute-done.l_ref, bf16[544,128]{1,0:T(8,128)(2,1)S(1)} %collective-permute-done.1.r_ref, f32[16,640]{1,0:T(8,128)S(1)} %get-tuple-element.28.beyond_ref, ...), custom_call_target="tpu_custom_call" | custom-call | tf_op jit(solution)/shard_map/pallas_call | solution.py:33
  46.4 1.8 %collective-permute-start.7 = (f32[8,8,768]{2,1,0:T(8,128)S(1)}, f32[8,8,768]{2,1,0:T(8,128)S(1)}, u32[]{:S(2)}, u32[]{:S(2)}) collective-permute-start(f32[8,8,768]{2,1,0:T(8,128)S(1)} %get-tuple-element.35), channel_id=1, source_target_pairs={{0,1},{1,0},{2,3},{3,2},{4,5},{5,4},{6,7},{7,6},{8,9},{9,8},{10,11... | collective-permute-start | bytes 589832 | tf_op jit(solution)/shard_map/ppermute | solution.py:549
  48.1 1.1 %collective-permute-done.7.b_ref = f32[8,8,768]{2,1,0:T(8,128)S(1)} collective-permute-done((f32[8,8,768]{2,1,0:T(8,128)S(1)}, f32[8,8,768]{2,1,0:T(8,128)S(1)}, u32[]{:S(2)}, u32[]{:S(2)}) %collective-permute-start.7) | collective-permute-done | bytes 196640 | tf_op jit(solution)/shard_map/ppermute | solution.py:549
  49.2 11.9 %all_to_all.15.in_ref = f32[8,8,768]{2,1,0:T(8,128)S(1)} all-to-all(f32[8,8,768]{2,1,0:T(8,128)S(1)} %shard_map.132), channel_id=1, replica_groups=mesh['zl'=2,'x'=4,'zh'=4,'y'=4,'core'=2] {'zl','zh'}, dimensions={0} | all-to-all | bytes 393216 | tf_op jit(solution)/shard_map/all_to_all | solution.py:608
  61.2 9.6 %all_to_all.16.in_ref = f32[16,24,128]{2,1,0:T(8,128)S(1)} all-to-all(f32[16,24,128]{2,1,0:T(8,128)S(1)} %shard_map.133), channel_id=1, replica_groups=mesh['zl'=2,'x'=4,'zh'=4,'y'=4,'core'=2] {'x','y'}, dimensions={0} | all-to-all | bytes 393216 | tf_op jit(solution)/shard_map/all_to_all | solution.py:610
  70.9 3.7 %collective-permute-start.8 = (f32[40,128]{1,0:T(8,128)S(1)}, f32[40,128]{1,0:T(8,128)S(1)}, u32[]{:S(2)}, u32[]{:S(2)}) collective-permute-start(f32[40,128]{1,0:T(8,128)S(1)} %shard_map.134.in_ref), channel_id=1, source_target_pairs={{0,1},{1,0},{2,3},{3,2},{4,5},{5,4},{6,7},{7,6},{8,9},{9,8},{10,11... | collective-permute-start | bytes 61448 | tf_op jit(solution)/shard_map/ppermute | solution.py:549
  74.6 0.8 %collective-permute-done.8.other_ref = f32[40,128]{1,0:T(8,128)S(1)} collective-permute-done((f32[40,128]{1,0:T(8,128)S(1)}, f32[40,128]{1,0:T(8,128)S(1)}, u32[]{:S(2)}, u32[]{:S(2)}) %collective-permute-start.8) | collective-permute-done | bytes 20512 | tf_op jit(solution)/shard_map/ppermute | solution.py:549
  75.4 0.9 %shard_map.135 = (f32[1,216]{1,0:T(1,128)}, f32[1,216]{1,0:T(1,128)}, f32[1,216]{1,0:T(1,128)}, f32[27,128]{1,0:T(8,128)}, f32[27,128]{1,0:T(8,128)}, /*index=5*/f32[27,128]{1,0:T(8,128)}) custom-call(f32[40,128]{1,0:T(8,128)S(1)} %shard_map.134.in_ref, f32[40,128]{1,0:T(8,128)S(1)} %collective-permute-done.8.other_ref, f32[8,128]{1,0:T(8,128)S(1)} %copy-done.2, ...), custom_call_target="tpu_custom_call" | custom-call | tf_op jit(solution)/shard_map/pallas_call | solution.py:33
  (19 shorter events, 0.1 us)
Async XLA Ops:
  3.7 13.8 %copy-start.5 = (bf16[544,128]{1,0:T(8,128)(2,1)S(1)}, bf16[544,128]{1,0:T(8,128)(2,1)}, u32[]{:S(2)}) copy-start(bf16[544,128]{1,0:T(8,128)(2,1)} %get-tuple-element.26) | copy-start | bytes 417796
  3.7 29.1 %copy-start = (bf16[4,544,128]{2,1,0:T(8,128)(2,1)S(1)}, bf16[4,544,128]{2,1,0:T(8,128)(2,1)}, u32[]{:S(2)}) copy-start(bf16[4,544,128]{2,1,0:T(8,128)(2,1)} %get-tuple-element.24.slab_ref) | copy-start | bytes 1671172
  3.7 21.4 %all-to-all-start = ((bf16[64,24,128]{2,1,0:T(8,128)(2,1)}), bf16[64,24,128]{2,1,0:T(8,128)(2,1)S(1)}, u32[]{:S(2)}, u32[]{:S(2)}) async-start(bf16[64,24,128]{2,1,0:T(8,128)(2,1)} %get-tuple-element.27), calls=%async_computation | async-start | bytes 786432 | tf_op jit(solution)/shard_map/all_to_all | solution.py:578
  14.2 16.2 %collective-permute-start = (bf16[544,128]{1,0:T(8,128)(2,1)}, bf16[544,128]{1,0:T(8,128)(2,1)S(1)}, u32[]{:S(2)}, u32[]{:S(2)}) collective-permute-start(bf16[544,128]{1,0:T(8,128)(2,1)} %get-tuple-element.25), channel_id=1, source_target_pairs={{0,32},{32,64},{64,96},{96,128},{128,160},{160,192},{192,224},{1,3... | collective-permute-start | bytes 417800 | tf_op jit(solution)/shard_map/ppermute | solution.py:539
  17.5 12.9 %collective-permute-start.1 = (bf16[544,128]{1,0:T(8,128)(2,1)S(1)}, bf16[544,128]{1,0:T(8,128)(2,1)S(1)}, u32[]{:S(2)}, u32[]{:S(2)}) collective-permute-start(bf16[544,128]{1,0:T(8,128)(2,1)S(1)} %copy-done.5), channel_id=1, source_target_pairs={{32,0},{64,32},{96,64},{128,96},{160,128},{192,160},{224,192},{33,... | collective-permute-start | bytes 417800 | tf_op jit(solution)/shard_map/ppermute | solution.py:540
  25.1 6.5 %collective-permute-start.2 = (bf16[128,128]{1,0:T(8,128)(2,1)S(1)}, bf16[128,128]{1,0:T(8,128)(2,1)S(1)}, u32[]{:S(2)}, u32[]{:S(2)}) collective-permute-start(bf16[128,128]{1,0:T(8,128)(2,1)S(1)} %shard_map.128.bank_ref), channel_id=1, source_target_pairs={{0,8},{8,16},{16,24},{24,0},{1,9},{9,17},{17,25},{25,1},{2,10},{10... | collective-permute-start | bytes 98312 | tf_op jit(solution)/shard_map/ppermute | solution.py:545
  28.2 4.6 %collective-permute-start.3 = (bf16[128,128]{1,0:T(8,128)(2,1)S(1)}, bf16[128,128]{1,0:T(8,128)(2,1)S(1)}, u32[]{:S(2)}, u32[]{:S(2)}) collective-permute-start(bf16[128,128]{1,0:T(8,128)(2,1)S(1)} %shard_map.128.bank_ref), channel_id=1, source_target_pairs={{0,24},{8,0},{16,8},{24,16},{1,25},{9,1},{17,9},{25,17},{2,26},{10... | collective-permute-start | bytes 98312 | tf_op jit(solution)/shard_map/ppermute | solution.py:545
  32.8 4.1 %copy-start.1 = (f32[3456]{0:T(1024)S(1)}, f32[3456]{0:T(1024)}, u32[]{:S(2)}) copy-start(f32[3456]{0:T(1024)} %param.10) | copy-start | bytes 41476
  33.0 3.6 %copy-start.2 = (f32[8,128]{1,0:T(8,128)S(1)}, f32[8,128]{1,0:T(8,128)}, u32[]{:S(2)}) copy-start(f32[8,128]{1,0:T(8,128)} %get-tuple-element.33.own_ref) | copy-start | bytes 12292
  33.0 6.6 %collective-permute-start.4 = (bf16[496,128]{1,0:T(8,128)(2,1)S(1)}, bf16[496,128]{1,0:T(8,128)(2,1)S(1)}, u32[]{:S(2)}, u32[]{:S(2)}) collective-permute-start(bf16[496,128]{1,0:T(8,128)(2,1)S(1)} %get-tuple-element.29), channel_id=1, source_target_pairs={{0,8},{8,16},{16,24},{24,0},{1,9},{9,17},{17,25},{25,1},{2,10},{10... | collective-permute-start | bytes 380936 | tf_op jit(solution)/shard_map/ppermute | solution.py:545
  36.6 6.4 %collective-permute-start.5 = (bf16[496,128]{1,0:T(8,128)(2,1)S(1)}, bf16[496,128]{1,0:T(8,128)(2,1)S(1)}, u32[]{:S(2)}, u32[]{:S(2)}) collective-permute-start(bf16[496,128]{1,0:T(8,128)(2,1)S(1)} %get-tuple-element.30), channel_id=1, source_target_pairs={{0,24},{8,0},{16,8},{24,16},{1,25},{9,1},{17,9},{25,17},{2,26},{10... | collective-permute-start | bytes 380936 | tf_op jit(solution)/shard_map/ppermute | solution.py:545
  36.6 2.5 %collective-permute-start.6 = (f32[8,128]{1,0:T(8,128)S(1)}, f32[8,128]{1,0:T(8,128)S(1)}, u32[]{:S(2)}, u32[]{:S(2)}) collective-permute-start(f32[8,128]{1,0:T(8,128)S(1)} %copy-done.2), channel_id=1, source_target_pairs={{0,2},{2,0},{4,6},{6,4},{1,3},{3,1},{5,7},{7,5},{8,10},{10,8},{12,... | collective-permute-start | bytes 12296 | tf_op jit(solution)/shard_map/ppermute | solution.py:577
  46.4 2.8 %collective-permute-start.7 = (f32[8,8,768]{2,1,0:T(8,128)S(1)}, f32[8,8,768]{2,1,0:T(8,128)S(1)}, u32[]{:S(2)}, u32[]{:S(2)}) collective-permute-start(f32[8,8,768]{2,1,0:T(8,128)S(1)} %get-tuple-element.35), channel_id=1, source_target_pairs={{0,1},{1,0},{2,3},{3,2},{4,5},{5,4},{6,7},{7,6},{8,9},{9,8},{10,11... | collective-permute-start | bytes 589832 | tf_op jit(solution)/shard_map/ppermute | solution.py:549
  70.8 4.6 %copy-start.3 = (f32[3456]{0:T(1024)S(1)}, f32[3456]{0:T(1024)}, u32[]{:S(2)}) copy-start(f32[3456]{0:T(1024)} %param.11) | copy-start | bytes 41476
  70.8 4.6 %copy-start.4 = (f32[3456]{0:T(1024)S(1)}, f32[3456]{0:T(1024)}, u32[]{:S(2)}) copy-start(f32[3456]{0:T(1024)} %param.12) | copy-start | bytes 41476
  70.9 4.6 %collective-permute-start.8 = (f32[40,128]{1,0:T(8,128)S(1)}, f32[40,128]{1,0:T(8,128)S(1)}, u32[]{:S(2)}, u32[]{:S(2)}) collective-permute-start(f32[40,128]{1,0:T(8,128)S(1)} %shard_map.134.in_ref), channel_id=1, source_target_pairs={{0,1},{1,0},{2,3},{3,2},{4,5},{5,4},{6,7},{7,6},{8,9},{9,8},{10,11... | collective-permute-start | bytes 61448 | tf_op jit(solution)/shard_map/ppermute | solution.py:549

commit v5 on v4

--- a/solution.py
+++ b/solution.py
@@ -13,6 +13,7 @@
 GX = ("zl", "x")
 GY = ("zh",)
 GZ = ("y", "core")
+PAST = ((3, 0), (2, 2))
 VMEM = pl.BlockSpec(memory_space=pltpu.VMEM)
 PARAMS = pltpu.CompilerParams(vmem_limit_bytes=32 * 1024 * 1024)
 
@@ -87,7 +88,7 @@
 
 
 def pack(
-    cot_hbm, vol_hbm, w2_hbm, f2_hbm, s2_hbm, slab_ref, up_ref, dn_ref, out_ref, own_ref,
+    cot_hbm, vol_hbm, w2_hbm, f2_hbm, s2_hbm, slab_ref, ahead_ref, out_ref, own_ref,
     cot_ref, vol_ref, w2_ref, f2_ref, s2_ref, cot32, vol32, sems,
 ):
     copies = [
@@ -108,8 +109,7 @@
         slab_ref[x, 512:544, :] = jnp.concatenate(
             [vol32[pl.ds(8 * x + y, 4, stride=32), :] for y in range(8)], axis=0
         ).astype(BF16)
-    up_ref[...] = slab_ref[3]
-    dn_ref[...] = slab_ref[0]
+    ahead_ref[...] = slab_ref[0:2]
     row = lax.broadcasted_iota(jnp.int32, (16, 512), 0)
     lane = lax.broadcasted_iota(jnp.int32, (16, 512), 1)
     pick = ((row < 4) & (lane == row * 128)) | ((row >= 4) & (row < 8) & (lane == row * 128 - 385))
@@ -122,22 +122,23 @@
     for side in range(2):
         at = slice(4 * side, 4 * side + 4)
         tail = edge[at, 512:640]
-        tail = [sum(roll(tail[x : x + 1], 32 * x) for x in range(4))] + own[0:2] + [jnp.zeros((5, 128), F32)]
+        tail = [sum(roll(tail[x : x + 1], 32 * x) for x in range(4))] + own[0:2] + [jnp.zeros((1, 128), F32)]
         ends.append(jnp.concatenate([edge[at, 128 * j : 128 * j + 128] for j in range(4)] + tail, axis=0))
     me = along_gz()
     for p in range(8):
         message = jnp.where(me < p, ends[1], ends[0]).astype(BF16)
         for x in range(8):
-            out_ref[8 * x + p] = message
+            for j in range(5):
+                out_ref[8 * x + p, j] = message[4 * j : 4 * j + 4]
 
 
 def bank_rows(in_ref, out_ref):
-    rows = [in_ref[p, 16:24, :].astype(F32)[1:3] for p in range(64)]
+    rows = [in_ref[p, 4].astype(F32)[1:3] for p in range(64)]
     out_ref[...] = jnp.concatenate(rows, axis=0).astype(BF16)
 
 
-def y_messages(slab_ref, l_ref, r_ref, in_ref, pb_ref, nb_ref, up_ref, dn_ref, beyond_ref):
-    slabs = [l_ref] + [slab_ref.at[x] for x in range(4)] + [r_ref]
+def y_messages(slab_ref, next_ref, in_ref, nb_ref, pb_ref, up_ref, dn_ref, beyond_ref):
+    slabs = [slab_ref.at[x] for x in range(4)] + [next_ref.at[x] for x in range(2)]
     first, last = [], []
     for xe, slab in enumerate(slabs):
         up_ref[xe * 64 : xe * 64 + 64, :] = slab[448:512, :]
@@ -154,18 +155,10 @@
         inside = (other >= 0) & (other <= 7)
         other = jnp.clip(other, 0, 7)
         mid = jnp.where(inside, in_ref[8 * across + other].astype(F32), 0.0)
-        before = in_ref[8 * jnp.maximum(across - 1, 0) + other].astype(F32)
-        before = jnp.where(inside & (across > 0), before, 0.0)
-        after = in_ref[8 * jnp.minimum(across + 1, 7) + other].astype(F32)
-        after = jnp.where(inside & (across < 7), after, 0.0)
-        parts = [
-            jnp.concatenate(
-                [before[4 * j + 3 : 4 * j + 4], mid[4 * j : 4 * j + 4], after[4 * j : 4 * j + 1]], axis=0
-            )
-            for j in range(4)
-        ]
-        tail = [before[16:17]] + [mid[16:17]] * 4 + [after[16:17]]
-        tail = [roll(row, -32 * x) for row, x in zip(tail, (3, 0, 1, 2, 3, 0), strict=True)]
+        after = jnp.where(inside, in_ref[8 * ((across + 1) % 8) + other].astype(F32), 0.0)
+        parts = [jnp.concatenate([mid[j], after[j, 0:2]], axis=0) for j in range(4)]
+        tail = [mid[4, 0:1]] * 4 + [after[4, 0:1]] * 2
+        tail = [roll(row, -32 * x) for row, x in zip(tail, (0, 1, 2, 3, 0, 1), strict=True)]
         parts.append(within(jnp.concatenate(tail, axis=0), 0, 32))
         for j in range(5):
             beyond_ref[8 * side : 8 * side + 8, 128 * j : 128 * j + 128] = jnp.concatenate(
@@ -179,17 +172,26 @@
     dn_ref[432:496, :] = nb_ref[64:128, :]
 
 
-def assemble(slab_ref, l_ref, r_ref, beyond_ref, yp_ref, yn_ref, e_ref, ve_ref):
-    slabs = [l_ref] + [slab_ref.at[x] for x in range(4)] + [r_ref]
+def assemble(slab_ref, next_ref, beyond_ref, yp_ref, yn_ref, e_ref, ve_ref, keep):
+    slabs = [slab_ref.at[x] for x in range(4)] + [next_ref.at[x] for x in range(2)]
     along_y = lax.axis_index("zh")
     some, more = along_y > 0, along_y < 3
     before = jnp.where(some, yp_ref[384:432, :].astype(F32), 0.0)
     after = jnp.where(more, yn_ref[384:432, :].astype(F32), 0.0)
     for xe, slab in enumerate(slabs):
-        at = slice(128 * xe, 128 * xe + 128)
-        e_ref[0:64, at] = jnp.where(some, yp_ref[xe * 64 : xe * 64 + 64, :].astype(F32), 0.0).astype(BF16)
-        e_ref[64:576, at] = slab[0:512, :]
-        e_ref[576:640, at] = jnp.where(more, yn_ref[xe * 64 : xe * 64 + 64, :].astype(F32), 0.0).astype(BF16)
+        rows = jnp.concatenate(
+            [
+                jnp.where(some, yp_ref[xe * 64 : xe * 64 + 64, :].astype(F32), 0.0).astype(BF16),
+                slab[0:512, :],
+                jnp.where(more, yn_ref[xe * 64 : xe * 64 + 64, :].astype(F32), 0.0).astype(BF16),
+            ],
+            axis=0,
+        )
+        for a in range(3):
+            x = xe - a
+            if 0 <= x < 4:
+                value = (rows.astype(F32) * keep).astype(BF16) if (x, a) in PAST else rows
+                e_ref[:, 512 * a + 128 * x : 512 * a + 128 * x + 128] = value
         vol = slab[512:544, :].astype(F32)
         ve_ref[xe] = jnp.concatenate(
             [before[xe * 4 : xe * 4 + 4], vol, after[xe * 4 : xe * 4 + 4], jnp.zeros((8, 128), F32)], axis=0
@@ -271,11 +273,13 @@
 
 
 def gradients(
-    slab_ref, l_ref, r_ref, beyond_ref, yp_ref, yn_ref, bank_ref, pb_ref, nb_ref, wb_ref, pick_ref, sib_ref,
+    slab_ref, next_ref, beyond_ref, yp_ref, yn_ref, bank_ref, pb_ref, nb_ref, wb_ref, pick_ref, sib_ref,
     keep_ref, send_ref,
     e_ref, ve_ref, ga_ref, rows_ref, wide_ref,
 ):
-    ends = assemble(slab_ref, l_ref, r_ref, beyond_ref, yp_ref, yn_ref, e_ref, ve_ref)
+    final = (lax.axis_index("zl") == 1) & (lax.axis_index("x") == 3)
+    keep = jnp.where(final, 0.0, 1.0)
+    ends = assemble(slab_ref, next_ref, beyond_ref, yp_ref, yn_ref, e_ref, ve_ref, keep)
     lane = lax.broadcasted_iota(jnp.int32, (1, 128), 1)
     low, high = lane == 0, lane == 127
     eye = (
@@ -296,7 +300,15 @@
     rest = jnp.zeros((80, 128), BF16)
     patches = jnp.concatenate(
         [
-            jnp.concatenate([shifted[x + a][c] for a in range(3) for c in range(3)] + [rest], axis=0)
+            jnp.concatenate(
+                [
+                    (shifted[x + a][c].astype(F32) * keep).astype(BF16) if (x, a) in PAST else shifted[x + a][c]
+                    for a in range(3)
+                    for c in range(3)
+                ]
+                + [rest],
+                axis=0,
+            )
             for x in range(4)
         ],
         axis=1,
@@ -308,10 +320,17 @@
     halos = []
     for end in ends:
         m = end[:, 0:640].astype(F32)
+        by_a = []
+        for a in range(3):
+            rows = m[a : a + 4]
+            if a != 1:
+                row = lax.broadcasted_iota(jnp.int32, (4, 1), 0)
+                rows = rows * jnp.where(row == (3 if a == 0 else 2), keep, 1.0)
+            by_a.append(rows)
         halos.append(
             jnp.concatenate(
                 [
-                    jnp.concatenate([m[a : a + 4, 128 * k : 128 * k + 256] for a in range(3)], axis=1)
+                    jnp.concatenate([rows[:, 128 * k : 128 * k + 256] for rows in by_a], axis=1)
                     for k in range(4)
                 ],
                 axis=0,
@@ -340,7 +359,7 @@
             v = sum(
                 dot(
                     bank[:, 256 * a : 256 * a + 256],
-                    e_ref[128 * k : 128 * k + 256, 128 * (2 * xp + a) : 128 * (2 * xp + a) + 256],
+                    e_ref[128 * k : 128 * k + 256, 512 * a + 256 * xp : 512 * a + 256 * xp + 256],
                 )
                 for a in range(3)
             )
@@ -383,7 +402,7 @@
     wide = jnp.concatenate(
         [
             sum(
-                dot_nt(e_ref[128 * k : 128 * k + 256, 128 * a : 128 * a + 512], rows[k])
+                dot_nt(e_ref[128 * k : 128 * k + 256, 512 * a : 512 * a + 512], rows[k])
                 for k in range(4)
             )
             for a in range(3)
@@ -417,18 +436,12 @@
     for j in range(7):
         wide_ref[64 * j : 64 * j + 64, :] = wide[:, 128 * j : 128 * j + 128]
     core = lax.axis_index("core")
-    gap = jnp.zeros((4, 128), F32)
     for p in range(8):
         zl, zh = p // 4, p % 4
         halves = []
         for yh in range(2):
-            rows = [
-                wide_ref[pl.ds(64 * j + 32 * zl + 2 * zh + yh, 4, stride=8), :] for j in range(7)
-            ]
-            under = [rows[6]] + [flat[16 * yh + 4 * j : 16 * yh + 4 * j + 4] for j in range(4)] + [gap]
-            halves.append(
-                jnp.concatenate([jnp.concatenate(rows[0:6], axis=1), jnp.concatenate(under, axis=1)], axis=0)
-            )
+            rows = [wide_ref[pl.ds(64 * j + 32 * zl + 2 * zh + yh, 4, stride=8), :] for j in range(7)]
+            halves.append(jnp.concatenate(rows + [flat[14 * yh : 14 * yh + 14]], axis=0))
         keep_ref[p] = jnp.where(core == 0, halves[0], halves[1])
         send_ref[p] = jnp.where(core == 0, halves[1], halves[0])
 
@@ -441,11 +454,9 @@
     total = in_ref[0]
     for p in range(1, 8):
         total = total + in_ref[p]
-    narrow = [total[4:8, 128 * j : 128 * j + 128] for j in range(1, 5)]
     for x in range(4):
-        block = [total[x : x + 1, 128 * j : 128 * j + 128] for j in range(6)]
-        block += [total[4 + x : 5 + x, 0:128], jnp.zeros((1, 128), F32)]
-        rows = jnp.concatenate(block + narrow, axis=0)
+        block = [total[4 * j + x : 4 * j + x + 1] for j in range(7)]
+        rows = jnp.concatenate(block + [total[28:42]], axis=0)
         for y in range(4):
             out_ref[4 * x + y] = rows
 
@@ -454,7 +465,8 @@
     total = in_ref[0]
     for p in range(1, 16):
         total = total + in_ref[p]
-    out_ref[0:24, :] = total
+    gap = [jnp.zeros((1, 128), F32)]
+    out_ref[0:24, :] = jnp.concatenate([total[0:7]] + gap + [total[7:21]] + gap + gap, axis=0)
     even = lax.axis_index("y") % 2 == 0
     own, sib = own_ref[...], sib_ref[...]
     out_ref[24:32, :] = jnp.where(even, own, sib)
@@ -524,7 +536,7 @@
         (s2_ref, second_new),
     ):
         ref[...] = jnp.concatenate([value[0:1], value[1:2, 0:88]], axis=1)
-    grad = jnp.concatenate([low[8:24], high[8:24]], axis=0)[0:27]
+    grad = jnp.concatenate([low[8:22], high[8:22]], axis=0)[0:27]
     master = m_ref[...]
     first_new, second_new, direction = moments(master, f_ref[...], s_ref[...], grad)
     ratio = jnp.sqrt(run_sums(master * master)) / (jnp.sqrt(run_sums(direction * direction)) + 1e-06)
@@ -533,14 +545,6 @@
     s1_ref[...] = second_new
 
 
-def exchange(up, down, axes):
-    size = lax.axis_size(axes)
-    pairs = [(i, i + 1) for i in range(size - 1)]
-    before = lax.ppermute(up, axes, pairs)
-    after = lax.ppermute(down, axes, [(j, i) for i, j in pairs])
-    return before, after
-
-
 def turn(value, by):
     return lax.ppermute(value, GY, [(i, (i + by) % 4) for i in range(4)])
 
@@ -553,10 +557,10 @@
     wide = [w.reshape(1, 216) for w in (w2_master, w2_first, w2_second)]
     narrow = [w.reshape(27, 128) for w in (w1_master, w1_first, w1_second)]
     narrow_band, pick = call(narrow_rows, (shape((256, 512), BF16), shape((512, 128), BF16)), narrow[0])
-    face, along_y = shape((544, 128), BF16), shape((496, 128), BF16)
-    slabs, up, down, message, own = call(
+    along_y = shape((496, 128), BF16)
+    slabs, ahead, message, own = call(
         pack,
-        (shape((4, 544, 128), BF16), face, face, shape((64, 24, 128), BF16), shape((8, 128), F32)),
+        (shape((4, 544, 128), BF16), shape((2, 544, 128), BF16), shape((64, 5, 4, 128), BF16), shape((8, 128), F32)),
         cotangent.reshape(2048, 128),
         volume.reshape(128, 128),
         *wide,
@@ -573,21 +577,20 @@
         space=pl.BlockSpec(memory_space=pltpu.HBM),
         params=pltpu.CompilerParams(vmem_limit_bytes=60 * 1024 * 1024),
     )
-    before_x, after_x = exchange(up, down, GX)
+    next_x = lax.ppermute(ahead, GX, [(i, (i + 7) % 8) for i in range(8)])
     sibling = lax.ppermute(own, "y", [(0, 1), (1, 0), (2, 3), (3, 2)])
     message = lax.all_to_all(message, GX + GZ, 0, 0, tiled=True)
     bank = call(bank_rows, shape((128, 128), BF16), message)
     near_banks = turn(bank, 1), turn(bank, 3)
     up, down, beyond = call(
-        y_messages, (along_y, along_y, shape((16, 640), F32)), slabs, before_x, after_x, message, *near_banks
+        y_messages, (along_y, along_y, shape((16, 640), F32)), slabs, next_x, message, *near_banks[::-1]
     )
     before_y, after_y = turn(up, 1), turn(down, 3)
     keep, send = call(
         gradients,
-        (shape((8, 8, 768), F32), shape((8, 8, 768), F32)),
+        (shape((8, 42, 128), F32), shape((8, 42, 128), F32)),
         slabs,
-        before_x,
-        after_x,
+        next_x,
         beyond,
         before_y,
         after_y,
@@ -597,16 +600,16 @@
         pick,
         sibling,
         scratch=(
-            pltpu.VMEM((640, 768), BF16),
+            pltpu.VMEM((640, 1536), BF16),
             pltpu.VMEM((6, 48, 128), BF16),
             pltpu.VMEM((256, 512), F32),
             pltpu.VMEM((512, 128), F32),
             pltpu.VMEM((448, 128), F32),
         ),
     )
-    sums = call(first_stage, shape((8, 8, 768), F32), keep, swap(send))
+    sums = call(first_stage, shape((8, 42, 128), F32), keep, swap(send))
     sums = lax.all_to_all(sums, ("zl", "zh"), 0, 0, tiled=True)
-    sums = call(second_stage, shape((16, 24, 128), F32), sums)
+    sums = call(second_stage, shape((16, 21, 128), F32), sums)
     sums = lax.all_to_all(sums, ("x", "y"), 0, 0, tiled=True)
     half = call(third_stage, shape((40, 128), F32), sums, own, sibling)
     one, rows = shape((1, 216), F32), shape((27, 128), F32)

time: 76.6 us -> 76 us (level)
  starting transfers between devices: 29.8 us -> 28.8 us
  waiting for transfers between devices: 15.8 us -> 16.6 us
    ppermute x2 -> x1, starting transfers between devices: 4.59 us -> 3.84 us  [local(): next_x = lax.ppermute(ahead, GX, [(i, (i + 7) % 8) for i in range(8)])]
  transfers between devices with their start and end apart: 10 -> 9, of which waited for: 8 -> 8; matrix products, arithmetic and copies ran while one was open for 0% -> 0% of each run, Pallas kernels for 1% -> 1%
where the time goes in v5:
time: 76 us; the launch traced here: 75.8 us
  starting transfers between devices  28.8 us (38%)
  blocking collectives  21.2 us (28%)
  waiting for transfers between devices  16.6 us (22%)
  Pallas kernels  8.43 us (11%)
    all_to_all x1, blocking collectives, local(): sums = lax.all_to_all(sums, ('zl', 'zh'), 0, 0, tiled=True)  11.3 us
    all_to_all x1, starting transfers between devices, local(): message = lax.all_to_all(message, GX + GZ, 0, 0, tiled=True)  10.5 us
    all_to_all x1, blocking collectives, local(): sums = lax.all_to_all(sums, ('x', 'y'), 0, 0, tiled=True)  9.89 us
    ppermute x4, starting transfers between devices, turn(): return lax.ppermute(value, GY, [(i, (i + by) % 4) for i in range(4)])  8.9 us
    pallas_call x9, Pallas kernels, call(): pl.pallas_call(kernel, out_shape=out_shapes, in_specs=[space] * len(args)...  8.43 us
    ppermute x4, waiting for transfers between devices, turn(): return lax.ppermute(value, GY, [(i, (i + by) % 4) for i in range(4)])  6.89 us
    all_to_all x1, waiting for transfers between devices, local(): message = lax.all_to_all(message, GX + GZ, 0, 0, tiled=True)  6.51 us
    ppermute x2, starting transfers between devices, swap(): return lax.ppermute(value, 'core', [(0, 1), (1, 0)])  5.32 us
  transfers between devices with their start and end apart: 9, of which 8 were waited for; matrix products, arithmetic and copies ran while one was open for 0% of the time, Pallas kernels for 1%

profile of v5, /device:TPU:1, one launch (start us, length us, event | category | flops | bytes accessed | tf_op | source)
XLA Modules:
  0.0 75.8 jit_solution(650681313375431113)
XLA Ops:
  0.6 3.0 %shard_map.127 = (bf16[4,544,128]{2,1,0:T(8,128)(2,1)}, bf16[2,544,128]{2,1,0:T(8,128)(2,1)}, bf16[64,5,4,128]{3,2,1,0:T(4,128)(2,1)}, f32[8,128]{1,0:T(8,128)}) custom-call(bf16[2048,128]{1,0:T(8,128)(2,1)} %bitcast.18, bf16[128,128]{1,0:T(8,128)(2,1)} %bitcast.19, f32[1,216]{1,0:T(1,128)} %bitcast.20, f32[1,216]{1,0:T(1,128)} %bitcast.21, f32[1,216]{1,0:T(1,128)} %bitcast.22), custom_call_target="tpu_custom_call" | custom-call | tf_op jit(solution)/shard_map/pallas_call | solution.py:34
  3.7 10.5 %all-to-all-start = ((bf16[64,5,4,128]{3,2,1,0:T(4,128)(2,1)}), bf16[64,5,4,128]{3,2,1,0:T(4,128)(2,1)S(1)}, u32[]{:S(2)}, u32[]{:S(2)}) async-start(bf16[64,5,4,128]{3,2,1,0:T(4,128)(2,1)} %get-tuple-element.25), calls=%async_computation | async-start | bytes 655360 | tf_op jit(solution)/shard_map/all_to_all | solution.py:582
  14.1 3.8 %collective-permute-start = (bf16[2,544,128]{2,1,0:T(8,128)(2,1)}, bf16[2,544,128]{2,1,0:T(8,128)(2,1)S(1)}, u32[]{:S(2)}, u32[]{:S(2)}) collective-permute-start(bf16[2,544,128]{2,1,0:T(8,128)(2,1)} %get-tuple-element.24), channel_id=1, source_target_pairs={{0,224},{32,0},{64,32},{96,64},{128,96},{160,128},{192,160},{224,1... | collective-permute-start | bytes 835592 | tf_op jit(solution)/shard_map/ppermute | solution.py:580
  18.0 6.5 %all-to-all-done.in_ref = bf16[64,5,4,128]{3,2,1,0:T(4,128)(2,1)S(1)} async-done(((bf16[64,5,4,128]{3,2,1,0:T(4,128)(2,1)}), bf16[64,5,4,128]{3,2,1,0:T(4,128)(2,1)S(1)}, u32[]{:S(2)}, u32[]{:S(2)}) %all-to-all-start) | async-done | bytes 327712 | tf_op jit(solution)/shard_map/all_to_all | solution.py:582
  24.5 3.1 %collective-permute-start.2 = (bf16[128,128]{1,0:T(8,128)(2,1)S(1)}, bf16[128,128]{1,0:T(8,128)(2,1)S(1)}, u32[]{:S(2)}, u32[]{:S(2)}) collective-permute-start(bf16[128,128]{1,0:T(8,128)(2,1)S(1)} %shard_map.128.bank_ref), channel_id=1, source_target_pairs={{0,8},{8,16},{16,24},{24,0},{1,9},{9,17},{17,25},{25,1},{2,10},{10... | collective-permute-start | bytes 98312 | tf_op jit(solution)/shard_map/ppermute | solution.py:549
  27.6 2.2 %collective-permute-start.1 = (bf16[128,128]{1,0:T(8,128)(2,1)S(1)}, bf16[128,128]{1,0:T(8,128)(2,1)S(1)}, u32[]{:S(2)}, u32[]{:S(2)}) collective-permute-start(bf16[128,128]{1,0:T(8,128)(2,1)S(1)} %shard_map.128.bank_ref), channel_id=1, source_target_pairs={{0,24},{8,0},{16,8},{24,16},{1,25},{9,1},{17,9},{25,17},{2,26},{10... | collective-permute-start | bytes 98312 | tf_op jit(solution)/shard_map/ppermute | solution.py:549
  29.8 1.2 %collective-permute-done.2.pb_ref = bf16[128,128]{1,0:T(8,128)(2,1)S(1)} collective-permute-done((bf16[128,128]{1,0:T(8,128)(2,1)S(1)}, bf16[128,128]{1,0:T(8,128)(2,1)S(1)}, u32[]{:S(2)}, u32[]{:S(2)}) %collective-permute-start.2) | collective-permute-done | bytes 32800 | tf_op jit(solution)/shard_map/ppermute | solution.py:549
  31.0 1.5 %collective-permute-done.1.nb_ref = bf16[128,128]{1,0:T(8,128)(2,1)S(1)} collective-permute-done((bf16[128,128]{1,0:T(8,128)(2,1)S(1)}, bf16[128,128]{1,0:T(8,128)(2,1)S(1)}, u32[]{:S(2)}, u32[]{:S(2)}) %collective-permute-start.1) | collective-permute-done | bytes 32800 | tf_op jit(solution)/shard_map/ppermute | solution.py:549
  32.6 0.2 shard_map.129
  32.7 3.6 %collective-permute-start.3 = (bf16[496,128]{1,0:T(8,128)(2,1)S(1)}, bf16[496,128]{1,0:T(8,128)(2,1)S(1)}, u32[]{:S(2)}, u32[]{:S(2)}) collective-permute-start(bf16[496,128]{1,0:T(8,128)(2,1)S(1)} %get-tuple-element.27), channel_id=1, source_target_pairs={{0,8},{8,16},{16,24},{24,0},{1,9},{9,17},{17,25},{25,1},{2,10},{10... | collective-permute-start | bytes 380936 | tf_op jit(solution)/shard_map/ppermute | solution.py:549
  36.3 0.0 collective-permute-start.4
  36.4 0.3 collective-permute-start.5
  36.7 0.9 %shard_map.130 = (bf16[256,512]{1,0:T(8,128)(2,1)S(1)}, bf16[512,128]{1,0:T(8,128)(2,1)S(1)}) custom-call(f32[27,128]{1,0:T(8,128)S(1)} %bitcast.14), custom_call_target="tpu_custom_call" | custom-call | tf_op jit(solution)/shard_map/pallas_call | solution.py:34
  37.5 1.3 %collective-permute-done.5.sib_ref = f32[8,128]{1,0:T(8,128)S(1)} collective-permute-done((f32[8,128]{1,0:T(8,128)S(1)}, f32[8,128]{1,0:T(8,128)S(1)}, u32[]{:S(2)}, u32[]{:S(2)}) %collective-permute-start.5) | collective-permute-done | bytes 4128 | tf_op jit(solution)/shard_map/ppermute | solution.py:581
  38.8 2.8 %collective-permute-done.3.yp_ref = bf16[496,128]{1,0:T(8,128)(2,1)S(1)} collective-permute-done((bf16[496,128]{1,0:T(8,128)(2,1)S(1)}, bf16[496,128]{1,0:T(8,128)(2,1)S(1)}, u32[]{:S(2)}, u32[]{:S(2)}) %collective-permute-start.3) | collective-permute-done | bytes 127008 | tf_op jit(solution)/shard_map/ppermute | solution.py:549
  41.7 1.3 %collective-permute-done.4.yn_ref = bf16[496,128]{1,0:T(8,128)(2,1)S(1)} collective-permute-done((bf16[496,128]{1,0:T(8,128)(2,1)S(1)}, bf16[496,128]{1,0:T(8,128)(2,1)S(1)}, u32[]{:S(2)}, u32[]{:S(2)}) %collective-permute-start.4) | collective-permute-done | bytes 127008 | tf_op jit(solution)/shard_map/ppermute | solution.py:549
  43.0 3.4 %shard_map.131 = (f32[8,42,128]{2,1,0:T(8,128)S(1)}, f32[8,42,128]{2,1,0:T(8,128)S(1)}) custom-call(bf16[4,544,128]{2,1,0:T(8,128)(2,1)S(1)} %copy-done, bf16[2,544,128]{2,1,0:T(8,128)(2,1)S(1)} %collective-permute-done.next_ref, f32[16,640]{1,0:T(8,128)S(1)} %get-tuple-element.26.beyond_ref, bf16[496,128]{1,0:T(8,128)(2,1)S(1)} %collective-permute-done.3.yp_ref, ...), custom_call_target="tpu_custom_call" | custom-call | tf_op jit(solution)/shard_map/pallas_call | solution.py:34
  46.4 1.6 %collective-permute-start.6 = (f32[8,42,128]{2,1,0:T(8,128)S(1)}, f32[8,42,128]{2,1,0:T(8,128)S(1)}, u32[]{:S(2)}, u32[]{:S(2)}) collective-permute-start(f32[8,42,128]{2,1,0:T(8,128)S(1)} %get-tuple-element.33), channel_id=1, source_target_pairs={{0,1},{1,0},{2,3},{3,2},{4,5},{5,4},{6,7},{7,6},{8,9},{9,8},{10,11... | collective-permute-start | bytes 516104 | tf_op jit(solution)/shard_map/ppermute | solution.py:553
  48.0 1.1 %collective-permute-done.6.b_ref = f32[8,42,128]{2,1,0:T(8,128)S(1)} collective-permute-done((f32[8,42,128]{2,1,0:T(8,128)S(1)}, f32[8,42,128]{2,1,0:T(8,128)S(1)}, u32[]{:S(2)}, u32[]{:S(2)}) %collective-permute-start.6) | collective-permute-done | bytes 172064 | tf_op jit(solution)/shard_map/ppermute | solution.py:553
  49.1 11.3 %all_to_all.15.in_ref = f32[8,42,128]{2,1,0:T(8,128)S(1)} all-to-all(f32[8,42,128]{2,1,0:T(8,128)S(1)} %shard_map.132), channel_id=1, replica_groups=mesh['zl'=2,'x'=4,'zh'=4,'y'=4,'core'=2] {'zl','zh'}, dimensions={0} | all-to-all | bytes 344064 | tf_op jit(solution)/shard_map/all_to_all | solution.py:611
  60.4 9.9 %all_to_all.16.in_ref = f32[16,21,128]{2,1,0:T(8,128)S(1)} all-to-all(f32[16,21,128]{2,1,0:T(8,128)S(1)} %shard_map.133), channel_id=1, replica_groups=mesh['zl'=2,'x'=4,'zh'=4,'y'=4,'core'=2] {'x','y'}, dimensions={0} | all-to-all | bytes 344064 | tf_op jit(solution)/shard_map/all_to_all | solution.py:613
  70.3 3.7 %collective-permute-start.7 = (f32[40,128]{1,0:T(8,128)S(1)}, f32[40,128]{1,0:T(8,128)S(1)}, u32[]{:S(2)}, u32[]{:S(2)}) collective-permute-start(f32[40,128]{1,0:T(8,128)S(1)} %shard_map.134.in_ref), channel_id=1, source_target_pairs={{0,1},{1,0},{2,3},{3,2},{4,5},{5,4},{6,7},{7,6},{8,9},{9,8},{10,11... | collective-permute-start | bytes 61448 | tf_op jit(solution)/shard_map/ppermute | solution.py:553
  74.1 0.8 %collective-permute-done.7.other_ref = f32[40,128]{1,0:T(8,128)S(1)} collective-permute-done((f32[40,128]{1,0:T(8,128)S(1)}, f32[40,128]{1,0:T(8,128)S(1)}, u32[]{:S(2)}, u32[]{:S(2)}) %collective-permute-start.7) | collective-permute-done | bytes 20512 | tf_op jit(solution)/shard_map/ppermute | solution.py:553
  74.9 0.9 %shard_map.135 = (f32[1,216]{1,0:T(1,128)}, f32[1,216]{1,0:T(1,128)}, f32[1,216]{1,0:T(1,128)}, f32[27,128]{1,0:T(8,128)}, f32[27,128]{1,0:T(8,128)}, /*index=5*/f32[27,128]{1,0:T(8,128)}) custom-call(f32[40,128]{1,0:T(8,128)S(1)} %shard_map.134.in_ref, f32[40,128]{1,0:T(8,128)S(1)} %collective-permute-done.7.other_ref, f32[8,128]{1,0:T(8,128)S(1)} %copy-done.2, ...), custom_call_target="tpu_custom_call" | custom-call | tf_op jit(solution)/shard_map/pallas_call | solution.py:34
  (15 shorter events, 0.1 us)
Async XLA Ops:
  3.6 28.9 %copy-start = (bf16[4,544,128]{2,1,0:T(8,128)(2,1)S(1)}, bf16[4,544,128]{2,1,0:T(8,128)(2,1)}, u32[]{:S(2)}) copy-start(bf16[4,544,128]{2,1,0:T(8,128)(2,1)} %get-tuple-element.23.slab_ref) | copy-start | bytes 1671172
  3.7 20.8 %all-to-all-start = ((bf16[64,5,4,128]{3,2,1,0:T(4,128)(2,1)}), bf16[64,5,4,128]{3,2,1,0:T(4,128)(2,1)S(1)}, u32[]{:S(2)}, u32[]{:S(2)}) async-start(bf16[64,5,4,128]{3,2,1,0:T(4,128)(2,1)} %get-tuple-element.25), calls=%async_computation | async-start | bytes 655360 | tf_op jit(solution)/shard_map/all_to_all | solution.py:582
  14.1 15.7 %collective-permute-start = (bf16[2,544,128]{2,1,0:T(8,128)(2,1)}, bf16[2,544,128]{2,1,0:T(8,128)(2,1)S(1)}, u32[]{:S(2)}, u32[]{:S(2)}) collective-permute-start(bf16[2,544,128]{2,1,0:T(8,128)(2,1)} %get-tuple-element.24), channel_id=1, source_target_pairs={{0,224},{32,0},{64,32},{96,64},{128,96},{160,128},{192,160},{224,1... | collective-permute-start | bytes 835592 | tf_op jit(solution)/shard_map/ppermute | solution.py:580
  24.5 6.5 %collective-permute-start.2 = (bf16[128,128]{1,0:T(8,128)(2,1)S(1)}, bf16[128,128]{1,0:T(8,128)(2,1)S(1)}, u32[]{:S(2)}, u32[]{:S(2)}) collective-permute-start(bf16[128,128]{1,0:T(8,128)(2,1)S(1)} %shard_map.128.bank_ref), channel_id=1, source_target_pairs={{0,8},{8,16},{16,24},{24,0},{1,9},{9,17},{17,25},{25,1},{2,10},{10... | collective-permute-start | bytes 98312 | tf_op jit(solution)/shard_map/ppermute | solution.py:549
  27.6 5.0 %collective-permute-start.1 = (bf16[128,128]{1,0:T(8,128)(2,1)S(1)}, bf16[128,128]{1,0:T(8,128)(2,1)S(1)}, u32[]{:S(2)}, u32[]{:S(2)}) collective-permute-start(bf16[128,128]{1,0:T(8,128)(2,1)S(1)} %shard_map.128.bank_ref), channel_id=1, source_target_pairs={{0,24},{8,0},{16,8},{24,16},{1,25},{9,1},{17,9},{25,17},{2,26},{10... | collective-permute-start | bytes 98312 | tf_op jit(solution)/shard_map/ppermute | solution.py:549
  32.6 4.1 %copy-start.1 = (f32[3456]{0:T(1024)S(1)}, f32[3456]{0:T(1024)}, u32[]{:S(2)}) copy-start(f32[3456]{0:T(1024)} %param.10) | copy-start | bytes 41476
  32.7 3.6 %copy-start.2 = (f32[8,128]{1,0:T(8,128)S(1)}, f32[8,128]{1,0:T(8,128)}, u32[]{:S(2)}) copy-start(f32[8,128]{1,0:T(8,128)} %get-tuple-element.31.own_ref) | copy-start | bytes 12292
  32.7 8.9 %collective-permute-start.3 = (bf16[496,128]{1,0:T(8,128)(2,1)S(1)}, bf16[496,128]{1,0:T(8,128)(2,1)S(1)}, u32[]{:S(2)}, u32[]{:S(2)}) collective-permute-start(bf16[496,128]{1,0:T(8,128)(2,1)S(1)} %get-tuple-element.27), channel_id=1, source_target_pairs={{0,8},{8,16},{16,24},{24,0},{1,9},{9,17},{17,25},{25,1},{2,10},{10... | collective-permute-start | bytes 380936 | tf_op jit(solution)/shard_map/ppermute | solution.py:549
  36.3 6.6 %collective-permute-start.4 = (bf16[496,128]{1,0:T(8,128)(2,1)S(1)}, bf16[496,128]{1,0:T(8,128)(2,1)S(1)}, u32[]{:S(2)}, u32[]{:S(2)}) collective-permute-start(bf16[496,128]{1,0:T(8,128)(2,1)S(1)} %get-tuple-element.28), channel_id=1, source_target_pairs={{0,24},{8,0},{16,8},{24,16},{1,25},{9,1},{17,9},{25,17},{2,26},{10... | collective-permute-start | bytes 380936 | tf_op jit(solution)/shard_map/ppermute | solution.py:549
  36.4 2.5 %collective-permute-start.5 = (f32[8,128]{1,0:T(8,128)S(1)}, f32[8,128]{1,0:T(8,128)S(1)}, u32[]{:S(2)}, u32[]{:S(2)}) collective-permute-start(f32[8,128]{1,0:T(8,128)S(1)} %copy-done.2), channel_id=1, source_target_pairs={{0,2},{2,0},{4,6},{6,4},{1,3},{3,1},{5,7},{7,5},{8,10},{10,8},{12,... | collective-permute-start | bytes 12296 | tf_op jit(solution)/shard_map/ppermute | solution.py:581
  46.4 2.7 %collective-permute-start.6 = (f32[8,42,128]{2,1,0:T(8,128)S(1)}, f32[8,42,128]{2,1,0:T(8,128)S(1)}, u32[]{:S(2)}, u32[]{:S(2)}) collective-permute-start(f32[8,42,128]{2,1,0:T(8,128)S(1)} %get-tuple-element.33), channel_id=1, source_target_pairs={{0,1},{1,0},{2,3},{3,2},{4,5},{5,4},{6,7},{7,6},{8,9},{9,8},{10,11... | collective-permute-start | bytes 516104 | tf_op jit(solution)/shard_map/ppermute | solution.py:553
  70.3 4.6 %copy-start.3 = (f32[3456]{0:T(1024)S(1)}, f32[3456]{0:T(1024)}, u32[]{:S(2)}) copy-start(f32[3456]{0:T(1024)} %param.11) | copy-start | bytes 41476
  70.3 4.6 %copy-start.4 = (f32[3456]{0:T(1024)S(1)}, f32[3456]{0:T(1024)}, u32[]{:S(2)}) copy-start(f32[3456]{0:T(1024)} %param.12) | copy-start | bytes 41476
  70.3 4.6 %collective-permute-start.7 = (f32[40,128]{1,0:T(8,128)S(1)}, f32[40,128]{1,0:T(8,128)S(1)}, u32[]{:S(2)}, u32[]{:S(2)}) collective-permute-start(f32[40,128]{1,0:T(8,128)S(1)} %shard_map.134.in_ref), channel_id=1, source_target_pairs={{0,1},{1,0},{2,3},{3,2},{4,5},{5,4},{6,7},{7,6},{8,9},{9,8},{10,11... | collective-permute-start | bytes 61448 | tf_op jit(solution)/shard_map/ppermute | solution.py:553

commit v6 on v5

--- a/solution.py
+++ b/solution.py
@@ -137,7 +137,7 @@
     out_ref[...] = jnp.concatenate(rows, axis=0).astype(BF16)
 
 
-def y_messages(slab_ref, next_ref, in_ref, nb_ref, pb_ref, up_ref, dn_ref, beyond_ref):
+def y_messages(slab_ref, next_ref, in_ref, pb_ref, nb_ref, up_ref, dn_ref, beyond_ref):
     slabs = [slab_ref.at[x] for x in range(4)] + [next_ref.at[x] for x in range(2)]
     first, last = [], []
     for xe, slab in enumerate(slabs):
@@ -273,7 +273,7 @@
 
 
 def gradients(
-    slab_ref, next_ref, beyond_ref, yp_ref, yn_ref, bank_ref, pb_ref, nb_ref, wb_ref, pick_ref, sib_ref,
+    slab_ref, next_ref, beyond_ref, yn_ref, yp_ref, bank_ref, pb_ref, nb_ref, wb_ref, pick_ref, sib_ref,
     keep_ref, send_ref,
     e_ref, ve_ref, ga_ref, rows_ref, wide_ref,
 ):
@@ -583,7 +583,7 @@
     bank = call(bank_rows, shape((128, 128), BF16), message)
     near_banks = turn(bank, 1), turn(bank, 3)
     up, down, beyond = call(
-        y_messages, (along_y, along_y, shape((16, 640), F32)), slabs, next_x, message, *near_banks[::-1]
+        y_messages, (along_y, along_y, shape((16, 640), F32)), slabs, next_x, message, *near_banks
     )
     before_y, after_y = turn(up, 1), turn(down, 3)
     keep, send = call(
@@ -592,8 +592,8 @@
         slabs,
         next_x,
         beyond,
+        after_y,
         before_y,
-        after_y,
         bank,
         *near_banks,
         narrow_band,

time: 76 us -> 75.7 us (level)
    ppermute x2, starting transfers between devices: 5.32 us -> 7.12 us  [swap(): return lax.ppermute(value, 'core', [(0, 1), (1, 0)])]
    ppermute x4, starting transfers between devices: 8.9 us -> 7.6 us  [turn(): return lax.ppermute(value, GY, [(i, (i + by) % 4) for i in range(4)])]
  transfers between devices with their start and end apart: 9 -> 9, of which waited for: 8 -> 7; matrix products, arithmetic and copies ran while one was open for 0% -> 0% of each run, Pallas kernels for 1% -> 1%
where the time goes in v6:
time: 75.7 us; the launch traced here: 75.5 us
  starting transfers between devices  29.3 us (39%)
  blocking collectives  20.6 us (27%)
  waiting for transfers between devices  16.4 us (22%)
  Pallas kernels  8.44 us (11%)
    all_to_all x1, blocking collectives, local(): sums = lax.all_to_all(sums, ('zl', 'zh'), 0, 0, tiled=True)  10.8 us
    all_to_all x1, starting transfers between devices, local(): message = lax.all_to_all(message, GX + GZ, 0, 0, tiled=True)  10.5 us
    all_to_all x1, blocking collectives, local(): sums = lax.all_to_all(sums, ('x', 'y'), 0, 0, tiled=True)  9.76 us
    pallas_call x9, Pallas kernels, call(): pl.pallas_call(kernel, out_shape=out_shapes, in_specs=[space] * len(args)...  8.44 us
    ppermute x4, starting transfers between devices, turn(): return lax.ppermute(value, GY, [(i, (i + by) % 4) for i in range(4)])  7.6 us
    ppermute x2, starting transfers between devices, swap(): return lax.ppermute(value, 'core', [(0, 1), (1, 0)])  7.12 us
    ppermute x4, waiting for transfers between devices, turn(): return lax.ppermute(value, GY, [(i, (i + by) % 4) for i in range(4)])  6.68 us
    all_to_all x1, waiting for transfers between devices, local(): message = lax.all_to_all(message, GX + GZ, 0, 0, tiled=True)  6.51 us
  transfers between devices with their start and end apart: 9, of which 7 were waited for; matrix products, arithmetic and copies ran while one was open for 0% of the time, Pallas kernels for 1%

profile of v6, /device:TPU:1, one launch (start us, length us, event | category | flops | bytes accessed | tf_op | source)
XLA Modules:
  0.0 75.5 jit_solution(2361658191539747484)
XLA Ops:
  0.6 3.0 %shard_map.127 = (bf16[4,544,128]{2,1,0:T(8,128)(2,1)}, bf16[2,544,128]{2,1,0:T(8,128)(2,1)}, bf16[64,5,4,128]{3,2,1,0:T(4,128)(2,1)}, f32[8,128]{1,0:T(8,128)}) custom-call(bf16[2048,128]{1,0:T(8,128)(2,1)} %bitcast.18, bf16[128,128]{1,0:T(8,128)(2,1)} %bitcast.19, f32[1,216]{1,0:T(1,128)} %bitcast.20, f32[1,216]{1,0:T(1,128)} %bitcast.21, f32[1,216]{1,0:T(1,128)} %bitcast.22), custom_call_target="tpu_custom_call" | custom-call | tf_op jit(solution)/shard_map/pallas_call | solution.py:34
  3.7 10.5 %all-to-all-start = ((bf16[64,5,4,128]{3,2,1,0:T(4,128)(2,1)}), bf16[64,5,4,128]{3,2,1,0:T(4,128)(2,1)S(1)}, u32[]{:S(2)}, u32[]{:S(2)}) async-start(bf16[64,5,4,128]{3,2,1,0:T(4,128)(2,1)} %get-tuple-element.25), calls=%async_computation | async-start | bytes 655360 | tf_op jit(solution)/shard_map/all_to_all | solution.py:582
  14.1 3.8 %collective-permute-start = (bf16[2,544,128]{2,1,0:T(8,128)(2,1)}, bf16[2,544,128]{2,1,0:T(8,128)(2,1)S(1)}, u32[]{:S(2)}, u32[]{:S(2)}) collective-permute-start(bf16[2,544,128]{2,1,0:T(8,128)(2,1)} %get-tuple-element.24), channel_id=1, source_target_pairs={{0,224},{32,0},{64,32},{96,64},{128,96},{160,128},{192,160},{224,1... | collective-permute-start | bytes 835592 | tf_op jit(solution)/shard_map/ppermute | solution.py:580
  18.0 6.5 %all-to-all-done.in_ref = bf16[64,5,4,128]{3,2,1,0:T(4,128)(2,1)S(1)} async-done(((bf16[64,5,4,128]{3,2,1,0:T(4,128)(2,1)}), bf16[64,5,4,128]{3,2,1,0:T(4,128)(2,1)S(1)}, u32[]{:S(2)}, u32[]{:S(2)}) %all-to-all-start) | async-done | bytes 327712 | tf_op jit(solution)/shard_map/all_to_all | solution.py:582
  24.5 5.2 %collective-permute-start.2 = (bf16[128,128]{1,0:T(8,128)(2,1)S(1)}, bf16[128,128]{1,0:T(8,128)(2,1)S(1)}, u32[]{:S(2)}, u32[]{:S(2)}) collective-permute-start(bf16[128,128]{1,0:T(8,128)(2,1)S(1)} %shard_map.128.bank_ref), channel_id=1, source_target_pairs={{0,24},{8,0},{16,8},{24,16},{1,25},{9,1},{17,9},{25,17},{2,26},{10... | collective-permute-start | bytes 98312 | tf_op jit(solution)/shard_map/ppermute | solution.py:549
  29.7 0.0 collective-permute-start.1
  29.7 0.0 collective-permute-done.next_ref
  29.7 1.0 %collective-permute-done.2.nb_ref = bf16[128,128]{1,0:T(8,128)(2,1)S(1)} collective-permute-done((bf16[128,128]{1,0:T(8,128)(2,1)S(1)}, bf16[128,128]{1,0:T(8,128)(2,1)S(1)}, u32[]{:S(2)}, u32[]{:S(2)}) %collective-permute-start.2) | collective-permute-done | bytes 32800 | tf_op jit(solution)/shard_map/ppermute | solution.py:549
  30.8 3.9 %collective-permute-done.1.pb_ref = bf16[128,128]{1,0:T(8,128)(2,1)S(1)} collective-permute-done((bf16[128,128]{1,0:T(8,128)(2,1)S(1)}, bf16[128,128]{1,0:T(8,128)(2,1)S(1)}, u32[]{:S(2)}, u32[]{:S(2)}) %collective-permute-start.1) | collective-permute-done | bytes 32800 | tf_op jit(solution)/shard_map/ppermute | solution.py:549
  34.6 0.2 shard_map.129
  34.8 0.4 collective-permute-start.3
  35.2 2.0 %collective-permute-start.4 = (bf16[496,128]{1,0:T(8,128)(2,1)S(1)}, bf16[496,128]{1,0:T(8,128)(2,1)S(1)}, u32[]{:S(2)}, u32[]{:S(2)}) collective-permute-start(bf16[496,128]{1,0:T(8,128)(2,1)S(1)} %get-tuple-element.28), channel_id=1, source_target_pairs={{0,8},{8,16},{16,24},{24,0},{1,9},{9,17},{17,25},{25,1},{2,10},{10... | collective-permute-start | bytes 380936 | tf_op jit(solution)/shard_map/ppermute | solution.py:549
  37.2 0.3 collective-permute-start.5
  37.5 0.9 %shard_map.130 = (bf16[256,512]{1,0:T(8,128)(2,1)S(1)}, bf16[512,128]{1,0:T(8,128)(2,1)S(1)}) custom-call(f32[27,128]{1,0:T(8,128)S(1)} %bitcast.14), custom_call_target="tpu_custom_call" | custom-call | tf_op jit(solution)/shard_map/pallas_call | solution.py:34
  38.4 1.3 %collective-permute-done.5.sib_ref = f32[8,128]{1,0:T(8,128)S(1)} collective-permute-done((f32[8,128]{1,0:T(8,128)S(1)}, f32[8,128]{1,0:T(8,128)S(1)}, u32[]{:S(2)}, u32[]{:S(2)}) %collective-permute-start.5) | collective-permute-done | bytes 4128 | tf_op jit(solution)/shard_map/ppermute | solution.py:581
  39.7 1.8 %collective-permute-done.3.yn_ref = bf16[496,128]{1,0:T(8,128)(2,1)S(1)} collective-permute-done((bf16[496,128]{1,0:T(8,128)(2,1)S(1)}, bf16[496,128]{1,0:T(8,128)(2,1)S(1)}, u32[]{:S(2)}, u32[]{:S(2)}) %collective-permute-start.3) | collective-permute-done | bytes 127008 | tf_op jit(solution)/shard_map/ppermute | solution.py:549
  41.5 3.4 %shard_map.131 = (f32[8,42,128]{2,1,0:T(8,128)S(1)}, f32[8,42,128]{2,1,0:T(8,128)S(1)}) custom-call(bf16[4,544,128]{2,1,0:T(8,128)(2,1)S(1)} %copy-done, bf16[2,544,128]{2,1,0:T(8,128)(2,1)S(1)} %collective-permute-done.next_ref, f32[16,640]{1,0:T(8,128)S(1)} %get-tuple-element.26.beyond_ref, bf16[496,128]{1,0:T(8,128)(2,1)S(1)} %collective-permute-done.3.yn_ref, ...), custom_call_target="tpu_custom_call" | custom-call | tf_op jit(solution)/shard_map/pallas_call | solution.py:34
  44.9 3.8 %collective-permute-start.6 = (f32[8,42,128]{2,1,0:T(8,128)S(1)}, f32[8,42,128]{2,1,0:T(8,128)S(1)}, u32[]{:S(2)}, u32[]{:S(2)}) collective-permute-start(f32[8,42,128]{2,1,0:T(8,128)S(1)} %get-tuple-element.33), channel_id=1, source_target_pairs={{0,1},{1,0},{2,3},{3,2},{4,5},{5,4},{6,7},{7,6},{8,9},{9,8},{10,11... | collective-permute-start | bytes 516104 | tf_op jit(solution)/shard_map/ppermute | solution.py:553
  48.7 1.1 %collective-permute-done.6.b_ref = f32[8,42,128]{2,1,0:T(8,128)S(1)} collective-permute-done((f32[8,42,128]{2,1,0:T(8,128)S(1)}, f32[8,42,128]{2,1,0:T(8,128)S(1)}, u32[]{:S(2)}, u32[]{:S(2)}) %collective-permute-start.6) | collective-permute-done | bytes 172064 | tf_op jit(solution)/shard_map/ppermute | solution.py:553
  49.8 10.8 %all_to_all.15.in_ref = f32[8,42,128]{2,1,0:T(8,128)S(1)} all-to-all(f32[8,42,128]{2,1,0:T(8,128)S(1)} %shard_map.132), channel_id=1, replica_groups=mesh['zl'=2,'x'=4,'zh'=4,'y'=4,'core'=2] {'zl','zh'}, dimensions={0} | all-to-all | bytes 344064 | tf_op jit(solution)/shard_map/all_to_all | solution.py:611
  60.6 9.8 %all_to_all.16.in_ref = f32[16,21,128]{2,1,0:T(8,128)S(1)} all-to-all(f32[16,21,128]{2,1,0:T(8,128)S(1)} %shard_map.133), channel_id=1, replica_groups=mesh['zl'=2,'x'=4,'zh'=4,'y'=4,'core'=2] {'x','y'}, dimensions={0} | all-to-all | bytes 344064 | tf_op jit(solution)/shard_map/all_to_all | solution.py:613
  70.4 3.3 %collective-permute-start.7 = (f32[40,128]{1,0:T(8,128)S(1)}, f32[40,128]{1,0:T(8,128)S(1)}, u32[]{:S(2)}, u32[]{:S(2)}) collective-permute-start(f32[40,128]{1,0:T(8,128)S(1)} %shard_map.134.in_ref), channel_id=1, source_target_pairs={{0,1},{1,0},{2,3},{3,2},{4,5},{5,4},{6,7},{7,6},{8,9},{9,8},{10,11... | collective-permute-start | bytes 61448 | tf_op jit(solution)/shard_map/ppermute | solution.py:553
  73.7 0.8 %collective-permute-done.7.other_ref = f32[40,128]{1,0:T(8,128)S(1)} collective-permute-done((f32[40,128]{1,0:T(8,128)S(1)}, f32[40,128]{1,0:T(8,128)S(1)}, u32[]{:S(2)}, u32[]{:S(2)}) %collective-permute-start.7) | collective-permute-done | bytes 20512 | tf_op jit(solution)/shard_map/ppermute | solution.py:553
  74.6 0.9 %shard_map.135 = (f32[1,216]{1,0:T(1,128)}, f32[1,216]{1,0:T(1,128)}, f32[1,216]{1,0:T(1,128)}, f32[27,128]{1,0:T(8,128)}, f32[27,128]{1,0:T(8,128)}, /*index=5*/f32[27,128]{1,0:T(8,128)}) custom-call(f32[40,128]{1,0:T(8,128)S(1)} %shard_map.134.in_ref, f32[40,128]{1,0:T(8,128)S(1)} %collective-permute-done.7.other_ref, f32[8,128]{1,0:T(8,128)S(1)} %copy-done.2, ...), custom_call_target="tpu_custom_call" | custom-call | tf_op jit(solution)/shard_map/pallas_call | solution.py:34
  (15 shorter events, 0.1 us)
Async XLA Ops:
  3.6 31.0 %copy-start = (bf16[4,544,128]{2,1,0:T(8,128)(2,1)S(1)}, bf16[4,544,128]{2,1,0:T(8,128)(2,1)}, u32[]{:S(2)}) copy-start(bf16[4,544,128]{2,1,0:T(8,128)(2,1)} %get-tuple-element.23.slab_ref) | copy-start | bytes 1671172
  3.7 20.8 %all-to-all-start = ((bf16[64,5,4,128]{3,2,1,0:T(4,128)(2,1)}), bf16[64,5,4,128]{3,2,1,0:T(4,128)(2,1)S(1)}, u32[]{:S(2)}, u32[]{:S(2)}) async-start(bf16[64,5,4,128]{3,2,1,0:T(4,128)(2,1)} %get-tuple-element.25), calls=%async_computation | async-start | bytes 655360 | tf_op jit(solution)/shard_map/all_to_all | solution.py:582
  14.1 15.6 %collective-permute-start = (bf16[2,544,128]{2,1,0:T(8,128)(2,1)}, bf16[2,544,128]{2,1,0:T(8,128)(2,1)S(1)}, u32[]{:S(2)}, u32[]{:S(2)}) collective-permute-start(bf16[2,544,128]{2,1,0:T(8,128)(2,1)} %get-tuple-element.24), channel_id=1, source_target_pairs={{0,224},{32,0},{64,32},{96,64},{128,96},{160,128},{192,160},{224,1... | collective-permute-start | bytes 835592 | tf_op jit(solution)/shard_map/ppermute | solution.py:580
  24.5 6.2 %collective-permute-start.2 = (bf16[128,128]{1,0:T(8,128)(2,1)S(1)}, bf16[128,128]{1,0:T(8,128)(2,1)S(1)}, u32[]{:S(2)}, u32[]{:S(2)}) collective-permute-start(bf16[128,128]{1,0:T(8,128)(2,1)S(1)} %shard_map.128.bank_ref), channel_id=1, source_target_pairs={{0,24},{8,0},{16,8},{24,16},{1,25},{9,1},{17,9},{25,17},{2,26},{10... | collective-permute-start | bytes 98312 | tf_op jit(solution)/shard_map/ppermute | solution.py:549
  29.7 4.9 %collective-permute-start.1 = (bf16[128,128]{1,0:T(8,128)(2,1)S(1)}, bf16[128,128]{1,0:T(8,128)(2,1)S(1)}, u32[]{:S(2)}, u32[]{:S(2)}) collective-permute-start(bf16[128,128]{1,0:T(8,128)(2,1)S(1)} %shard_map.128.bank_ref), channel_id=1, source_target_pairs={{0,8},{8,16},{16,24},{24,0},{1,9},{9,17},{17,25},{25,1},{2,10},{10... | collective-permute-start | bytes 98312 | tf_op jit(solution)/shard_map/ppermute | solution.py:549
  34.6 2.9 %copy-start.1 = (f32[3456]{0:T(1024)S(1)}, f32[3456]{0:T(1024)}, u32[]{:S(2)}) copy-start(f32[3456]{0:T(1024)} %param.10) | copy-start | bytes 41476
  34.8 2.4 %copy-start.2 = (f32[8,128]{1,0:T(8,128)S(1)}, f32[8,128]{1,0:T(8,128)}, u32[]{:S(2)}) copy-start(f32[8,128]{1,0:T(8,128)} %get-tuple-element.31.own_ref) | copy-start | bytes 12292
  34.8 6.7 %collective-permute-start.3 = (bf16[496,128]{1,0:T(8,128)(2,1)S(1)}, bf16[496,128]{1,0:T(8,128)(2,1)S(1)}, u32[]{:S(2)}, u32[]{:S(2)}) collective-permute-start(bf16[496,128]{1,0:T(8,128)(2,1)S(1)} %get-tuple-element.27), channel_id=1, source_target_pairs={{0,24},{8,0},{16,8},{24,16},{1,25},{9,1},{17,9},{25,17},{2,26},{10... | collective-permute-start | bytes 380936 | tf_op jit(solution)/shard_map/ppermute | solution.py:549
  35.2 6.3 %collective-permute-start.4 = (bf16[496,128]{1,0:T(8,128)(2,1)S(1)}, bf16[496,128]{1,0:T(8,128)(2,1)S(1)}, u32[]{:S(2)}, u32[]{:S(2)}) collective-permute-start(bf16[496,128]{1,0:T(8,128)(2,1)S(1)} %get-tuple-element.28), channel_id=1, source_target_pairs={{0,8},{8,16},{16,24},{24,0},{1,9},{9,17},{17,25},{25,1},{2,10},{10... | collective-permute-start | bytes 380936 | tf_op jit(solution)/shard_map/ppermute | solution.py:549
  37.2 2.5 %collective-permute-start.5 = (f32[8,128]{1,0:T(8,128)S(1)}, f32[8,128]{1,0:T(8,128)S(1)}, u32[]{:S(2)}, u32[]{:S(2)}) collective-permute-start(f32[8,128]{1,0:T(8,128)S(1)} %copy-done.2), channel_id=1, source_target_pairs={{0,2},{2,0},{4,6},{6,4},{1,3},{3,1},{5,7},{7,5},{8,10},{10,8},{12,... | collective-permute-start | bytes 12296 | tf_op jit(solution)/shard_map/ppermute | solution.py:581
  44.9 4.9 %collective-permute-start.6 = (f32[8,42,128]{2,1,0:T(8,128)S(1)}, f32[8,42,128]{2,1,0:T(8,128)S(1)}, u32[]{:S(2)}, u32[]{:S(2)}) collective-permute-start(f32[8,42,128]{2,1,0:T(8,128)S(1)} %get-tuple-element.33), channel_id=1, source_target_pairs={{0,1},{1,0},{2,3},{3,2},{4,5},{5,4},{6,7},{7,6},{8,9},{9,8},{10,11... | collective-permute-start | bytes 516104 | tf_op jit(solution)/shard_map/ppermute | solution.py:553
  70.4 4.2 %copy-start.3 = (f32[3456]{0:T(1024)S(1)}, f32[3456]{0:T(1024)}, u32[]{:S(2)}) copy-start(f32[3456]{0:T(1024)} %param.11) | copy-start | bytes 41476
  70.4 4.2 %copy-start.4 = (f32[3456]{0:T(1024)S(1)}, f32[3456]{0:T(1024)}, u32[]{:S(2)}) copy-start(f32[3456]{0:T(1024)} %param.12) | copy-start | bytes 41476
  70.4 4.2 %collective-permute-start.7 = (f32[40,128]{1,0:T(8,128)S(1)}, f32[40,128]{1,0:T(8,128)S(1)}, u32[]{:S(2)}, u32[]{:S(2)}) collective-permute-start(f32[40,128]{1,0:T(8,128)S(1)} %shard_map.134.in_ref), channel_id=1, source_target_pairs={{0,1},{1,0},{2,3},{3,2},{4,5},{5,4},{6,7},{7,6},{8,9},{9,8},{10,11... | collective-permute-start | bytes 61448 | tf_op jit(solution)/shard_map/ppermute | solution.py:553

commit v7 on v6

--- a/solution.py
+++ b/solution.py
@@ -436,14 +436,15 @@
     for j in range(7):
         wide_ref[64 * j : 64 * j + 64, :] = wide[:, 128 * j : 128 * j + 128]
     core = lax.axis_index("core")
+    parts = [flat[0:14], flat[14:28]]
+    mine = jnp.where(core == 0, parts[0], parts[1])
+    others = jnp.where(core == 0, parts[1], parts[0])
     for p in range(8):
         zl, zh = p // 4, p % 4
-        halves = []
-        for yh in range(2):
-            rows = [wide_ref[pl.ds(64 * j + 32 * zl + 2 * zh + yh, 4, stride=8), :] for j in range(7)]
-            halves.append(jnp.concatenate(rows + [flat[14 * yh : 14 * yh + 14]], axis=0))
-        keep_ref[p] = jnp.where(core == 0, halves[0], halves[1])
-        send_ref[p] = jnp.where(core == 0, halves[1], halves[0])
+        for ref, yh, part in ((keep_ref, core, mine), (send_ref, 1 - core, others)):
+            for j in range(7):
+                ref[p, 4 * j : 4 * j + 4, :] = wide_ref[pl.ds(64 * j + 32 * zl + 2 * zh + yh, 4, stride=8), :]
+            ref[p, 28:42, :] = part
 
 
 def first_stage(a_ref, b_ref, out_ref):
@@ -458,7 +459,7 @@
         block = [total[4 * j + x : 4 * j + x + 1] for j in range(7)]
         rows = jnp.concatenate(block + [total[28:42]], axis=0)
         for y in range(4):
-            out_ref[4 * x + y] = rows
+            out_ref[4 * y + x] = rows
 
 
 def third_stage(in_ref, own_ref, sib_ref, out_ref):
@@ -610,7 +611,7 @@
     sums = call(first_stage, shape((8, 42, 128), F32), keep, swap(send))
     sums = lax.all_to_all(sums, ("zl", "zh"), 0, 0, tiled=True)
     sums = call(second_stage, shape((16, 21, 128), F32), sums)
-    sums = lax.all_to_all(sums, ("x", "y"), 0, 0, tiled=True)
+    sums = lax.all_to_all(sums, ("y", "x"), 0, 0, tiled=True)
     half = call(third_stage, shape((40, 128), F32), sums, own, sibling)
     one, rows = shape((1, 216), F32), shape((27, 128), F32)
     new = call(update, (one, one, one, rows, rows, rows), half, swap(half), own, *narrow)

time: 75.7 us -> 76 us (level)
  no operation moved by 1% of the time
where the time goes in v7:
time: 76 us; the launch traced here: 75.7 us
  starting transfers between devices  29.6 us (39%)
  blocking collectives  20.6 us (27%)
  waiting for transfers between devices  16.4 us (22%)
  Pallas kernels  8.44 us (11%)
    all_to_all x1, blocking collectives, local(): sums = lax.all_to_all(sums, ('zl', 'zh'), 0, 0, tiled=True)  10.8 us
    all_to_all x1, starting transfers between devices, local(): message = lax.all_to_all(message, GX + GZ, 0, 0, tiled=True)  10.5 us
    all_to_all x1, blocking collectives, local(): sums = lax.all_to_all(sums, ('y', 'x'), 0, 0, tiled=True)  9.81 us
    pallas_call x9, Pallas kernels, call(): pl.pallas_call(kernel, out_shape=out_shapes, in_specs=[space] * len(args)...  8.44 us
    ppermute x4, starting transfers between devices, turn(): return lax.ppermute(value, GY, [(i, (i + by) % 4) for i in range(4)])  7.6 us
    ppermute x2, starting transfers between devices, swap(): return lax.ppermute(value, 'core', [(0, 1), (1, 0)])  7.34 us
    ppermute x4, waiting for transfers between devices, turn(): return lax.ppermute(value, GY, [(i, (i + by) % 4) for i in range(4)])  6.68 us
    all_to_all x1, waiting for transfers between devices, local(): message = lax.all_to_all(message, GX + GZ, 0, 0, tiled=True)  6.51 us
  transfers between devices with their start and end apart: 9, of which 7 were waited for; matrix products, arithmetic and copies ran while one was open for 0% of the time, Pallas kernels for 1%

profile of v7, /device:TPU:1, one launch (start us, length us, event | category | flops | bytes accessed | tf_op | source)
XLA Modules:
  0.0 75.7 jit_solution(4718563452515284320)
XLA Ops:
  0.6 3.0 %shard_map.127 = (bf16[4,544,128]{2,1,0:T(8,128)(2,1)}, bf16[2,544,128]{2,1,0:T(8,128)(2,1)}, bf16[64,5,4,128]{3,2,1,0:T(4,128)(2,1)}, f32[8,128]{1,0:T(8,128)}) custom-call(bf16[2048,128]{1,0:T(8,128)(2,1)} %bitcast.18, bf16[128,128]{1,0:T(8,128)(2,1)} %bitcast.19, f32[1,216]{1,0:T(1,128)} %bitcast.20, f32[1,216]{1,0:T(1,128)} %bitcast.21, f32[1,216]{1,0:T(1,128)} %bitcast.22), custom_call_target="tpu_custom_call" | custom-call | tf_op jit(solution)/shard_map/pallas_call | solution.py:34
  3.7 10.5 %all-to-all-start = ((bf16[64,5,4,128]{3,2,1,0:T(4,128)(2,1)}), bf16[64,5,4,128]{3,2,1,0:T(4,128)(2,1)S(1)}, u32[]{:S(2)}, u32[]{:S(2)}) async-start(bf16[64,5,4,128]{3,2,1,0:T(4,128)(2,1)} %get-tuple-element.25), calls=%async_computation | async-start | bytes 655360 | tf_op jit(solution)/shard_map/all_to_all | solution.py:583
  14.1 3.8 %collective-permute-start = (bf16[2,544,128]{2,1,0:T(8,128)(2,1)}, bf16[2,544,128]{2,1,0:T(8,128)(2,1)S(1)}, u32[]{:S(2)}, u32[]{:S(2)}) collective-permute-start(bf16[2,544,128]{2,1,0:T(8,128)(2,1)} %get-tuple-element.24), channel_id=1, source_target_pairs={{0,224},{32,0},{64,32},{96,64},{128,96},{160,128},{192,160},{224,1... | collective-permute-start | bytes 835592 | tf_op jit(solution)/shard_map/ppermute | solution.py:581
  18.0 6.5 %all-to-all-done.in_ref = bf16[64,5,4,128]{3,2,1,0:T(4,128)(2,1)S(1)} async-done(((bf16[64,5,4,128]{3,2,1,0:T(4,128)(2,1)}), bf16[64,5,4,128]{3,2,1,0:T(4,128)(2,1)S(1)}, u32[]{:S(2)}, u32[]{:S(2)}) %all-to-all-start) | async-done | bytes 327712 | tf_op jit(solution)/shard_map/all_to_all | solution.py:583
  24.5 5.2 %collective-permute-start.2 = (bf16[128,128]{1,0:T(8,128)(2,1)S(1)}, bf16[128,128]{1,0:T(8,128)(2,1)S(1)}, u32[]{:S(2)}, u32[]{:S(2)}) collective-permute-start(bf16[128,128]{1,0:T(8,128)(2,1)S(1)} %shard_map.128.bank_ref), channel_id=1, source_target_pairs={{0,24},{8,0},{16,8},{24,16},{1,25},{9,1},{17,9},{25,17},{2,26},{10... | collective-permute-start | bytes 98312 | tf_op jit(solution)/shard_map/ppermute | solution.py:550
  29.7 0.0 collective-permute-start.1
  29.7 0.0 collective-permute-done.next_ref
  29.7 1.0 %collective-permute-done.2.nb_ref = bf16[128,128]{1,0:T(8,128)(2,1)S(1)} collective-permute-done((bf16[128,128]{1,0:T(8,128)(2,1)S(1)}, bf16[128,128]{1,0:T(8,128)(2,1)S(1)}, u32[]{:S(2)}, u32[]{:S(2)}) %collective-permute-start.2) | collective-permute-done | bytes 32800 | tf_op jit(solution)/shard_map/ppermute | solution.py:550
  30.8 3.9 %collective-permute-done.1.pb_ref = bf16[128,128]{1,0:T(8,128)(2,1)S(1)} collective-permute-done((bf16[128,128]{1,0:T(8,128)(2,1)S(1)}, bf16[128,128]{1,0:T(8,128)(2,1)S(1)}, u32[]{:S(2)}, u32[]{:S(2)}) %collective-permute-start.1) | collective-permute-done | bytes 32800 | tf_op jit(solution)/shard_map/ppermute | solution.py:550
  34.6 0.2 shard_map.129
  34.8 0.4 collective-permute-start.3
  35.2 2.0 %collective-permute-start.4 = (bf16[496,128]{1,0:T(8,128)(2,1)S(1)}, bf16[496,128]{1,0:T(8,128)(2,1)S(1)}, u32[]{:S(2)}, u32[]{:S(2)}) collective-permute-start(bf16[496,128]{1,0:T(8,128)(2,1)S(1)} %get-tuple-element.28), channel_id=1, source_target_pairs={{0,8},{8,16},{16,24},{24,0},{1,9},{9,17},{17,25},{25,1},{2,10},{10... | collective-permute-start | bytes 380936 | tf_op jit(solution)/shard_map/ppermute | solution.py:550
  37.2 0.3 collective-permute-start.5
  37.5 0.9 %shard_map.130 = (bf16[256,512]{1,0:T(8,128)(2,1)S(1)}, bf16[512,128]{1,0:T(8,128)(2,1)S(1)}) custom-call(f32[27,128]{1,0:T(8,128)S(1)} %bitcast.14), custom_call_target="tpu_custom_call" | custom-call | tf_op jit(solution)/shard_map/pallas_call | solution.py:34
  38.4 1.3 %collective-permute-done.5.sib_ref = f32[8,128]{1,0:T(8,128)S(1)} collective-permute-done((f32[8,128]{1,0:T(8,128)S(1)}, f32[8,128]{1,0:T(8,128)S(1)}, u32[]{:S(2)}, u32[]{:S(2)}) %collective-permute-start.5) | collective-permute-done | bytes 4128 | tf_op jit(solution)/shard_map/ppermute | solution.py:582
  39.7 1.8 %collective-permute-done.3.yn_ref = bf16[496,128]{1,0:T(8,128)(2,1)S(1)} collective-permute-done((bf16[496,128]{1,0:T(8,128)(2,1)S(1)}, bf16[496,128]{1,0:T(8,128)(2,1)S(1)}, u32[]{:S(2)}, u32[]{:S(2)}) %collective-permute-start.3) | collective-permute-done | bytes 127008 | tf_op jit(solution)/shard_map/ppermute | solution.py:550
  41.5 3.4 %shard_map.131 = (f32[8,42,128]{2,1,0:T(8,128)S(1)}, f32[8,42,128]{2,1,0:T(8,128)S(1)}) custom-call(bf16[4,544,128]{2,1,0:T(8,128)(2,1)S(1)} %copy-done, bf16[2,544,128]{2,1,0:T(8,128)(2,1)S(1)} %collective-permute-done.next_ref, f32[16,640]{1,0:T(8,128)S(1)} %get-tuple-element.26.beyond_ref, bf16[496,128]{1,0:T(8,128)(2,1)S(1)} %collective-permute-done.3.yn_ref, ...), custom_call_target="tpu_custom_call" | custom-call | tf_op jit(solution)/shard_map/pallas_call | solution.py:34
  44.9 3.8 %collective-permute-start.6 = (f32[8,42,128]{2,1,0:T(8,128)S(1)}, f32[8,42,128]{2,1,0:T(8,128)S(1)}, u32[]{:S(2)}, u32[]{:S(2)}) collective-permute-start(f32[8,42,128]{2,1,0:T(8,128)S(1)} %get-tuple-element.33), channel_id=1, source_target_pairs={{0,1},{1,0},{2,3},{3,2},{4,5},{5,4},{6,7},{7,6},{8,9},{9,8},{10,11... | collective-permute-start | bytes 516104 | tf_op jit(solution)/shard_map/ppermute | solution.py:554
  48.7 1.1 %collective-permute-done.6.b_ref = f32[8,42,128]{2,1,0:T(8,128)S(1)} collective-permute-done((f32[8,42,128]{2,1,0:T(8,128)S(1)}, f32[8,42,128]{2,1,0:T(8,128)S(1)}, u32[]{:S(2)}, u32[]{:S(2)}) %collective-permute-start.6) | collective-permute-done | bytes 172064 | tf_op jit(solution)/shard_map/ppermute | solution.py:554
  49.8 10.8 %all_to_all.15.in_ref = f32[8,42,128]{2,1,0:T(8,128)S(1)} all-to-all(f32[8,42,128]{2,1,0:T(8,128)S(1)} %shard_map.132), channel_id=1, replica_groups=mesh['zl'=2,'x'=4,'zh'=4,'y'=4,'core'=2] {'zl','zh'}, dimensions={0} | all-to-all | bytes 344064 | tf_op jit(solution)/shard_map/all_to_all | solution.py:612
  60.6 9.8 %all_to_all.16.in_ref = f32[16,21,128]{2,1,0:T(8,128)S(1)} all-to-all(f32[16,21,128]{2,1,0:T(8,128)S(1)} %shard_map.133), channel_id=1, replica_groups=mesh['zl'=2,'x'=4,'zh'=4,'y'=4,'core'=2] {'y','x'}, dimensions={0} | all-to-all | bytes 344064 | tf_op jit(solution)/shard_map/all_to_all | solution.py:614
  70.5 3.5 %collective-permute-start.7 = (f32[40,128]{1,0:T(8,128)S(1)}, f32[40,128]{1,0:T(8,128)S(1)}, u32[]{:S(2)}, u32[]{:S(2)}) collective-permute-start(f32[40,128]{1,0:T(8,128)S(1)} %shard_map.134.in_ref), channel_id=1, source_target_pairs={{0,1},{1,0},{2,3},{3,2},{4,5},{5,4},{6,7},{7,6},{8,9},{9,8},{10,11... | collective-permute-start | bytes 61448 | tf_op jit(solution)/shard_map/ppermute | solution.py:554
  74.0 0.8 %collective-permute-done.7.other_ref = f32[40,128]{1,0:T(8,128)S(1)} collective-permute-done((f32[40,128]{1,0:T(8,128)S(1)}, f32[40,128]{1,0:T(8,128)S(1)}, u32[]{:S(2)}, u32[]{:S(2)}) %collective-permute-start.7) | collective-permute-done | bytes 20512 | tf_op jit(solution)/shard_map/ppermute | solution.py:554
  74.9 0.9 %shard_map.135 = (f32[1,216]{1,0:T(1,128)}, f32[1,216]{1,0:T(1,128)}, f32[1,216]{1,0:T(1,128)}, f32[27,128]{1,0:T(8,128)}, f32[27,128]{1,0:T(8,128)}, /*index=5*/f32[27,128]{1,0:T(8,128)}) custom-call(f32[40,128]{1,0:T(8,128)S(1)} %shard_map.134.in_ref, f32[40,128]{1,0:T(8,128)S(1)} %collective-permute-done.7.other_ref, f32[8,128]{1,0:T(8,128)S(1)} %copy-done.2, ...), custom_call_target="tpu_custom_call" | custom-call | tf_op jit(solution)/shard_map/pallas_call | solution.py:34
  (15 shorter events, 0.1 us)
Async XLA Ops:
  3.6 31.0 %copy-start = (bf16[4,544,128]{2,1,0:T(8,128)(2,1)S(1)}, bf16[4,544,128]{2,1,0:T(8,128)(2,1)}, u32[]{:S(2)}) copy-start(bf16[4,544,128]{2,1,0:T(8,128)(2,1)} %get-tuple-element.23.slab_ref) | copy-start | bytes 1671172
  3.7 20.8 %all-to-all-start = ((bf16[64,5,4,128]{3,2,1,0:T(4,128)(2,1)}), bf16[64,5,4,128]{3,2,1,0:T(4,128)(2,1)S(1)}, u32[]{:S(2)}, u32[]{:S(2)}) async-start(bf16[64,5,4,128]{3,2,1,0:T(4,128)(2,1)} %get-tuple-element.25), calls=%async_computation | async-start | bytes 655360 | tf_op jit(solution)/shard_map/all_to_all | solution.py:583
  14.1 15.6 %collective-permute-start = (bf16[2,544,128]{2,1,0:T(8,128)(2,1)}, bf16[2,544,128]{2,1,0:T(8,128)(2,1)S(1)}, u32[]{:S(2)}, u32[]{:S(2)}) collective-permute-start(bf16[2,544,128]{2,1,0:T(8,128)(2,1)} %get-tuple-element.24), channel_id=1, source_target_pairs={{0,224},{32,0},{64,32},{96,64},{128,96},{160,128},{192,160},{224,1... | collective-permute-start | bytes 835592 | tf_op jit(solution)/shard_map/ppermute | solution.py:581
  24.5 6.2 %collective-permute-start.2 = (bf16[128,128]{1,0:T(8,128)(2,1)S(1)}, bf16[128,128]{1,0:T(8,128)(2,1)S(1)}, u32[]{:S(2)}, u32[]{:S(2)}) collective-permute-start(bf16[128,128]{1,0:T(8,128)(2,1)S(1)} %shard_map.128.bank_ref), channel_id=1, source_target_pairs={{0,24},{8,0},{16,8},{24,16},{1,25},{9,1},{17,9},{25,17},{2,26},{10... | collective-permute-start | bytes 98312 | tf_op jit(solution)/shard_map/ppermute | solution.py:550
  29.7 4.9 %collective-permute-start.1 = (bf16[128,128]{1,0:T(8,128)(2,1)S(1)}, bf16[128,128]{1,0:T(8,128)(2,1)S(1)}, u32[]{:S(2)}, u32[]{:S(2)}) collective-permute-start(bf16[128,128]{1,0:T(8,128)(2,1)S(1)} %shard_map.128.bank_ref), channel_id=1, source_target_pairs={{0,8},{8,16},{16,24},{24,0},{1,9},{9,17},{17,25},{25,1},{2,10},{10... | collective-permute-start | bytes 98312 | tf_op jit(solution)/shard_map/ppermute | solution.py:550
  34.6 2.9 %copy-start.1 = (f32[3456]{0:T(1024)S(1)}, f32[3456]{0:T(1024)}, u32[]{:S(2)}) copy-start(f32[3456]{0:T(1024)} %param.10) | copy-start | bytes 41476
  34.8 2.4 %copy-start.2 = (f32[8,128]{1,0:T(8,128)S(1)}, f32[8,128]{1,0:T(8,128)}, u32[]{:S(2)}) copy-start(f32[8,128]{1,0:T(8,128)} %get-tuple-element.31.own_ref) | copy-start | bytes 12292
  34.8 6.7 %collective-permute-start.3 = (bf16[496,128]{1,0:T(8,128)(2,1)S(1)}, bf16[496,128]{1,0:T(8,128)(2,1)S(1)}, u32[]{:S(2)}, u32[]{:S(2)}) collective-permute-start(bf16[496,128]{1,0:T(8,128)(2,1)S(1)} %get-tuple-element.27), channel_id=1, source_target_pairs={{0,24},{8,0},{16,8},{24,16},{1,25},{9,1},{17,9},{25,17},{2,26},{10... | collective-permute-start | bytes 380936 | tf_op jit(solution)/shard_map/ppermute | solution.py:550
  35.2 6.3 %collective-permute-start.4 = (bf16[496,128]{1,0:T(8,128)(2,1)S(1)}, bf16[496,128]{1,0:T(8,128)(2,1)S(1)}, u32[]{:S(2)}, u32[]{:S(2)}) collective-permute-start(bf16[496,128]{1,0:T(8,128)(2,1)S(1)} %get-tuple-element.28), channel_id=1, source_target_pairs={{0,8},{8,16},{16,24},{24,0},{1,9},{9,17},{17,25},{25,1},{2,10},{10... | collective-permute-start | bytes 380936 | tf_op jit(solution)/shard_map/ppermute | solution.py:550
  37.2 2.5 %collective-permute-start.5 = (f32[8,128]{1,0:T(8,128)S(1)}, f32[8,128]{1,0:T(8,128)S(1)}, u32[]{:S(2)}, u32[]{:S(2)}) collective-permute-start(f32[8,128]{1,0:T(8,128)S(1)} %copy-done.2), channel_id=1, source_target_pairs={{0,2},{2,0},{4,6},{6,4},{1,3},{3,1},{5,7},{7,5},{8,10},{10,8},{12,... | collective-permute-start | bytes 12296 | tf_op jit(solution)/shard_map/ppermute | solution.py:582
  44.9 4.9 %collective-permute-start.6 = (f32[8,42,128]{2,1,0:T(8,128)S(1)}, f32[8,42,128]{2,1,0:T(8,128)S(1)}, u32[]{:S(2)}, u32[]{:S(2)}) collective-permute-start(f32[8,42,128]{2,1,0:T(8,128)S(1)} %get-tuple-element.33), channel_id=1, source_target_pairs={{0,1},{1,0},{2,3},{3,2},{4,5},{5,4},{6,7},{7,6},{8,9},{9,8},{10,11... | collective-permute-start | bytes 516104 | tf_op jit(solution)/shard_map/ppermute | solution.py:554
  70.4 4.4 %copy-start.3 = (f32[3456]{0:T(1024)S(1)}, f32[3456]{0:T(1024)}, u32[]{:S(2)}) copy-start(f32[3456]{0:T(1024)} %param.11) | copy-start | bytes 41476
  70.4 4.4 %copy-start.4 = (f32[3456]{0:T(1024)S(1)}, f32[3456]{0:T(1024)}, u32[]{:S(2)}) copy-start(f32[3456]{0:T(1024)} %param.12) | copy-start | bytes 41476
  70.5 4.4 %collective-permute-start.7 = (f32[40,128]{1,0:T(8,128)S(1)}, f32[40,128]{1,0:T(8,128)S(1)}, u32[]{:S(2)}, u32[]{:S(2)}) collective-permute-start(f32[40,128]{1,0:T(8,128)S(1)} %shard_map.134.in_ref), channel_id=1, source_target_pairs={{0,1},{1,0},{2,3},{3,2},{4,5},{5,4},{6,7},{7,6},{8,9},{9,8},{10,11... | collective-permute-start | bytes 61448 | tf_op jit(solution)/shard_map/ppermute | solution.py:554

commit v8 on v7

--- a/solution.py
+++ b/solution.py
@@ -459,7 +459,7 @@
         block = [total[4 * j + x : 4 * j + x + 1] for j in range(7)]
         rows = jnp.concatenate(block + [total[28:42]], axis=0)
         for y in range(4):
-            out_ref[4 * y + x] = rows
+            out_ref[4 * x + y] = rows
 
 
 def third_stage(in_ref, own_ref, sib_ref, out_ref):
@@ -611,7 +611,7 @@
     sums = call(first_stage, shape((8, 42, 128), F32), keep, swap(send))
     sums = lax.all_to_all(sums, ("zl", "zh"), 0, 0, tiled=True)
     sums = call(second_stage, shape((16, 21, 128), F32), sums)
-    sums = lax.all_to_all(sums, ("y", "x"), 0, 0, tiled=True)
+    sums = lax.all_to_all(sums, ("x", "y"), 0, 0, tiled=True)
     half = call(third_stage, shape((40, 128), F32), sums, own, sibling)
     one, rows = shape((1, 216), F32), shape((27, 128), F32)
     new = call(update, (one, one, one, rows, rows, rows), half, swap(half), own, *narrow)

time: 76 us -> 75.7 us (level)
  no operation moved by 1% of the time
where the time goes in v8:
time: 75.7 us; the launch traced here: 75.5 us
  starting transfers between devices  29.3 us (39%)
  blocking collectives  20.6 us (27%)
  waiting for transfers between devices  16.4 us (22%)
  Pallas kernels  8.44 us (11%)
    all_to_all x1, blocking collectives, local(): sums = lax.all_to_all(sums, ('zl', 'zh'), 0, 0, tiled=True)  10.8 us
    all_to_all x1, starting transfers between devices, local(): message = lax.all_to_all(message, GX + GZ, 0, 0, tiled=True)  10.5 us
    all_to_all x1, blocking collectives, local(): sums = lax.all_to_all(sums, ('x', 'y'), 0, 0, tiled=True)  9.76 us
    pallas_call x9, Pallas kernels, call(): pl.pallas_call(kernel, out_shape=out_shapes, in_specs=[space] * len(args)...  8.44 us
    ppermute x4, starting transfers between devices, turn(): return lax.ppermute(value, GY, [(i, (i + by) % 4) for i in range(4)])  7.6 us
    ppermute x2, starting transfers between devices, swap(): return lax.ppermute(value, 'core', [(0, 1), (1, 0)])  7.12 us
    ppermute x4, waiting for transfers between devices, turn(): return lax.ppermute(value, GY, [(i, (i + by) % 4) for i in range(4)])  6.68 us
    all_to_all x1, waiting for transfers between devices, local(): message = lax.all_to_all(message, GX + GZ, 0, 0, tiled=True)  6.51 us
  transfers between devices with their start and end apart: 9, of which 7 were waited for; matrix products, arithmetic and copies ran while one was open for 0% of the time, Pallas kernels for 1%

profile of v8, /device:TPU:1, one launch (start us, length us, event | category | flops | bytes accessed | tf_op | source)
XLA Modules:
  0.0 75.5 jit_solution(14994944648881176597)
XLA Ops:
  0.6 3.0 %shard_map.127 = (bf16[4,544,128]{2,1,0:T(8,128)(2,1)}, bf16[2,544,128]{2,1,0:T(8,128)(2,1)}, bf16[64,5,4,128]{3,2,1,0:T(4,128)(2,1)}, f32[8,128]{1,0:T(8,128)}) custom-call(bf16[2048,128]{1,0:T(8,128)(2,1)} %bitcast.18, bf16[128,128]{1,0:T(8,128)(2,1)} %bitcast.19, f32[1,216]{1,0:T(1,128)} %bitcast.20, f32[1,216]{1,0:T(1,128)} %bitcast.21, f32[1,216]{1,0:T(1,128)} %bitcast.22), custom_call_target="tpu_custom_call" | custom-call | tf_op jit(solution)/shard_map/pallas_call | solution.py:34
  3.7 10.5 %all-to-all-start = ((bf16[64,5,4,128]{3,2,1,0:T(4,128)(2,1)}), bf16[64,5,4,128]{3,2,1,0:T(4,128)(2,1)S(1)}, u32[]{:S(2)}, u32[]{:S(2)}) async-start(bf16[64,5,4,128]{3,2,1,0:T(4,128)(2,1)} %get-tuple-element.25), calls=%async_computation | async-start | bytes 655360 | tf_op jit(solution)/shard_map/all_to_all | solution.py:583
  14.1 3.8 %collective-permute-start = (bf16[2,544,128]{2,1,0:T(8,128)(2,1)}, bf16[2,544,128]{2,1,0:T(8,128)(2,1)S(1)}, u32[]{:S(2)}, u32[]{:S(2)}) collective-permute-start(bf16[2,544,128]{2,1,0:T(8,128)(2,1)} %get-tuple-element.24), channel_id=1, source_target_pairs={{0,224},{32,0},{64,32},{96,64},{128,96},{160,128},{192,160},{224,1... | collective-permute-start | bytes 835592 | tf_op jit(solution)/shard_map/ppermute | solution.py:581
  18.0 6.5 %all-to-all-done.in_ref = bf16[64,5,4,128]{3,2,1,0:T(4,128)(2,1)S(1)} async-done(((bf16[64,5,4,128]{3,2,1,0:T(4,128)(2,1)}), bf16[64,5,4,128]{3,2,1,0:T(4,128)(2,1)S(1)}, u32[]{:S(2)}, u32[]{:S(2)}) %all-to-all-start) | async-done | bytes 327712 | tf_op jit(solution)/shard_map/all_to_all | solution.py:583
  24.5 5.2 %collective-permute-start.2 = (bf16[128,128]{1,0:T(8,128)(2,1)S(1)}, bf16[128,128]{1,0:T(8,128)(2,1)S(1)}, u32[]{:S(2)}, u32[]{:S(2)}) collective-permute-start(bf16[128,128]{1,0:T(8,128)(2,1)S(1)} %shard_map.128.bank_ref), channel_id=1, source_target_pairs={{0,24},{8,0},{16,8},{24,16},{1,25},{9,1},{17,9},{25,17},{2,26},{10... | collective-permute-start | bytes 98312 | tf_op jit(solution)/shard_map/ppermute | solution.py:550
  29.7 0.0 collective-permute-start.1
  29.7 0.0 collective-permute-done.next_ref
  29.7 1.0 %collective-permute-done.2.nb_ref = bf16[128,128]{1,0:T(8,128)(2,1)S(1)} collective-permute-done((bf16[128,128]{1,0:T(8,128)(2,1)S(1)}, bf16[128,128]{1,0:T(8,128)(2,1)S(1)}, u32[]{:S(2)}, u32[]{:S(2)}) %collective-permute-start.2) | collective-permute-done | bytes 32800 | tf_op jit(solution)/shard_map/ppermute | solution.py:550
  30.8 3.9 %collective-permute-done.1.pb_ref = bf16[128,128]{1,0:T(8,128)(2,1)S(1)} collective-permute-done((bf16[128,128]{1,0:T(8,128)(2,1)S(1)}, bf16[128,128]{1,0:T(8,128)(2,1)S(1)}, u32[]{:S(2)}, u32[]{:S(2)}) %collective-permute-start.1) | collective-permute-done | bytes 32800 | tf_op jit(solution)/shard_map/ppermute | solution.py:550
  34.6 0.2 shard_map.129
  34.8 0.4 collective-permute-start.3
  35.2 2.0 %collective-permute-start.4 = (bf16[496,128]{1,0:T(8,128)(2,1)S(1)}, bf16[496,128]{1,0:T(8,128)(2,1)S(1)}, u32[]{:S(2)}, u32[]{:S(2)}) collective-permute-start(bf16[496,128]{1,0:T(8,128)(2,1)S(1)} %get-tuple-element.28), channel_id=1, source_target_pairs={{0,8},{8,16},{16,24},{24,0},{1,9},{9,17},{17,25},{25,1},{2,10},{10... | collective-permute-start | bytes 380936 | tf_op jit(solution)/shard_map/ppermute | solution.py:550
  37.2 0.3 collective-permute-start.5
  37.5 0.9 %shard_map.130 = (bf16[256,512]{1,0:T(8,128)(2,1)S(1)}, bf16[512,128]{1,0:T(8,128)(2,1)S(1)}) custom-call(f32[27,128]{1,0:T(8,128)S(1)} %bitcast.14), custom_call_target="tpu_custom_call" | custom-call | tf_op jit(solution)/shard_map/pallas_call | solution.py:34
  38.4 1.3 %collective-permute-done.5.sib_ref = f32[8,128]{1,0:T(8,128)S(1)} collective-permute-done((f32[8,128]{1,0:T(8,128)S(1)}, f32[8,128]{1,0:T(8,128)S(1)}, u32[]{:S(2)}, u32[]{:S(2)}) %collective-permute-start.5) | collective-permute-done | bytes 4128 | tf_op jit(solution)/shard_map/ppermute | solution.py:582
  39.7 1.8 %collective-permute-done.3.yn_ref = bf16[496,128]{1,0:T(8,128)(2,1)S(1)} collective-permute-done((bf16[496,128]{1,0:T(8,128)(2,1)S(1)}, bf16[496,128]{1,0:T(8,128)(2,1)S(1)}, u32[]{:S(2)}, u32[]{:S(2)}) %collective-permute-start.3) | collective-permute-done | bytes 127008 | tf_op jit(solution)/shard_map/ppermute | solution.py:550
  41.5 3.4 %shard_map.131 = (f32[8,42,128]{2,1,0:T(8,128)S(1)}, f32[8,42,128]{2,1,0:T(8,128)S(1)}) custom-call(bf16[4,544,128]{2,1,0:T(8,128)(2,1)S(1)} %copy-done, bf16[2,544,128]{2,1,0:T(8,128)(2,1)S(1)} %collective-permute-done.next_ref, f32[16,640]{1,0:T(8,128)S(1)} %get-tuple-element.26.beyond_ref, bf16[496,128]{1,0:T(8,128)(2,1)S(1)} %collective-permute-done.3.yn_ref, ...), custom_call_target="tpu_custom_call" | custom-call | tf_op jit(solution)/shard_map/pallas_call | solution.py:34
  44.9 3.8 %collective-permute-start.6 = (f32[8,42,128]{2,1,0:T(8,128)S(1)}, f32[8,42,128]{2,1,0:T(8,128)S(1)}, u32[]{:S(2)}, u32[]{:S(2)}) collective-permute-start(f32[8,42,128]{2,1,0:T(8,128)S(1)} %get-tuple-element.33), channel_id=1, source_target_pairs={{0,1},{1,0},{2,3},{3,2},{4,5},{5,4},{6,7},{7,6},{8,9},{9,8},{10,11... | collective-permute-start | bytes 516104 | tf_op jit(solution)/shard_map/ppermute | solution.py:554
  48.7 1.1 %collective-permute-done.6.b_ref = f32[8,42,128]{2,1,0:T(8,128)S(1)} collective-permute-done((f32[8,42,128]{2,1,0:T(8,128)S(1)}, f32[8,42,128]{2,1,0:T(8,128)S(1)}, u32[]{:S(2)}, u32[]{:S(2)}) %collective-permute-start.6) | collective-permute-done | bytes 172064 | tf_op jit(solution)/shard_map/ppermute | solution.py:554
  49.8 10.8 %all_to_all.15.in_ref = f32[8,42,128]{2,1,0:T(8,128)S(1)} all-to-all(f32[8,42,128]{2,1,0:T(8,128)S(1)} %shard_map.132), channel_id=1, replica_groups=mesh['zl'=2,'x'=4,'zh'=4,'y'=4,'core'=2] {'zl','zh'}, dimensions={0} | all-to-all | bytes 344064 | tf_op jit(solution)/shard_map/all_to_all | solution.py:612
  60.6 9.8 %all_to_all.16.in_ref = f32[16,21,128]{2,1,0:T(8,128)S(1)} all-to-all(f32[16,21,128]{2,1,0:T(8,128)S(1)} %shard_map.133), channel_id=1, replica_groups=mesh['zl'=2,'x'=4,'zh'=4,'y'=4,'core'=2] {'x','y'}, dimensions={0} | all-to-all | bytes 344064 | tf_op jit(solution)/shard_map/all_to_all | solution.py:614
  70.4 3.3 %collective-permute-start.7 = (f32[40,128]{1,0:T(8,128)S(1)}, f32[40,128]{1,0:T(8,128)S(1)}, u32[]{:S(2)}, u32[]{:S(2)}) collective-permute-start(f32[40,128]{1,0:T(8,128)S(1)} %shard_map.134.in_ref), channel_id=1, source_target_pairs={{0,1},{1,0},{2,3},{3,2},{4,5},{5,4},{6,7},{7,6},{8,9},{9,8},{10,11... | collective-permute-start | bytes 61448 | tf_op jit(solution)/shard_map/ppermute | solution.py:554
  73.7 0.8 %collective-permute-done.7.other_ref = f32[40,128]{1,0:T(8,128)S(1)} collective-permute-done((f32[40,128]{1,0:T(8,128)S(1)}, f32[40,128]{1,0:T(8,128)S(1)}, u32[]{:S(2)}, u32[]{:S(2)}) %collective-permute-start.7) | collective-permute-done | bytes 20512 | tf_op jit(solution)/shard_map/ppermute | solution.py:554
  74.6 0.9 %shard_map.135 = (f32[1,216]{1,0:T(1,128)}, f32[1,216]{1,0:T(1,128)}, f32[1,216]{1,0:T(1,128)}, f32[27,128]{1,0:T(8,128)}, f32[27,128]{1,0:T(8,128)}, /*index=5*/f32[27,128]{1,0:T(8,128)}) custom-call(f32[40,128]{1,0:T(8,128)S(1)} %shard_map.134.in_ref, f32[40,128]{1,0:T(8,128)S(1)} %collective-permute-done.7.other_ref, f32[8,128]{1,0:T(8,128)S(1)} %copy-done.2, ...), custom_call_target="tpu_custom_call" | custom-call | tf_op jit(solution)/shard_map/pallas_call | solution.py:34
  (15 shorter events, 0.1 us)
Async XLA Ops:
  3.6 31.0 %copy-start = (bf16[4,544,128]{2,1,0:T(8,128)(2,1)S(1)}, bf16[4,544,128]{2,1,0:T(8,128)(2,1)}, u32[]{:S(2)}) copy-start(bf16[4,544,128]{2,1,0:T(8,128)(2,1)} %get-tuple-element.23.slab_ref) | copy-start | bytes 1671172
  3.7 20.8 %all-to-all-start = ((bf16[64,5,4,128]{3,2,1,0:T(4,128)(2,1)}), bf16[64,5,4,128]{3,2,1,0:T(4,128)(2,1)S(1)}, u32[]{:S(2)}, u32[]{:S(2)}) async-start(bf16[64,5,4,128]{3,2,1,0:T(4,128)(2,1)} %get-tuple-element.25), calls=%async_computation | async-start | bytes 655360 | tf_op jit(solution)/shard_map/all_to_all | solution.py:583
  14.1 15.6 %collective-permute-start = (bf16[2,544,128]{2,1,0:T(8,128)(2,1)}, bf16[2,544,128]{2,1,0:T(8,128)(2,1)S(1)}, u32[]{:S(2)}, u32[]{:S(2)}) collective-permute-start(bf16[2,544,128]{2,1,0:T(8,128)(2,1)} %get-tuple-element.24), channel_id=1, source_target_pairs={{0,224},{32,0},{64,32},{96,64},{128,96},{160,128},{192,160},{224,1... | collective-permute-start | bytes 835592 | tf_op jit(solution)/shard_map/ppermute | solution.py:581
  24.5 6.2 %collective-permute-start.2 = (bf16[128,128]{1,0:T(8,128)(2,1)S(1)}, bf16[128,128]{1,0:T(8,128)(2,1)S(1)}, u32[]{:S(2)}, u32[]{:S(2)}) collective-permute-start(bf16[128,128]{1,0:T(8,128)(2,1)S(1)} %shard_map.128.bank_ref), channel_id=1, source_target_pairs={{0,24},{8,0},{16,8},{24,16},{1,25},{9,1},{17,9},{25,17},{2,26},{10... | collective-permute-start | bytes 98312 | tf_op jit(solution)/shard_map/ppermute | solution.py:550
  29.7 4.9 %collective-permute-start.1 = (bf16[128,128]{1,0:T(8,128)(2,1)S(1)}, bf16[128,128]{1,0:T(8,128)(2,1)S(1)}, u32[]{:S(2)}, u32[]{:S(2)}) collective-permute-start(bf16[128,128]{1,0:T(8,128)(2,1)S(1)} %shard_map.128.bank_ref), channel_id=1, source_target_pairs={{0,8},{8,16},{16,24},{24,0},{1,9},{9,17},{17,25},{25,1},{2,10},{10... | collective-permute-start | bytes 98312 | tf_op jit(solution)/shard_map/ppermute | solution.py:550
  34.6 2.9 %copy-start.1 = (f32[3456]{0:T(1024)S(1)}, f32[3456]{0:T(1024)}, u32[]{:S(2)}) copy-start(f32[3456]{0:T(1024)} %param.10) | copy-start | bytes 41476
  34.8 2.4 %copy-start.2 = (f32[8,128]{1,0:T(8,128)S(1)}, f32[8,128]{1,0:T(8,128)}, u32[]{:S(2)}) copy-start(f32[8,128]{1,0:T(8,128)} %get-tuple-element.31.own_ref) | copy-start | bytes 12292
  34.8 6.7 %collective-permute-start.3 = (bf16[496,128]{1,0:T(8,128)(2,1)S(1)}, bf16[496,128]{1,0:T(8,128)(2,1)S(1)}, u32[]{:S(2)}, u32[]{:S(2)}) collective-permute-start(bf16[496,128]{1,0:T(8,128)(2,1)S(1)} %get-tuple-element.27), channel_id=1, source_target_pairs={{0,24},{8,0},{16,8},{24,16},{1,25},{9,1},{17,9},{25,17},{2,26},{10... | collective-permute-start | bytes 380936 | tf_op jit(solution)/shard_map/ppermute | solution.py:550
  35.2 6.3 %collective-permute-start.4 = (bf16[496,128]{1,0:T(8,128)(2,1)S(1)}, bf16[496,128]{1,0:T(8,128)(2,1)S(1)}, u32[]{:S(2)}, u32[]{:S(2)}) collective-permute-start(bf16[496,128]{1,0:T(8,128)(2,1)S(1)} %get-tuple-element.28), channel_id=1, source_target_pairs={{0,8},{8,16},{16,24},{24,0},{1,9},{9,17},{17,25},{25,1},{2,10},{10... | collective-permute-start | bytes 380936 | tf_op jit(solution)/shard_map/ppermute | solution.py:550
  37.2 2.5 %collective-permute-start.5 = (f32[8,128]{1,0:T(8,128)S(1)}, f32[8,128]{1,0:T(8,128)S(1)}, u32[]{:S(2)}, u32[]{:S(2)}) collective-permute-start(f32[8,128]{1,0:T(8,128)S(1)} %copy-done.2), channel_id=1, source_target_pairs={{0,2},{2,0},{4,6},{6,4},{1,3},{3,1},{5,7},{7,5},{8,10},{10,8},{12,... | collective-permute-start | bytes 12296 | tf_op jit(solution)/shard_map/ppermute | solution.py:582
  44.9 4.9 %collective-permute-start.6 = (f32[8,42,128]{2,1,0:T(8,128)S(1)}, f32[8,42,128]{2,1,0:T(8,128)S(1)}, u32[]{:S(2)}, u32[]{:S(2)}) collective-permute-start(f32[8,42,128]{2,1,0:T(8,128)S(1)} %get-tuple-element.33), channel_id=1, source_target_pairs={{0,1},{1,0},{2,3},{3,2},{4,5},{5,4},{6,7},{7,6},{8,9},{9,8},{10,11... | collective-permute-start | bytes 516104 | tf_op jit(solution)/shard_map/ppermute | solution.py:554
  70.4 4.2 %copy-start.3 = (f32[3456]{0:T(1024)S(1)}, f32[3456]{0:T(1024)}, u32[]{:S(2)}) copy-start(f32[3456]{0:T(1024)} %param.11) | copy-start | bytes 41476
  70.4 4.2 %copy-start.4 = (f32[3456]{0:T(1024)S(1)}, f32[3456]{0:T(1024)}, u32[]{:S(2)}) copy-start(f32[3456]{0:T(1024)} %param.12) | copy-start | bytes 41476
  70.4 4.2 %collective-permute-start.7 = (f32[40,128]{1,0:T(8,128)S(1)}, f32[40,128]{1,0:T(8,128)S(1)}, u32[]{:S(2)}, u32[]{:S(2)}) collective-permute-start(f32[40,128]{1,0:T(8,128)S(1)} %shard_map.134.in_ref), channel_id=1, source_target_pairs={{0,1},{1,0},{2,3},{3,2},{4,5},{5,4},{6,7},{7,6},{8,9},{9,8},{10,11... | collective-permute-start | bytes 61448 | tf_op jit(solution)/shard_map/ppermute | solution.py:554
